TPU v7x, 32 devices: a whole 2x2x4 slice. The times are simulated.
32 devices in a mesh: dp: 4 (over z), expert: 8 (over y, x, core).
Axes of the slice: x: 2, y: 2, z: 4, core: 2. Of those that a mesh axis runs over, the one named last changes fastest.
Arguments:
- tokens_in: bfloat16 [64, 1024, 768], P(('dp', 'expert')), may hold values from -6 to 6
- buckets: int32 [64, 1024], P(('dp', 'expert')), may hold values from 0 to 7, as said below
- ln1_gain: float32 [768], replicated, may hold values from 0.5 to 1.5
- ln1_bias: float32 [768], replicated, may hold values from -1.5 to 1.5
- w_qkv: bfloat16 [768, 2304], P('dp'), may hold values from -0.21875 to 0.21875
- w_out: bfloat16 [768, 768], P('dp'), may hold values from -0.875 to 0.875
- ln2_gain: float32 [768], replicated, may hold values from 0.5 to 1.5
- ln2_bias: float32 [768], replicated, may hold values from -1.5 to 1.5
- w_in: bfloat16 [8, 768, 3072], P('expert'), may hold values from -0.21875 to 0.21875
- w_down: bfloat16 [8, 3072, 768], P('expert'), may hold values from -0.109375 to 0.109375
- cotangent: bfloat16 [64, 1024, 768], P(('dp', 'expert')), may hold values from -6 to 6
Outputs:
- block_out: float32 [64, 1024, 768], P(('dp', 'expert'))
- grad_input: float32 [64, 1024, 768], P(('dp', 'expert'))
- grad_ln1_gain: float32 [768], P('dp')
- grad_ln1_bias: float32 [768], P('dp')
- grad_w_qkv: float32 [768, 2304], P('dp')
- grad_w_out: float32 [768, 768], P('dp')
- grad_ln2_gain: float32 [768], P('dp')
- grad_ln2_bias: float32 [768], P('dp')
- grad_w_in: float32 [8, 768, 3072], P('expert', None, 'dp')
- grad_w_down: float32 [8, 3072, 768], P('expert', 'dp')
Inputs may be any that keep to these rules, and one draw needn't show every extreme that they name: `buckets`: within the 1024 tokens of one sequence no bucket is named more than 160 times, and in every draw some bucket (which one may differ from sequence to sequence) is named exactly 160 times in each sequence.
All inputs are finite; a program needn't handle non-finite values.
Results may differ from a plain program's by a relative error of at most 0.019.
Values may be sent and summed in bfloat16 or wider, within the bound.
A program may use at most 384 MiB of HBM per device.

v0:
```python
import jax
import jax.numpy as jnp
from jax import lax
from jax.sharding import PartitionSpec as P

H = 12


epsilon = 1e-05
neg_large = -1e30
contract_rows = (((0,), (0,)), ((), ()))
contract_cols = (((1,), (1,)), ((), ()))


def layer_norm(values, gain_row, offset):
    centre = jnp.mean(values, axis=-1, keepdims=True)
    shifted = values - centre
    spread = jnp.mean(shifted * shifted, axis=-1, keepdims=True)
    return shifted * lax.rsqrt(spread + epsilon) * gain_row + offset


def slot_table(bucket_row, experts, capacity):
    length = bucket_row.shape[0]
    onehot = (bucket_row[:, None] == jnp.arange(experts, dtype=jnp.int32)[None, :]).astype(
        jnp.int32
    )
    expert_ranking = jnp.sum(jnp.cumsum(onehot, axis=0) * onehot, axis=1) - 1
    slot_of = bucket_row * capacity + expert_ranking
    owner_of = (
        jnp.full((experts * capacity,), length, jnp.int32)
        .at[slot_of]
        .set(jnp.arange(length, dtype=jnp.int32))
    )
    return (slot_of, owner_of)


def causal_scores(query_part, key_part, first_row, score_scale):
    row_count = query_part.shape[0]
    key_count = key_part.shape[0]
    scores = (
        jnp.einsum("qhd,khd->hqk", query_part, key_part, preferred_element_type=jnp.float32)
        * score_scale
    )
    future = (
        jnp.arange(key_count, dtype=jnp.int32)[None, :]
        > (first_row + jnp.arange(row_count, dtype=jnp.int32))[:, None]
    )
    return jnp.where(future[None], neg_large, scores)


def attention_forward(qkv_rows, heads_count, row_block, score_scale):
    length, triple = qkv_rows.shape
    head_size = triple // (3 * heads_count)
    split_qkv = qkv_rows.reshape(length, 3, heads_count, head_size)
    outputs, log_totals = ([], [])
    for first_row in range(0, length, row_block):
        last_row = first_row + row_block
        scores = causal_scores(
            split_qkv[first_row:last_row, 0], split_qkv[:last_row, 1], first_row, score_scale
        )
        largest = jnp.max(scores, axis=-1, keepdims=True)
        raised = jnp.exp(scores - largest)
        totals = jnp.sum(raised, axis=-1, keepdims=True)
        weights = (raised / totals).astype(jnp.bfloat16)
        mixed_out = jnp.einsum(
            "hqk,khd->qhd", weights, split_qkv[:last_row, 2], preferred_element_type=jnp.float32
        )
        outputs.append(mixed_out.reshape(row_block, heads_count * head_size))
        log_totals.append(largest + jnp.log(totals))
    return (jnp.concatenate(outputs, axis=0), log_totals)


def attention_backward(qkv_rows, log_totals, grad_mixed, heads_count, row_block, score_scale):
    length, triple = qkv_rows.shape
    head_size = triple // (3 * heads_count)
    split_qkv = qkv_rows.reshape(length, 3, heads_count, head_size)
    query_grads = []
    grad_key = jnp.zeros((length, heads_count, head_size), jnp.float32)
    grad_value = jnp.zeros((length, heads_count, head_size), jnp.float32)
    for number, first_row in enumerate(range(0, length, row_block)):
        last_row = first_row + row_block
        query_part = split_qkv[first_row:last_row, 0]
        key_part = split_qkv[:last_row, 1]
        value_part = split_qkv[:last_row, 2]
        scores = causal_scores(query_part, key_part, first_row, score_scale)
        prob_rows = jnp.exp(scores - log_totals[number])
        grad_part = grad_mixed[first_row:last_row].reshape(row_block, heads_count, head_size)
        grad_value = grad_value.at[:last_row].add(
            jnp.einsum(
                "hqk,qhd->khd",
                prob_rows.astype(jnp.bfloat16),
                grad_part,
                preferred_element_type=jnp.float32,
            )
        )
        grad_prob = jnp.einsum(
            "qhd,khd->hqk", grad_part, value_part, preferred_element_type=jnp.float32
        )
        inner_sum = jnp.sum(prob_rows * grad_prob, axis=-1, keepdims=True)
        grad_scores = (prob_rows * (grad_prob - inner_sum)).astype(jnp.bfloat16)
        query_grads.append(
            jnp.einsum("hqk,khd->qhd", grad_scores, key_part, preferred_element_type=jnp.float32)
            * score_scale
        )
        grad_key = grad_key.at[:last_row].add(
            jnp.einsum("hqk,qhd->khd", grad_scores, query_part, preferred_element_type=jnp.float32)
            * score_scale
        )
    grad_query = jnp.concatenate(query_grads, axis=0)
    return jnp.stack([grad_query, grad_key, grad_value], axis=1).reshape(length, triple)


def fetch_weights(w_qkv, w_out):
    return (
        lax.all_gather(w_qkv, "dp", axis=0, tiled=True),
        lax.all_gather(w_out, "dp", axis=0, tiled=True),
    )


def regroup(array_in, sources, per_source):
    return array_in.reshape(sources, per_source, array_in.shape[-1])


def on_device(
    tokens_in,
    buckets,
    ln1_gain,
    ln1_bias,
    w_qkv,
    w_out,
    ln2_gain,
    ln2_bias,
    w_in,
    w_down,
    cotangent,
):
    experts = lax.axis_size("expert")
    micro_count, length, width = tokens_in.shape
    capacity = 5 * length // (4 * experts)
    heads_count = H
    row_block = min(512, length)
    score_scale = (width // heads_count) ** (-0.5)
    w_in_local = w_in[0]
    w_down_local = w_down[0]
    hidden_width = w_in_local.shape[1]
    grad_qkv = jnp.zeros((width, 3 * width), jnp.float32)
    grad_out = jnp.zeros((width, width), jnp.float32)
    grad_in = jnp.zeros((width, hidden_width), jnp.float32)
    grad_down = jnp.zeros((hidden_width, width), jnp.float32)
    gain_one_sum = jnp.zeros((width,), jnp.float32)
    bias_one_sum = jnp.zeros((width,), jnp.float32)
    gain_two_sum = jnp.zeros((width,), jnp.float32)
    bias_two_sum = jnp.zeros((width,), jnp.float32)
    spare_row = jnp.zeros((1, width), jnp.bfloat16)
    results, input_grads = ([], [])
    for micro_step in range(micro_count):
        full_qkv, full_out = fetch_weights(w_qkv, w_out)
        inputs_f32 = tokens_in[micro_step].astype(jnp.float32)
        normed, norm_one_back = jax.vjp(layer_norm, inputs_f32, ln1_gain, ln1_bias)
        normed_low = normed.astype(jnp.bfloat16)
        qkv_rows = jnp.dot(normed_low, full_qkv, preferred_element_type=jnp.float32).astype(
            jnp.bfloat16
        )
        mixed_out, log_totals = attention_forward(qkv_rows, heads_count, row_block, score_scale)
        mixed_low = mixed_out.astype(jnp.bfloat16)
        after_attn = inputs_f32 + jnp.dot(mixed_low, full_out, preferred_element_type=jnp.float32)
        normed_two, norm_two_back = jax.vjp(layer_norm, after_attn, ln2_gain, ln2_bias)
        tokens_low = normed_two.astype(jnp.bfloat16)
        slot_of, owner_of = slot_table(buckets[micro_step], experts, capacity)
        dispatched = jnp.concatenate([tokens_low, spare_row], axis=0)[owner_of].reshape(
            experts, capacity, width
        )
        cot_low = cotangent[micro_step]
        cot_slots = jnp.concatenate([cot_low, spare_row], axis=0)[owner_of].reshape(
            experts, capacity, width
        )
        arrived = lax.all_to_all(dispatched, "expert", split_axis=0, concat_axis=0, tiled=True)
        sources, per_source, width_in = arrived.shape
        flat_rows = arrived.reshape(sources * per_source, width_in)
        hidden_pre = jnp.dot(flat_rows, w_in_local, preferred_element_type=jnp.float32)
        hidden_act = jax.nn.gelu(hidden_pre).astype(jnp.bfloat16)
        expert_out = jnp.dot(hidden_act, w_down_local, preferred_element_type=jnp.float32).astype(
            jnp.bfloat16
        )
        kept_rows, hidden_pre, hidden_act, expert_out = (
            arrived,
            regroup(hidden_pre, sources, per_source),
            regroup(hidden_act, sources, per_source),
            regroup(expert_out, sources, per_source),
        )
        returned = lax.all_to_all(expert_out, "expert", split_axis=0, concat_axis=0, tiled=True)
        results.append(
            after_attn + returned.reshape(experts * capacity, width)[slot_of].astype(jnp.float32)
        )
        grad_rows = lax.all_to_all(cot_slots, "expert", split_axis=0, concat_axis=0, tiled=True)
        rows_flat = kept_rows.reshape(-1, width)
        grads_flat = grad_rows.reshape(-1, width)
        pre_flat = hidden_pre.reshape(-1, hidden_width)
        act_flat = hidden_act.reshape(-1, hidden_width)
        grad_act = lax.dot_general(
            grads_flat, w_down_local, contract_cols, preferred_element_type=jnp.float32
        )
        grad_down = grad_down + lax.dot_general(
            act_flat, grads_flat, contract_rows, preferred_element_type=jnp.float32
        )
        gelu_back = jax.vjp(jax.nn.gelu, pre_flat)[1]
        grad_pre = gelu_back(grad_act)[0].astype(jnp.bfloat16)
        grad_in = grad_in + lax.dot_general(
            rows_flat, grad_pre, contract_rows, preferred_element_type=jnp.float32
        )
        grad_tokens = lax.dot_general(
            grad_pre, w_in_local, contract_cols, preferred_element_type=jnp.float32
        ).astype(jnp.bfloat16)
        came_back = lax.all_to_all(
            grad_tokens.reshape(experts, capacity, width),
            "expert",
            split_axis=0,
            concat_axis=0,
            tiled=True,
        )
        grad_normed_two = came_back.reshape(experts * capacity, width)[slot_of].astype(jnp.float32)
        grad_after, grad_gain_two, grad_bias_two = norm_two_back(grad_normed_two)
        grad_after = grad_after + cot_low.astype(jnp.float32)
        grad_after_low = grad_after.astype(jnp.bfloat16)
        grad_out = grad_out + lax.dot_general(
            mixed_low, grad_after_low, contract_rows, preferred_element_type=jnp.float32
        )
        grad_mixed = lax.dot_general(
            grad_after_low, full_out, contract_cols, preferred_element_type=jnp.float32
        ).astype(jnp.bfloat16)
        grad_qkv_rows = attention_backward(
            qkv_rows, log_totals, grad_mixed, heads_count, row_block, score_scale
        ).astype(jnp.bfloat16)
        grad_qkv = grad_qkv + lax.dot_general(
            normed_low, grad_qkv_rows, contract_rows, preferred_element_type=jnp.float32
        )
        grad_normed = lax.dot_general(
            grad_qkv_rows, full_qkv, contract_cols, preferred_element_type=jnp.float32
        )
        grad_inputs, grad_gain_one, grad_bias_one = norm_one_back(grad_normed)
        input_grads.append(grad_after + grad_inputs)
        gain_one_sum = gain_one_sum + grad_gain_one
        bias_one_sum = bias_one_sum + grad_bias_one
        gain_two_sum = gain_two_sum + grad_gain_two
        bias_two_sum = bias_two_sum + grad_bias_two
    shares = (
        lax.psum_scatter(
            grad_qkv.astype(jnp.bfloat16), "dp", scatter_dimension=0, tiled=True
        ).astype(jnp.float32),
        lax.psum_scatter(
            grad_out.astype(jnp.bfloat16), "dp", scatter_dimension=0, tiled=True
        ).astype(jnp.float32),
        lax.psum_scatter(
            gain_one_sum.astype(jnp.bfloat16), "dp", scatter_dimension=0, tiled=True
        ).astype(jnp.float32),
        lax.psum_scatter(
            bias_one_sum.astype(jnp.bfloat16), "dp", scatter_dimension=0, tiled=True
        ).astype(jnp.float32),
        lax.psum_scatter(
            gain_two_sum.astype(jnp.bfloat16), "dp", scatter_dimension=0, tiled=True
        ).astype(jnp.float32),
        lax.psum_scatter(
            bias_two_sum.astype(jnp.bfloat16), "dp", scatter_dimension=0, tiled=True
        ).astype(jnp.float32),
    )
    totals = (
        lax.psum(shares[0].astype(jnp.bfloat16), "expert").astype(jnp.float32),
        lax.psum(shares[1].astype(jnp.bfloat16), "expert").astype(jnp.float32),
        lax.psum(shares[2].astype(jnp.bfloat16), "expert").astype(jnp.float32),
        lax.psum(shares[3].astype(jnp.bfloat16), "expert").astype(jnp.float32),
        lax.psum(shares[4].astype(jnp.bfloat16), "expert").astype(jnp.float32),
        lax.psum(shares[5].astype(jnp.bfloat16), "expert").astype(jnp.float32),
    )
    expert_shares = (
        lax.psum_scatter(
            grad_in[None].astype(jnp.bfloat16), "dp", scatter_dimension=2, tiled=True
        ).astype(jnp.float32),
        lax.psum_scatter(
            grad_down[None].astype(jnp.bfloat16), "dp", scatter_dimension=1, tiled=True
        ).astype(jnp.float32),
    )
    return (
        jnp.stack(results),
        jnp.stack(input_grads),
        totals[2],
        totals[3],
        totals[0],
        totals[1],
        totals[4],
        totals[5],
        expert_shares[0],
        expert_shares[1],
    )


def solution(mesh):
    placed = (
        P(("dp", "expert"), None, None),
        P(("dp", "expert"), None),
        P(),
        P(),
        P("dp", None),
        P("dp", None),
        P(),
        P(),
        P("expert", None, None),
        P("expert", None, None),
        P(("dp", "expert"), None, None),
    )
    return jax.shard_map(
        on_device,
        mesh=mesh,
        in_specs=placed,
        out_specs=(
            P(("dp", "expert"), None, None),
            P(("dp", "expert"), None, None),
            P("dp"),
            P("dp"),
            P("dp", None),
            P("dp", None),
            P("dp"),
            P("dp"),
            P("expert", None, "dp"),
            P("expert", "dp", None),
        ),
        check_vma=False,
    )
```

profile of v0, /device:TPU:0, one launch (start us, length us, event | category | flops | bytes accessed | tf_op | source)
XLA Modules:
  0.0 1065.5 jit_solution(10757684666629724084)
XLA Ops:
  25.8 56.5 %all-gather.3.cloned.1.call-done = bf16[768,2304]{1,0:T(8,128)(2,1)} async-done(((bf16[192,2304]{1,0:T(8,128)(2,1)}), bf16[768,2304]{1,0:T(8,128)(2,1)}) %all-gather.3.cloned.1.call-update) | async-done | bytes 3538960 | tf_op jit(solution)/shard_map/all_gather | solution.py:115
  130.9 22.3 %fusion = (f32[12,512]{1,0:T(8,128)S(1)}, f32[12,512]{1,0:T(8,128)}, f32[12,512,1024]{2,1,0:T(8,128)}) fusion(f32[12,512]{1,0:T(8,128)S(1)} %get-tuple-element.198, f32[12,512,1024]{2,1,0:T(8,128)} %get-tuple-element.199, pred[512,1024]{1,0:T(8,128)(4,1)} %iota_compare_fusion, bf16[1024,3,12,64]{0,3,2,1:T(8,128)(2,1)} %bitcast.389), kind=kOutput, calls=%fused_computation.26 | convolution fusion | flops 849334272 | bytes 53288960 | tf_op jit(solution)/shard_map/qhd,khd->hqk/dot_general | solution.py:41
  153.2 12.8 %fusion.154 = bf16[12,64,512]{2,1,0:T(8,128)(2,1)} fusion(f32[12,512]{1,0:T(8,128)S(1)} %get-tuple-element.160, f32[12,512]{1,0:T(8,128)S(1)} %get-tuple-element.198, f32[12,512,1024]{2,1,0:T(8,128)} %get-tuple-element.199, pred[512,1024]{1,0:T(8,128)(4,1)} %iota_compare_fusion, bf16[1024,3,12,64]{0,3,2,1:T(8,128)(2,1)} %bitcast.378), kind=kOutput, calls=%fused_computation.229 | convolution fusion | flops 837156864 | bytes 28098560 | tf_op jit(solution)/shard_map/hqk,khd->qhd/dot_general | solution.py:65
  208.4 18.9 %all-to-all-done = bf16[8,160,768]{2,1,0:T(8,128)(2,1)} async-done(((bf16[8,160,768]{2,1,0:T(8,128)(2,1)}), bf16[8,160,768]{2,1,0:T(8,128)(2,1)}, u32[]{:S(2)}, u32[]{:S(2)}) %all-to-all-start) | async-done | bytes 1966112 | tf_op jit(solution)/shard_map/all_to_all | solution.py:177
  245.1 12.6 %fusion.84 = bf16[1280,768]{1,0:T(8,128)(2,1)} fusion(bf16[1,3072,768]{2,1,0:T(8,128)(2,1)} %param.44, f32[1280,3072]{1,0:T(8,128)S(1)} %fusion.52), kind=kOutput, calls=%fused_computation.141 | convolution fusion | flops 6076170240 | bytes 22413312 | tf_op jit(solution)/shard_map/dot_general | solution.py:182
  263.5 18.5 %fusion.10 = bf16[1280,3072]{1,0:T(8,128)(2,1)S(1)} fusion(f32[1280,3072]{1,0:T(8,128)} %copy-done.105, bf16[1280,768]{1,0:T(8,128)(2,1)} %bitcast.413, bf16[1,3072,768]{2,1,0:T(8,128)(2,1)} %param.44), kind=kOutput, calls=%fused_computation.36 | convolution fusion | flops 6118440960 | bytes 30277632 | tf_op jit(solution)/shard_map/dot_general | solution.py:200
  309.4 15.3 %all-to-all-done.5 = bf16[8,160,768]{2,1,0:T(8,128)(2,1)} async-done(((bf16[8,160,768]{2,1,0:T(8,128)(2,1)}), bf16[8,160,768]{2,1,0:T(8,128)(2,1)}, u32[]{:S(2)}, u32[]{:S(2)}) %all-to-all-start.5) | async-done | bytes 1966112 | tf_op jit(solution)/shard_map/all_to_all | solution.py:214
  345.3 13.0 %multiply_reduce_fusion.3 = (f32[12,512]{1,0:T(8,128)}, f32[12,512]{1,0:T(8,128)S(1)}, f32[12,512,512]{1,2,0:T(8,128)}) fusion(f32[12,512]{1,0:T(8,128)S(1)} %log_add_fusion.3, f32[12,512,512]{1,2,0:T(8,128)S(1)} %bitcast.374, pred[512,512]{0,1:T(8,128)(4,1)S(1)} %iota_compare_fusion.1, f32[12,512]{1,0:T(8,128)S(1)} %copy-done.75, ...), kind=kOutput, calls=%fused_computation.54 | convolution fusion | flops 430952448 | bytes 39682048 | tf_op jit(solution)/shard_map/qhd,khd->hqk/dot_general | solution.py:96
  366.9 28.6 %multiply_reduce_fusion.1 = (f32[12,512]{1,0:T(8,128)}, f32[12,512]{1,0:T(8,128)S(1)}, f32[12,512,1024]{2,1,0:T(8,128)}) fusion(f32[12,512]{1,0:T(8,128)S(1)} %log_add_fusion.2, f32[12,512,1024]{2,1,0:T(8,128)} %get-tuple-element.199, pred[512,1024]{1,0:T(8,128)(4,1)S(1)} %copy-done.23, f32[12,512]{1,0:T(8,128)S(1)} %copy-done.74, ...), kind=kOutput, calls=%fused_computation.14 | convolution fusion | flops 861917184 | bytes 78479360 | tf_op jit(solution)/shard_map/qhd,khd->hqk/dot_general | solution.py:96
  395.5 12.1 %fusion.153 = bf16[12,64,512]{2,1,0:T(8,128)(2,1)S(1)} fusion(f32[12,512]{1,0:T(8,128)S(1)} %get-tuple-element.159, f32[12,512]{1,0:T(8,128)S(1)} %copy-done.74, f32[12,512,1024]{2,1,0:T(8,128)} %get-tuple-element.200, pred[512,1024]{1,0:T(8,128)(4,1)S(1)} %copy-done.23, bf16[1024,3,12,64]{0,3,2,1:T(8,128)(2,1)S(1)} %bitcast.398), kind=kOutput, calls=%fused_computation.228 | convolution fusion | flops 837156864 | bytes 28114944 | tf_op jit(solution)/shard_map/hqk,khd->qhd/dot_general | solution.py:65
  463.6 12.5 %fusion.87 = bf16[1280,768]{1,0:T(8,128)(2,1)} fusion(bf16[1,3072,768]{2,1,0:T(8,128)(2,1)} %param.44, f32[1280,3072]{1,0:T(8,128)S(1)} %fusion.50), kind=kOutput, calls=%fused_computation.142 | convolution fusion | flops 6076170240 | bytes 22413312 | tf_op jit(solution)/shard_map/dot_general | solution.py:182
  476.1 19.2 %fusion.17 = bf16[1280,3072]{1,0:T(8,128)(2,1)} fusion(f32[1280,3072]{1,0:T(8,128)} %copy-done.106, bf16[1280,768]{1,0:T(8,128)(2,1)S(1)} %bitcast.415, bf16[1,3072,768]{2,1,0:T(8,128)(2,1)} %param.44), kind=kOutput, calls=%fused_computation.43 | convolution fusion | flops 6118440960 | bytes 30277632 | tf_op jit(solution)/shard_map/dot_general | solution.py:200
  510.5 14.2 %all-to-all-done.3 = bf16[8,160,768]{2,1,0:T(8,128)(2,1)S(1)} async-done(((bf16[8,160,768]{2,1,0:T(8,128)(2,1)}), bf16[8,160,768]{2,1,0:T(8,128)(2,1)S(1)}, u32[]{:S(2)}, u32[]{:S(2)}) %all-to-all-start.3) | async-done | bytes 1966112 | tf_op jit(solution)/shard_map/all_to_all | solution.py:191
  529.3 13.5 %fusion.114 = bf16[1024,1,12,64]{0,3,2,1:T(8,128)(2,1)} fusion(f32[512,12,64]{0,2,1:T(8,128)} %fusion.145, bf16[512,12,64]{0,2,1:T(8,128)(2,1)} %bitcast.421, f32[12,512]{1,0:T(8,128)S(1)} %copy-done.46, f32[12,512,1024]{2,1,0:T(8,128)} %get-tuple-element.199, pred[512,1024]{1,0:T(8,128)(4,1)S(1)} %copy-done.23), kind=kOutput, calls=%fused_computation.172 | convolution fusion | flops 832045056 | bytes 29646848 | tf_op jit(solution)/shard_map/hqk,qhd->khd/dot_general | solution.py:89
  586.6 21.5 %multiply_convert_fusion.4 = (bf16[12,512,512]{1,2,0:T(8,128)(2,1)}, bf16[12,512,512]{1,2,0:T(8,128)(2,1)S(1)}) fusion(f32[12,512,512]{1,2,0:T(8,128)} %get-tuple-element.211, f32[12,512]{1,0:T(8,128)S(1)} %get-tuple-element.210, f32[12,512]{1,0:T(8,128)S(1)} %log_add_fusion.1, f32[12,512,512]{1,2,0:T(8,128)} %get-tuple-element.203, ...), kind=kLoop, calls=%fused_computation.49 | loop fusion | flops 37748736 | bytes 63275008 | tf_op jit(solution)/shard_map/convert_element_type | solution.py:100
  627.4 20.7 %multiply_reduce_fusion = (f32[12,512]{1,0:T(8,128)S(1)}, f32[12,512,1024]{2,1,0:T(8,128)}) fusion(f32[12,512]{1,0:T(8,128)S(1)} %log_add_fusion, f32[12,512,1024]{2,1,0:T(8,128)} %get-tuple-element.200, pred[512,1024]{1,0:T(8,128)(4,1)S(1)} %copy-done.24, bf16[512,12,64]{0,2,1:T(8,128)(2,1)S(1)} %bitcast.412, bf16[1024,3,12,64]{0,3,2,1:T(8,128)(2,1)} %bitcast.395), kind=kOutput, calls=%fused_computation.11 | convolution fusion | flops 836757504 | bytes 53264384 | tf_op jit(solution)/shard_map/qhd,khd->hqk/dot_general | solution.py:96
  648.1 13.7 %fusion.112 = bf16[1024,1,12,64]{0,3,2,1:T(8,128)(2,1)} fusion(f32[512,12,64]{0,2,1:T(8,128)} %fusion.148, bf16[512,12,64]{0,2,1:T(8,128)(2,1)} %bitcast.411, f32[12,512]{1,0:T(8,128)S(1)} %log_add_fusion, f32[12,512,1024]{2,1,0:T(8,128)} %get-tuple-element.200, pred[512,1024]{1,0:T(8,128)(4,1)S(1)} %copy-done.24), kind=kOutput, calls=%fused_computation.168 | convolution fusion | flops 832045056 | bytes 29646848 | tf_op jit(solution)/shard_map/hqk,qhd->khd/dot_general | solution.py:89
  661.8 41.8 %multiply_convert_fusion = (bf16[12,512,1024]{2,1,0:T(8,128)(2,1)}, bf16[12,512,1024]{2,1,0:T(8,128)(2,1)}) fusion(f32[12,512,1024]{2,1,0:T(8,128)} %get-tuple-element.213, f32[12,512]{1,0:T(8,128)S(1)} %get-tuple-element.212, f32[12,512]{1,0:T(8,128)S(1)} %log_add_fusion, f32[12,512,1024]{2,1,0:T(8,128)} %get-tuple-element.200, ...), kind=kLoop, calls=%fused_computation.10 | loop fusion | flops 75497472 | bytes 126451712 | tf_op jit(solution)/shard_map/convert_element_type | solution.py:100
  756.9 15.1 %fusion.204 = f32[3072,768]{1,0:T(8,128)} fusion(bf16[1280,768]{1,0:T(8,128)(2,1)} %bitcast.414, f32[1280,3072]{1,0:T(8,128)} %copy-done.105), kind=kOutput, calls=%fused_computation.335 | convolution fusion | flops 6075187200 | bytes 27131904 | tf_op jit(solution)/shard_map/dot_general | solution.py:203
  772.0 48.1 %reduce-scatter.5.cloned.1.call-done = bf16[192,2304]{1,0:T(8,128)(2,1)} async-done(((bf16[768,2304]{1,0:T(8,128)(2,1)}), bf16[192,2304]{1,0:T(8,128)(2,1)}) %reduce-scatter.5.cloned.1.call-update) | async-done | bytes 884752 | tf_op jit(solution)/shard_map/reduce_scatter | solution.py:247
  820.2 15.2 %fusion.55 = bf16[1,3072,768]{2,1,0:T(8,128)(2,1)} fusion(f32[3072,768]{1,0:T(8,128)} %fusion.204, bf16[1280,768]{1,0:T(8,128)(2,1)} %bitcast.416, f32[1280,3072]{1,0:T(8,128)} %copy-done.106), kind=kOutput, calls=%fused_computation.116 | convolution fusion | flops 6079905792 | bytes 31850496 | tf_op jit(solution)/shard_map/dot_general | solution.py:203
  887.9 11.9 %all-reduce.12 = (bf16[192]{0:T(256)(128)(2,1)S(1)}, bf16[192]{0:T(256)(128)(2,1)S(1)}, bf16[192]{0:T(256)(128)(2,1)S(1)}, bf16[192]{0:T(256)(128)(2,1)S(1)}) all-reduce(bf16[192]{0:T(256)(128)(2,1)S(1)} %dynamic-slice.51, bf16[192]{0:T(256)(128)(2,1)S(1)} %dynamic-slice.53, ...), channel_id=1, replica_groups=mesh['dp'=4,'expert'=8] {'expert'}, use_global_device_ids=true, to_apply=%region_39.40 | all-reduce | flops 768 | bytes 3072 | tf_op jit(solution)/shard_map/psum | solution.py:269
  923.0 44.3 %reduce-scatter.11.cloned.1.call-done = bf16[1,768,768]{2,1,0:T(8,128)(2,1)} async-done(((bf16[1,3072,768]{2,1,0:T(8,128)(2,1)}), bf16[1,768,768]{2,1,0:T(8,128)(2,1)}) %reduce-scatter.11.cloned.1.call-update) | async-done | bytes 1179664 | tf_op jit(solution)/shard_map/reduce_scatter | solution.py:278
  970.2 85.4 %reduce-scatter.9.cloned.1.call-done = bf16[1,768,768]{2,1,0:T(8,128)(2,1)} async-done(((bf16[1,768,3072]{2,1,0:T(8,128)(2,1)}), bf16[1,768,768]{2,1,0:T(8,128)(2,1)}) %reduce-scatter.9.cloned.1.call-update) | async-done | bytes 1179664 | tf_op jit(solution)/shard_map/reduce_scatter | solution.py:275
  (410 shorter events, 461.1 us)
Async XLA Ops:
  7.2 75.1 %all-gather.3.cloned.1.call-start = ((), (), s32[]{:S(2)}) async-start(), calls=%async_computation.12 | async-start | bytes 4423680 | tf_op jit(solution)/shard_map/all_gather | solution.py:115
  7.9 179.3 %all-gather.5.cloned.1.call-start = ((), (), s32[]{:S(2)}) async-start(), calls=%async_computation.13 | async-start | bytes 1474560 | tf_op jit(solution)/shard_map/all_gather | solution.py:116
  9.6 72.7 %copy-start.81 = (f32[768]{0:T(1024)S(1)}, f32[768]{0:T(1024)}, u32[]{:S(2)}) copy-start(f32[768]{0:T(1024)} %param.37) | copy-start | bytes 9220
  9.6 72.7 %copy-start.96 = (f32[768]{0:T(1024)S(1)}, f32[768]{0:T(1024)}, u32[]{:S(2)}) copy-start(f32[768]{0:T(1024)} %param.38) | copy-start | bytes 9220
  12.0 78.7 %copy-start.47 = (f32[1024]{0:T(1024)}, f32[1024]{0:T(1024)S(1)}, u32[]{:S(2)}) copy-start(f32[1024]{0:T(1024)S(1)} %get-tuple-element.215) | copy-start | bytes 12292
  12.0 85.3 %copy-start.49 = (f32[1024]{0:T(1024)}, f32[1024]{0:T(1024)S(1)}, u32[]{:S(2)}) copy-start(f32[1024]{0:T(1024)S(1)} %get-tuple-element.216) | copy-start | bytes 12292
  13.4 83.9 %copy-start.55 = (f32[1024]{0:T(1024)}, f32[1024]{0:T(1024)S(1)}, u32[]{:S(2)}) copy-start(f32[1024]{0:T(1024)S(1)} %fusion.178) | copy-start | bytes 12292
  13.5 77.2 %copy-start.57 = (f32[1024]{0:T(1024)}, f32[1024]{0:T(1024)S(1)}, u32[]{:S(2)}) copy-start(f32[1024]{0:T(1024)S(1)} %fusion.180) | copy-start | bytes 12292
  20.3 70.3 %copy-start.90 = (s32[1024,1]{0,1:T(1,128)}, s32[1024,1]{0,1:T(1,128)S(1)}, u32[]{:S(2)}) copy-start(s32[1024,1]{0,1:T(1,128)S(1)} %get-tuple-element.195) | copy-start | bytes 12292
  197.2 30.1 %all-to-all-start = ((bf16[8,160,768]{2,1,0:T(8,128)(2,1)}), bf16[8,160,768]{2,1,0:T(8,128)(2,1)}, u32[]{:S(2)}, u32[]{:S(2)}) async-start(bf16[8,160,768]{2,1,0:T(8,128)(2,1)} %bitcast.404), calls=%async_computation | async-start | bytes 3932160 | tf_op jit(solution)/shard_map/all_to_all | solution.py:177
  227.3 30.3 %all-to-all-start.4 = ((bf16[8,160,768]{2,1,0:T(8,128)(2,1)}), bf16[8,160,768]{2,1,0:T(8,128)(2,1)S(1)}, u32[]{:S(2)}, u32[]{:S(2)}) async-start(bf16[8,160,768]{2,1,0:T(8,128)(2,1)} %bitcast.49), calls=%async_computation.4 | async-start | bytes 3932160 | tf_op jit(solution)/shard_map/all_to_all | solution.py:195
  258.9 36.0 %all-to-all-start.1 = ((bf16[8,160,768]{2,1,0:T(8,128)(2,1)}), bf16[8,160,768]{2,1,0:T(8,128)(2,1)S(1)}, u32[]{:S(2)}, u32[]{:S(2)}) async-start(bf16[8,160,768]{2,1,0:T(8,128)(2,1)} %bitcast.419), calls=%async_computation.1 | async-start | bytes 3932160 | tf_op jit(solution)/shard_map/all_to_all | solution.py:191
  294.9 29.7 %all-to-all-start.5 = ((bf16[8,160,768]{2,1,0:T(8,128)(2,1)}), bf16[8,160,768]{2,1,0:T(8,128)(2,1)}, u32[]{:S(2)}, u32[]{:S(2)}) async-start(bf16[8,160,768]{2,1,0:T(8,128)(2,1)} %bitcast.417), calls=%async_computation.5 | async-start | bytes 3932160 | tf_op jit(solution)/shard_map/all_to_all | solution.py:214
  304.0 62.8 %copy-start.45 = (f32[12,512]{1,0:T(8,128)}, f32[12,512]{1,0:T(8,128)S(1)}, u32[]{:S(2)}) copy-start(f32[12,512]{1,0:T(8,128)S(1)} %log_add_fusion.2) | copy-start | bytes 73732
  416.0 29.6 %all-to-all-start.2 = ((bf16[8,160,768]{2,1,0:T(8,128)(2,1)}), bf16[8,160,768]{2,1,0:T(8,128)(2,1)}, u32[]{:S(2)}, u32[]{:S(2)}) async-start(bf16[8,160,768]{2,1,0:T(8,128)(2,1)} %bitcast.403), calls=%async_computation.2 | async-start | bytes 3932160 | tf_op jit(solution)/shard_map/all_to_all | solution.py:177
  445.5 30.6 %all-to-all-start.6 = ((bf16[8,160,768]{2,1,0:T(8,128)(2,1)}), bf16[8,160,768]{2,1,0:T(8,128)(2,1)S(1)}, u32[]{:S(2)}, u32[]{:S(2)}) async-start(bf16[8,160,768]{2,1,0:T(8,128)(2,1)} %bitcast.67), calls=%async_computation.6 | async-start | bytes 3932160 | tf_op jit(solution)/shard_map/all_to_all | solution.py:195
  495.3 29.4 %all-to-all-start.3 = ((bf16[8,160,768]{2,1,0:T(8,128)(2,1)}), bf16[8,160,768]{2,1,0:T(8,128)(2,1)S(1)}, u32[]{:S(2)}, u32[]{:S(2)}) async-start(bf16[8,160,768]{2,1,0:T(8,128)(2,1)} %bitcast.420), calls=%async_computation.3 | async-start | bytes 3932160 | tf_op jit(solution)/shard_map/all_to_all | solution.py:191
  524.7 29.8 %all-to-all-start.7 = ((bf16[8,160,768]{2,1,0:T(8,128)(2,1)}), bf16[8,160,768]{2,1,0:T(8,128)(2,1)}, u32[]{:S(2)}, u32[]{:S(2)}) async-start(bf16[8,160,768]{2,1,0:T(8,128)(2,1)} %bitcast.418), calls=%async_computation.7 | async-start | bytes 3932160 | tf_op jit(solution)/shard_map/all_to_all | solution.py:214
  529.3 242.7 %reduce-scatter.7.cloned.1.call-start = ((), (), s32[]{:S(2)}) async-start(), calls=%async_computation.15 | async-start | bytes 1474560 | tf_op jit(solution)/shard_map/reduce_scatter | solution.py:250
  627.3 192.7 %reduce-scatter.5.cloned.1.call-start = ((), (), s32[]{:S(2)}) async-start(), calls=%async_computation.14 | async-start | bytes 4423680 | tf_op jit(solution)/shard_map/reduce_scatter | solution.py:247
  648.1 55.5 %slice-start.10 = ((s8[4718592]{0:T(1024)(128)(4,1)}), s8[4194304]{0:T(1024)(128)(4,1)S(1)}, s32[]{:S(2)}) async-start(s8[4718592]{0:T(1024)(128)(4,1)} %bitcast.399), calls=%async_computation.29 | async-start | bytes 8388608
  756.9 161.8 %all-reduce.17.cloned.1.call-start = ((), (), s32[]{:S(2)}) async-start(), calls=%async_computation.18 | async-start | bytes 2359296 | tf_op jit(solution)/shard_map/psum | solution.py:267
  820.1 147.2 %reduce-scatter.11.cloned.1.call-start = ((), (), s32[]{:S(2)}) async-start(), calls=%async_computation.17 | async-start | bytes 5898240 | tf_op jit(solution)/shard_map/reduce_scatter | solution.py:278
  835.4 220.2 %reduce-scatter.9.cloned.1.call-start = ((), (), s32[]{:S(2)}) async-start(), calls=%async_computation.16 | async-start | bytes 5898240 | tf_op jit(solution)/shard_map/reduce_scatter | solution.py:275
  (110 other events, 783.8 us)
Sparse Core Ops, SparseCore 0:
  9.6 72.6 all-gather.2
  83.9 29.0 all-gather.4
  627.5 26.0 reduce-scatter.6
  757.0 63.0 reduce-scatter.4
  823.2 57.5 all-reduce.16
  883.0 84.3 reduce-scatter.10
  969.8 85.7 reduce-scatter.8
where the time goes:
time: 1070 us
  matrix products  464 us (43%)
  waiting for transfers between devices  297 us (28%)
  other arithmetic  121 us (11%)
  local copies, waits for them, and re-layouts  109 us (10%)
  starting transfers between devices  34.5 us (3%)
  blocking collectives  22.9 us (2%)
  between operations  16.5 us (2%)
    reduce_scatter x1, waiting for transfers between devices, on_device(): lax.psum_scatter(grad_in[None].astype(jnp.bfloat16), 'dp', scatter_dimens...  85.4 us
    dot_general x4, matrix products, attention_backward(): jnp.einsum('qhd,khd->hqk', grad_part, value_part, preferred_element_type=...  70.2 us
    convert_element_type x2, other arithmetic, attention_backward(): grad_scores = (prob_rows * (grad_prob - inner_sum)).astype(jnp.bfloat16)  63.3 us
    all_gather x1, waiting for transfers between devices, fetch_weights(): lax.all_gather(w_qkv, 'dp', axis=0, tiled=True)  56.5 us
    dot_general x4, matrix products, causal_scores(): jnp.einsum('qhd,khd->hqk', query_part, key_part, preferred_element_type=j...  52.6 us
    reduce_scatter x1, waiting for transfers between devices, on_device(): lax.psum_scatter(grad_qkv.astype(jnp.bfloat16), 'dp', scatter_dimension=0...  48.1 us
    reduce_scatter x1, waiting for transfers between devices, on_device(): lax.psum_scatter(grad_down[None].astype(jnp.bfloat16), 'dp', scatter_dime...  44.3 us
    dot_general x4, matrix products, attention_forward(): jnp.einsum('hqk,khd->qhd', weights, split_qkv[:last_row, 2], preferred_el...  42.7 us
  transfers between devices with their start and end apart: 15, of which 9 were waited for; matrix products, arithmetic and copies ran while one was open for 44% of the time, Pallas kernels for 0%

commit v1 on v0

v1 whole, which is shorter than its diff:
```python
import functools

import jax
import jax.numpy as jnp
from jax import lax
from jax.experimental import pallas as pl
from jax.experimental.pallas import tpu as pltpu
from jax.sharding import PartitionSpec as P

HEADS = 12
EPS = 1e-5
NEG = -1e30
bf16 = jnp.bfloat16
f32 = jnp.float32
NN = (((1,), (0,)), ((), ()))
NT = (((1,), (1,)), ((), ()))
TN = (((0,), (0,)), ((), ()))
GELU_A = 0.7978845608028654
GELU_B = 0.044715
BLK = 256
FFT = 256


def dot(a, b, dims=NN):
    return lax.dot_general(a, b, dims, preferred_element_type=f32)


def params(mib=56):
    return pltpu.CompilerParams(vmem_limit_bytes=mib << 20)


def cost(flops, nbytes, trans=0):
    return pl.CostEstimate(flops=int(flops), bytes_accessed=int(nbytes), transcendentals=int(trans))


def sds(shape, dtype):
    return jax.ShapeDtypeStruct(shape, dtype)


VM = pl.BlockSpec(memory_space=pltpu.VMEM)


def norm_parts(v):
    centre = jnp.mean(v, axis=-1, keepdims=True)
    shifted = v - centre
    spread = jnp.mean(shifted * shifted, axis=-1, keepdims=True)
    r = lax.rsqrt(spread + EPS)
    return shifted * r, r


def qkv_body(x_ref, g_ref, b_ref, w_ref, o_ref):
    hat, _ = norm_parts(x_ref[0].astype(f32))
    low = (hat * g_ref[...] + b_ref[...]).astype(bf16)
    o_ref[0] = dot(low, w_ref[...]).astype(bf16)


def qkv_call(x, gain, bias, w):
    n, length, width = x.shape
    triple = w.shape[1]
    rows = min(512, length)
    row = pl.BlockSpec((1, width), lambda s, r: (0, 0))
    return pl.pallas_call(
        qkv_body,
        grid=(n, length // rows),
        in_specs=[
            pl.BlockSpec((1, rows, width), lambda s, r: (s, r, 0)),
            row,
            row,
            pl.BlockSpec((width, triple), lambda s, r: (0, 0)),
        ],
        out_specs=pl.BlockSpec((1, rows, triple), lambda s, r: (s, r, 0)),
        out_shape=sds((n, length, triple), bf16),
        compiler_params=params(),
        cost_estimate=cost(2 * n * length * width * triple, n * length * (width + triple) * 2),
    )(x, gain.reshape(1, -1), bias.reshape(1, -1), w)


def attn_fwd_body(q_ref, k_ref, v_ref, o_ref, lse_ref, *, blk, hs, scale, depth):
    length = q_ref.shape[1]
    lane = lax.broadcasted_iota(jnp.int32, (1, 2 * hs), 1) // hs
    v_t = v_ref[0].T
    keys = k_ref[0]
    kh = [jnp.where(lane == h, keys, jnp.zeros_like(keys)) for h in range(2)]
    ones = jnp.ones((16, length), bf16)
    vh = [jnp.concatenate([v_t[h * hs : (h + 1) * hs], ones], axis=0) for h in range(2)]
    future = lax.broadcasted_iota(jnp.int32, (blk, blk), 0) > lax.broadcasted_iota(
        jnp.int32, (blk, blk), 1
    )
    tasks = [(i, h) for i in range(length // blk) for h in range(2)]

    def score(task):
        i, h = task
        top = (i + 1) * blk
        q = q_ref[0, i * blk : top, :] * jnp.asarray(scale, bf16)
        s = dot(kh[h][:top], q, NT)
        diag = jnp.where(future, NEG, s[i * blk :])
        s = jnp.concatenate([s[: i * blk], diag], axis=0) if i else diag
        return s, jnp.max(s, axis=0, keepdims=True)

    queue = [score(t) for t in tasks[:depth]]
    done = {}
    for at, task in enumerate(tasks):
        if at + depth < len(tasks):
            queue.append(score(tasks[at + depth]))
        s, largest = queue.pop(0)
        i, h = task
        top = (i + 1) * blk
        o = dot(vh[h][:, :top], jnp.exp(s - largest).astype(bf16))
        total = o[hs : hs + 1]
        done[task] = o[:hs] * (1.0 / total)
        lse_ref[0, 0, h : h + 1, i * blk : top] = largest + jnp.log(total)
        if h == 1:
            both = jnp.concatenate([done[(i, 0)], done[(i, 1)]], axis=0)
            o_ref[0, i * blk : top, :] = both.T.astype(bf16)


def attn_fwd_call(qkv, heads):
    n, length, triple = qkv.shape
    width = triple // 3
    hs = width // heads
    pairs = heads // 2
    blk = min(BLK, length)

    def spec(o):
        return pl.BlockSpec((1, length, 2 * hs), lambda s, p, o=o: (s, 0, o * pairs + p))

    half = n * heads * length * length // 2
    return pl.pallas_call(
        functools.partial(attn_fwd_body, blk=blk, hs=hs, scale=hs**-0.5, depth=3),
        grid=(n, pairs),
        in_specs=[spec(0), spec(1), spec(2)],
        out_specs=[spec(0), pl.BlockSpec((1, 1, 2, length), lambda s, p: (s, p, 0, 0))],
        out_shape=[sds((n, length, width), bf16), sds((n, pairs, 2, length), f32)],
        compiler_params=params(48),
        cost_estimate=cost(half * 2 * 2 * 256, n * length * width * 8, half),
    )(qkv, qkv, qkv)


def attn_bwd_body(
    q_ref, k_ref, v_ref, o_ref, do_ref, lse_ref, dq_ref, dk_ref, dv_ref, dqa, doa, *, blk, hs, scale, depth
):
    length = q_ref.shape[1]
    n = length // blk
    lanes = lax.broadcasted_iota(jnp.int32, (1, 2 * hs), 1)
    lane = lanes // hs
    spot = lanes % hs
    keys = k_ref[0]
    vals = v_ref[0]
    k_t = (keys * jnp.asarray(scale, bf16)).T
    kh = [jnp.where(lane == h, keys, jnp.zeros_like(keys)) for h in range(2)]
    vh = [
        jnp.where(lane == h, vals, jnp.where(spot < 2, jnp.ones_like(vals), jnp.zeros_like(vals)))
        for h in range(2)
    ]
    future = lax.broadcasted_iota(jnp.int32, (blk, blk), 0) > lax.broadcasted_iota(
        jnp.int32, (blk, blk), 1
    )
    q = q_ref[0] * jnp.asarray(scale, bf16)
    do = do_ref[0]
    prod = do.astype(f32) * o_ref[0].astype(f32)
    for h in range(2):
        inside = lane == h
        inner = -jnp.sum(jnp.where(inside, prod, 0.0), axis=1, keepdims=True)
        high = inner.astype(bf16)
        rest = (inner - high.astype(f32)).astype(bf16)
        doa[h] = jnp.where(
            inside,
            do,
            jnp.where(spot == 0, high, jnp.where(spot == 1, rest, jnp.zeros_like(high))),
        )
    tasks = [(j, h) for j in range(n) for h in range(2)]

    def score(task):
        j, h = task
        a = j * blk
        return (
            dot(kh[h][a : a + blk], q[a:], NT),
            dot(vh[h][a : a + blk], doa[h, a:], NT),
        )

    queue = [score(t) for t in tasks[:depth]]
    kept = None
    for at, task in enumerate(tasks):
        if at + depth < len(tasks):
            queue.append(score(tasks[at + depth]))
        s, dp = queue.pop(0)
        j, h = task
        a = j * blk
        p = jnp.exp(s - lse_ref[0, 0, h : h + 1, a:])
        diag = jnp.where(future, 0.0, p[:, :blk])
        p = jnp.concatenate([diag, p[:, blk:]], axis=1) if j < n - 1 else diag
        ds = (p * dp).astype(bf16)
        dv = dot(p.astype(bf16), do[a:])
        dk = dot(ds, q[a:])
        dq = dot(k_t[h * hs : (h + 1) * hs, a : a + blk], ds)
        if j == 0:
            dqa[h * hs : (h + 1) * hs, :] = dq
        else:
            dqa[h * hs : (h + 1) * hs, a:] += dq
        if h == 0:
            kept = (dk, dv)
        else:
            dk_ref[0, a : a + blk, :] = jnp.where(lane == 0, kept[0], dk).astype(bf16)
            dv_ref[0, a : a + blk, :] = jnp.where(lane == 0, kept[1], dv).astype(bf16)
            dq_ref[0, a : a + blk, :] = dqa[:, a : a + blk].T.astype(bf16)


def attn_bwd_call(qkv, o, do, lse, heads):
    n, length, triple = qkv.shape
    width = triple // 3
    hs = width // heads
    pairs = heads // 2
    blk = min(BLK, length)

    def spec(o):
        return pl.BlockSpec((1, length, 2 * hs), lambda s, p, o=o: (s, 0, o * pairs + p))

    half = n * heads * length * length // 2
    return pl.pallas_call(
        functools.partial(attn_bwd_body, blk=blk, hs=hs, scale=hs**-0.5, depth=2),
        grid=(n, pairs),
        in_specs=[spec(0), spec(1), spec(2), spec(0), spec(0)]
        + [pl.BlockSpec((1, 1, 2, length), lambda s, p: (s, p, 0, 0))],
        out_specs=[spec(0)] * 3,
        out_shape=[sds((n, length, width), bf16)] * 3,
        scratch_shapes=[
            pltpu.VMEM((2 * hs, length), f32),
            pltpu.VMEM((2, length, 2 * hs), bf16),
        ],
        compiler_params=params(48),
        cost_estimate=cost(half * 5 * 2 * 256, n * length * width * 16, half),
    )(qkv, qkv, qkv, o, do, lse)


def slot_chunk(total):
    return 256 if total % 256 == 0 else total


def place_rows(rows, slot_row, out_ref):
    total = out_ref.shape[0]
    step = slot_chunk(total)
    length = rows.shape[0]
    base = lax.broadcasted_iota(jnp.int32, (step, length), 0)
    for at in range(0, total, step):
        hot = jnp.where(base + at == slot_row, 1.0, 0.0).astype(bf16)
        out_ref[at : at + step, :] = dot(hot, rows).astype(bf16)


def take_rows(slots, slot_col):
    total = slots.shape[0]
    at = lax.broadcasted_iota(jnp.int32, (slot_col.shape[0], total), 1)
    return dot(jnp.where(at == slot_col, 1.0, 0.0).astype(bf16), slots)


def send_body(rows_ref, slot_ref, out_ref):
    place_rows(rows_ref[...], slot_ref[...], out_ref)


def send_call(rows, slot_row, total):
    length, width = rows.shape
    return pl.pallas_call(
        send_body,
        in_specs=[VM, VM],
        out_specs=VM,
        out_shape=sds((total, width), bf16),
        compiler_params=params(32),
        cost_estimate=cost(2 * length * total * width, (length + total) * width * 2),
    )(rows, slot_row)


def out_body(x_ref, mixed_ref, w_ref, g_ref, b_ref, slot_ref, after_ref, sent_ref, toks):
    length = x_ref.shape[0]
    blk = min(BLK, length)
    for a in range(0, length, blk):
        rows = slice(a, a + blk)
        after = x_ref[rows].astype(f32) + dot(mixed_ref[rows], w_ref[...])
        after_ref[rows] = after
        hat, _ = norm_parts(after)
        toks[rows] = (hat * g_ref[...] + b_ref[...]).astype(bf16)
    place_rows(toks[...], slot_ref[...], sent_ref)


def out_call(x, mixed, w, gain, bias, slot_row, total):
    length, width = x.shape
    return pl.pallas_call(
        out_body,
        in_specs=[VM] * 6,
        out_specs=[VM] * 2,
        out_shape=[sds((length, width), f32), sds((total, width), bf16)],
        scratch_shapes=[pltpu.VMEM((length, width), bf16)],
        compiler_params=params(40),
        cost_estimate=cost(2 * length * width * (width + total), length * width * 12),
    )(x, mixed, w, gain.reshape(1, -1), bias.reshape(1, -1), slot_row)


def add_back_body(after_ref, back_ref, slot_ref, out_ref):
    length = after_ref.shape[0]
    blk = min(BLK, length)
    for a in range(0, length, blk):
        rows = slice(a, a + blk)
        out_ref[rows] = after_ref[rows] + take_rows(back_ref[...], slot_ref[rows])


def add_back_call(after, back, slot_col):
    length, width = after.shape
    total = back.shape[0]
    return pl.pallas_call(
        add_back_body,
        in_specs=[VM] * 3,
        out_specs=VM,
        out_shape=sds((length, width), f32),
        compiler_params=params(40),
        cost_estimate=cost(2 * length * width * total, length * width * 12),
    )(after, back, slot_col)


def gelu_parts(pre):
    sq = pre * pre
    half = 0.5 + 0.5 * jnp.tanh(pre * (GELU_A + (GELU_A * GELU_B) * sq))
    act = pre * half
    slope = half + (act - act * half) * (2 * GELU_A + (6 * GELU_A * GELU_B) * sq)
    return act, slope


def hidden_rows(rows_ref, cot_ref, w_in, w_down, act_ref, gpre_ref, use=None):
    total = rows_ref.shape[0]
    step = slot_chunk(total)
    starts = list(range(0, total, step))

    def first(a):
        return dot(rows_ref[a : a + step], w_in), dot(cot_ref[a : a + step], w_down, NT)

    ahead = first(starts[0])
    for at, a in enumerate(starts):
        pre, gact = ahead
        if at + 1 < len(starts):
            ahead = first(starts[at + 1])
        act, slope = gelu_parts(pre)
        act_low = act.astype(bf16)
        gpre_low = (gact * slope).astype(bf16)
        act_ref[0, a : a + step] = act_low
        gpre_ref[0, a : a + step] = gpre_low
        if use is not None:
            use(a, a + step, act_low, gpre_low)


def join_cols(refs):
    return jnp.concatenate([r[...] for r in refs], axis=1)


def join_rows(refs):
    return jnp.concatenate([r[...] for r in refs], axis=0)


def expert_a_body(*refs, nz):
    rows_ref, cot_ref = refs[:2]
    w_in = join_cols(refs[2 : 2 + nz])
    w_down = join_rows(refs[2 + nz : 2 + 2 * nz])
    act_ref, gpre_ref, out_ref, gtok_ref, acc_out, acc_tok = refs[2 + 2 * nz :]
    c = pl.program_id(0)
    last = pl.num_programs(0) - 1

    @pl.when(c == 0)
    def _():
        acc_out[...] = jnp.zeros_like(acc_out)
        acc_tok[...] = jnp.zeros_like(acc_tok)

    def use(a, b, act_low, gpre_low):
        acc_out[a:b] += dot(act_low, w_down)
        acc_tok[a:b] += dot(gpre_low, w_in, NT)

    hidden_rows(rows_ref, cot_ref, w_in, w_down, act_ref, gpre_ref, use)

    @pl.when(c == last)
    def _():
        out_ref[...] = acc_out[...].astype(bf16)
        gtok_ref[...] = acc_tok[...].astype(bf16)


def weight_specs(width, hidden, nz, first=0):
    per = hidden // (nz * FFT)
    ins = [
        pl.BlockSpec((width, FFT), lambda c, z=z: (0, z * per + c + first)) for z in range(nz)
    ]
    downs = [
        pl.BlockSpec((FFT, width), lambda c, z=z: (z * per + c + first, 0)) for z in range(nz)
    ]
    return ins + downs


def expert_a_call(rows, cot, w_in, w_down, nz):
    total, width = rows.shape
    hidden = w_in.shape[1]
    chunks = hidden // (nz * FFT)
    tile = nz * FFT
    keep = pl.BlockSpec((total, width), lambda c: (0, 0))
    mid = pl.BlockSpec((1, total, tile), lambda c: (c, 0, 0))
    return pl.pallas_call(
        functools.partial(expert_a_body, nz=nz),
        grid=(chunks,),
        in_specs=[keep, keep] + weight_specs(width, hidden, nz),
        out_specs=[mid, mid, keep, keep],
        out_shape=[sds((chunks, total, tile), bf16)] * 2 + [sds((total, width), bf16)] * 2,
        scratch_shapes=[pltpu.VMEM((total, width), f32)] * 2,
        compiler_params=params(60),
        cost_estimate=cost(8 * total * width * hidden, 30 << 20),
    )(rows, cot, *([w_in] * nz), *([w_down] * nz))


def expert_b_body(*refs, nz):
    rows_a, cot_a, act_a, gpre_a, rows_b, cot_b = refs[:6]
    w_in = join_cols(refs[6 : 6 + nz])
    w_down = join_rows(refs[6 + nz : 6 + 2 * nz])
    act_b, gpre_b, gdown_ref, gin_ref = refs[6 + 2 * nz :]
    hidden_rows(rows_b, cot_b, w_in, w_down, act_b, gpre_b)
    for z in range(nz):
        cols = slice(z * FFT, (z + 1) * FFT)
        gdown = dot(act_a[0, :, cols], cot_a[...], TN) + dot(act_b[0, :, cols], cot_b[...], TN)
        gdown_ref[z, 0] = gdown.astype(bf16)
        gin = dot(rows_a[...], gpre_a[0, :, cols], TN) + dot(rows_b[...], gpre_b[0, :, cols], TN)
        gin_ref[z, 0] = gin.astype(bf16)


def expert_b_call(rows_a, cot_a, act_a, gpre_a, rows_b, cot_b, w_in, w_down, nz, first, count):
    total, width = rows_a.shape
    hidden = w_in.shape[1]
    tile = nz * FFT
    keep = pl.BlockSpec((total, width), lambda c: (0, 0))
    mid = pl.BlockSpec((1, total, tile), lambda c: (c + first, 0, 0))
    mid_out = pl.BlockSpec((1, total, tile), lambda c: (c, 0, 0))
    return pl.pallas_call(
        functools.partial(expert_b_body, nz=nz),
        grid=(count,),
        in_specs=[keep, keep, mid, mid, keep, keep] + weight_specs(width, hidden, nz, first),
        out_specs=[
            mid_out,
            mid_out,
            pl.BlockSpec((nz, 1, FFT, width), lambda c: (0, c, 0, 0)),
            pl.BlockSpec((nz, 1, width, FFT), lambda c: (0, c, 0, 0)),
        ],
        out_shape=[
            sds((count, total, tile), bf16),
            sds((count, total, tile), bf16),
            sds((nz, count, FFT, width), bf16),
            sds((nz, count, width, FFT), bf16),
        ],
        compiler_params=params(60),
        cost_estimate=cost(12 * total * width * tile * count, 30 << 20),
    )(rows_a, cot_a, act_a, gpre_a, rows_b, cot_b, *([w_in] * nz), *([w_down] * nz))


def expert_c_body(*refs, nz, parts, dims):
    mids = refs[:parts]
    w_refs = refs[parts : parts + nz]
    out_ref, acc = refs[parts + nz :]
    w = join_cols(w_refs) if dims is NT else join_rows(w_refs)
    c = pl.program_id(0)
    total = acc.shape[0]
    step = slot_chunk(total)
    counts = [m.shape[0] for m in mids]
    lo = 0
    for m, k in zip(mids, counts):

        @pl.when((c >= lo) & (c < lo + k))
        def _(m=m, lo=lo):
            for a in range(0, total, step):
                term = dot(m[c - lo, a : a + step], w, dims)
                if lo == 0:
                    acc[a : a + step] = jnp.where(c == 0, term, acc[a : a + step] + term)
                else:
                    acc[a : a + step] += term

        lo += k

    @pl.when(c == pl.num_programs(0) - 1)
    def _():
        out_ref[...] = acc[...].astype(bf16)


def expert_c_call(mids, w, nz, dims):
    total, tile = mids[0].shape[1:]
    hidden = tile * sum(m.shape[0] for m in mids)
    width = w.shape[0] if dims is NT else w.shape[1]
    chunks = hidden // tile
    specs = weight_specs(width, hidden, nz)
    specs = specs[:nz] if dims is NT else specs[nz:]
    return pl.pallas_call(
        functools.partial(expert_c_body, nz=nz, parts=len(mids), dims=dims),
        grid=(chunks,),
        in_specs=[pl.BlockSpec(m.shape, lambda c: (0, 0, 0)) for m in mids] + specs,
        out_specs=pl.BlockSpec((total, width), lambda c: (0, 0)),
        out_shape=sds((total, width), bf16),
        scratch_shapes=[pltpu.VMEM((total, width), f32)],
        compiler_params=params(60),
        cost_estimate=cost(2 * total * width * hidden, 14 << 20),
    )(*mids, *([w] * nz))


def norm_two_body(
    back_ref, slot_ref, after_ref, cot_ref, mixed_ref, w_ref, g_ref, seed_ref, ga_ref, gmix_ref, gw_ref, sums_ref, low
):
    length = after_ref.shape[0]
    blk = min(BLK, length)
    gain_sum = 0.0
    bias_sum = 0.0
    for a in range(0, length, blk):
        rows = slice(a, a + blk)
        gt = take_rows(back_ref[...], slot_ref[rows])
        hat, r = norm_parts(after_ref[rows])
        gain_sum = gain_sum + jnp.sum(gt * hat, axis=0, keepdims=True)
        bias_sum = bias_sum + jnp.sum(gt, axis=0, keepdims=True)
        s = gt * g_ref[...]
        ga = cot_ref[rows].astype(f32) + r * (
            s
            - jnp.mean(s, axis=-1, keepdims=True)
            - hat * jnp.mean(s * hat, axis=-1, keepdims=True)
        )
        ga_ref[rows] = ga
        ga_low = ga.astype(bf16)
        low[rows] = ga_low
        gmix_ref[rows] = dot(ga_low, w_ref[...], NT).astype(bf16)
    gw_ref[...] = seed_ref[...] + dot(mixed_ref[...], low[...], TN)
    sums_ref[0:1] = gain_sum
    sums_ref[1:2] = bias_sum


def norm_two_call(back, slot_col, after, cot, mixed, w, gain, seed):
    length, width = after.shape
    total = back.shape[0]
    return pl.pallas_call(
        norm_two_body,
        in_specs=[VM] * 8,
        out_specs=[VM] * 4,
        out_shape=[
            sds((length, width), f32),
            sds((length, width), bf16),
            sds((width, width), f32),
            sds((2, width), f32),
        ],
        scratch_shapes=[pltpu.VMEM((length, width), bf16)],
        compiler_params=params(56),
        cost_estimate=cost(2 * length * width * (total + 2 * width), length * width * 20),
    )(back, slot_col, after, cot, mixed, w, gain.reshape(1, -1), seed)


def norm_one_body(
    dq_ref, dk_ref, dv_ref, x_ref, w_ref, g_ref, b_ref, ga_ref, seed_ref, gx_ref, gw_ref, sums_ref, low
):
    length, width = x_ref.shape
    blk = min(BLK, length)
    gain_sum = 0.0
    bias_sum = 0.0
    parts = (dq_ref, dk_ref, dv_ref)
    for a in range(0, length, blk):
        rows = slice(a, a + blk)
        gn = 0.0
        for t, ref in enumerate(parts):
            gn = gn + dot(ref[rows], w_ref[:, t * width : (t + 1) * width], NT)
        hat, r = norm_parts(x_ref[rows].astype(f32))
        low[rows] = (hat * g_ref[...] + b_ref[...]).astype(bf16)
        gain_sum = gain_sum + jnp.sum(gn * hat, axis=0, keepdims=True)
        bias_sum = bias_sum + jnp.sum(gn, axis=0, keepdims=True)
        s = gn * g_ref[...]
        gx_ref[rows] = ga_ref[rows] + r * (
            s
            - jnp.mean(s, axis=-1, keepdims=True)
            - hat * jnp.mean(s * hat, axis=-1, keepdims=True)
        )
    for t, ref in enumerate(parts):
        cols = slice(t * width, (t + 1) * width)
        term = dot(low[...], ref[...], TN)
        if seed_ref is None:
            gw_ref[:, cols] = term.astype(gw_ref.dtype)
        else:
            gw_ref[:, cols] = (seed_ref[:, cols] + term).astype(gw_ref.dtype)
    sums_ref[0:1] = gain_sum
    sums_ref[1:2] = bias_sum


def norm_one_call(dq, dk, dv, x, w, gain, bias, ga, seed):
    length, width = x.shape
    args = [dq, dk, dv, x, w, gain.reshape(1, -1), bias.reshape(1, -1), ga]
    if seed is None:

        def body(*refs):
            norm_one_body(*refs[:8], None, *refs[8:])

        kind = f32
    else:
        args.append(seed)
        body = norm_one_body
        kind = bf16
    return pl.pallas_call(
        body,
        in_specs=[VM] * len(args),
        out_specs=[VM] * 3,
        out_shape=[sds((length, width), f32), sds((width, 3 * width), kind), sds((2, width), f32)],
        scratch_shapes=[pltpu.VMEM((length, width), bf16)],
        compiler_params=params(60),
        cost_estimate=cost(12 * length * width * width, length * width * 30),
    )(*args)


def gather_line(x, axis):
    size = lax.axis_size(axis)
    me = lax.axis_index(axis)
    up = [(i, i + 1) for i in range(size - 1)]
    down = [(i + 1, i) for i in range(size - 1)]
    full = jnp.zeros((size,) + x.shape, x.dtype)
    full = lax.dynamic_update_index_in_dim(full, x, me, 0)
    from_below = from_above = x
    for step in range(1, size):
        from_below = lax.ppermute(from_below, axis, up)
        from_above = lax.ppermute(from_above, axis, down)
        low = jnp.where(me >= step, me - step, me)
        high = jnp.where(me + step < size, me + step, me)
        own = lax.dynamic_index_in_dim(full, me, 0, keepdims=False)
        full = lax.dynamic_update_index_in_dim(
            full, jnp.where(me >= step, from_below, own), low, 0
        )
        full = lax.dynamic_update_index_in_dim(
            full, jnp.where(me + step < size, from_above, own), high, 0
        )
    return full


def exchange(x, experts, capacity):
    parts = x.reshape(experts, capacity, x.shape[-1])
    got = lax.all_to_all(parts, "expert", split_axis=0, concat_axis=0, tiled=True)
    return got.reshape(x.shape)


def on_device(
    tokens_in,
    buckets,
    ln1_gain,
    ln1_bias,
    w_qkv,
    w_out,
    ln2_gain,
    ln2_bias,
    w_in,
    w_down,
    cotangent,
):
    experts = lax.axis_size("expert")
    nz = lax.axis_size("dp")
    seqs, length, width = tokens_in.shape
    capacity = 5 * length // (4 * experts)
    total = experts * capacity
    w_in_local = w_in[0]
    w_down_local = w_down[0]
    hidden = w_in_local.shape[1]
    chunks = hidden // (nz * FFT)

    hot = (buckets[:, None, :] == jnp.arange(experts, dtype=jnp.int32)[None, :, None]).astype(bf16)
    upto = (
        jnp.arange(length, dtype=jnp.int32)[:, None] <= jnp.arange(length, dtype=jnp.int32)[None, :]
    ).astype(bf16)
    count = jnp.einsum("sel,lm->sem", hot, upto, preferred_element_type=f32)
    rank = jnp.sum(count * hot.astype(f32), axis=1).astype(jnp.int32) - 1
    slot = buckets * capacity + rank
    slot_row = slot[:, None, :]
    slot_col = slot[:, :, None]

    full_qkv = lax.all_gather(w_qkv, "dp", axis=0, tiled=True)
    full_out = lax.all_gather(w_out, "dp", axis=0, tiled=True)

    cots = [
        exchange(send_call(cotangent[s], slot_row[s], total), experts, capacity)
        for s in range(seqs)
    ]
    saved = []
    rows = []
    for s in range(seqs):
        qkv = qkv_call(tokens_in[s : s + 1], ln1_gain, ln1_bias, full_qkv)
        mixed, lse = attn_fwd_call(qkv, HEADS)
        after, sent = out_call(
            tokens_in[s], mixed[0], full_out, ln2_gain, ln2_bias, slot_row[s], total
        )
        rows.append(exchange(sent, experts, capacity))
        saved.append((qkv, mixed, lse, after))

    act_a, gpre_a, out_a, gtok_a = expert_a_call(rows[0], cots[0], w_in_local, w_down_local, nz)
    outs = [exchange(out_a, experts, capacity)]
    gtoks = [exchange(gtok_a, experts, capacity)]

    acts, gpres, gdowns, gins = [], [], [], []
    for first, many in ((0, 1), (1, chunks - 1)):
        act_b, gpre_b, gdown, gin = expert_b_call(
            rows[0], cots[0], act_a, gpre_a, rows[1], cots[1], w_in_local, w_down_local, nz, first, many
        )
        acts.append(act_b)
        gpres.append(gpre_b)
        gdowns.append(lax.psum_scatter(gdown, "dp", scatter_dimension=0, tiled=True))
        gins.append(lax.psum_scatter(gin, "dp", scatter_dimension=0, tiled=True))
    gtoks.append(exchange(expert_c_call(gpres, w_in_local, nz, NT), experts, capacity))
    outs.append(exchange(expert_c_call(acts, w_down_local, nz, NN), experts, capacity))

    results = []
    gxs = []
    gw_out = jnp.zeros((width, width), f32)
    gw_qkv = None
    sums = 0.0
    for s in range(seqs):
        qkv, mixed, lse, after = saved[s]
        ga, gmix, gw_out, sums_two = norm_two_call(
            gtoks[s], slot_col[s], after, cotangent[s], mixed[0], full_out, ln2_gain, gw_out
        )
        dq, dk, dv = attn_bwd_call(qkv, mixed, gmix[None], lse, HEADS)
        gx, gw_qkv, sums_one = norm_one_call(
            dq[0], dk[0], dv[0], tokens_in[s], full_qkv, ln1_gain, ln1_bias, ga, gw_qkv
        )
        gxs.append(gx)
        sums = sums + jnp.concatenate([sums_one, sums_two], axis=0)
        results.append(add_back_call(after, outs[s], slot_col[s]))

    both = ("expert", "dp")
    dense = jnp.concatenate([gw_qkv, gw_out.astype(bf16)], axis=1)
    piece = lax.psum_scatter(
        dense.reshape(nz, experts, width // nz // experts, 4 * width).swapaxes(0, 1),
        "expert",
        scatter_dimension=0,
        tiled=True,
    )
    piece = lax.psum_scatter(piece[0], "dp", scatter_dimension=0, tiled=True)
    dense = lax.all_gather(piece, "expert", axis=0, tiled=True).reshape(width // nz, 4 * width)
    dense = dense.astype(f32)
    sums = lax.psum(sums, both)
    mine = lax.dynamic_slice_in_dim(
        sums, lax.axis_index("dp") * (width // nz), width // nz, axis=1
    )
    gdown = jnp.concatenate([g[0] for g in gdowns], axis=0).reshape(1, hidden // nz, width)
    gin = jnp.concatenate([g[0, i] for g in gins for i in range(g.shape[1])], axis=1)[None]
    return (
        jnp.stack(results),
        jnp.stack(gxs),
        mine[0],
        mine[1],
        dense[:, : 3 * width],
        dense[:, 3 * width :],
        mine[2],
        mine[3],
        gin.astype(f32),
        gdown.astype(f32),
    )


def solution(mesh):
    placed = (
        P(("dp", "expert"), None, None),
        P(("dp", "expert"), None),
        P(),
        P(),
        P("dp", None),
        P("dp", None),
        P(),
        P(),
        P("expert", None, None),
        P("expert", None, None),
        P(("dp", "expert"), None, None),
    )
    return jax.shard_map(
        on_device,
        mesh=mesh,
        in_specs=placed,
        out_specs=(
            P(("dp", "expert"), None, None),
            P(("dp", "expert"), None, None),
            P("dp"),
            P("dp"),
            P("dp", None),
            P("dp", None),
            P("dp"),
            P("dp"),
            P("expert", None, "dp"),
            P("expert", "dp", None),
        ),
        check_vma=False,
    )
```

time: 1070 us -> 758 us (0.71)
  matrix products: 464 us -> 1.12 us
  Pallas kernels: 0 us -> 290 us
  other arithmetic: 121 us -> 19.6 us
  blocking collectives: 22.9 us -> 92.2 us
  local copies, waits for them, and re-layouts: 109 us -> 42.6 us
  waiting for transfers between devices: 297 us -> 260 us
    dot_general x48 -> x1, matrix products: 464 us -> 1.12 us  [on_device(): count = jnp.einsum('sel,lm->sem', hot, upto, preferred_element_type=f32)]
    pallas_call x0 -> x21, Pallas kernels: none -> 290 us  [the longest x2 57.1 us: expert_b_call(): pl.pallas_call(functools.partial(expert_b_body, nz=nz), grid=(count,), in...]
    reduce_scatter x4 -> x5, waiting for transfers between devices: 178 us -> 86.4 us  [the longest x2 86.4 us: on_device(): gins.append(lax.psum_scatter(gin, 'dp', scatter_dimension=0, tiled=True))]
    unnamed x7 -> x10, waiting for transfers between devices: 1.46 us -> 87.6 us
    convert_element_type x22 -> x4, other arithmetic: 79.2 us -> 7.45 us  [the longest x1 2.57 us: on_device(): gin.astype(f32)]
    psum x1, blocking collectives: 11.9 us -> 62.7 us  [on_device(): sums = lax.psum(sums, both)]
    gather x8 -> x0, local copies, waits for them, and re-layouts: 45.5 us -> none  [the longest x2 15.3 us: on_device(): came_back.reshape(experts * capacity, width)[slot_of].astype(jnp.float32)]
    all_to_all x8 -> x7, waiting for transfers between devices: 61.5 us -> 29.6 us  [exchange(): lax.all_to_all(parts, 'expert', split_axis=0, concat_axis=0, tiled=True)]
  transfers between devices with their start and end apart: 15 -> 16, of which waited for: 9 -> 8; matrix products, arithmetic and copies ran while one was open for 44% -> 3% of each run, Pallas kernels for 0% -> 26%
where the time goes in v1:
time: 758 us; the launch traced here: 753 us
  Pallas kernels  290 us (38%)
  waiting for transfers between devices  260 us (34%)
  blocking collectives  92.2 us (12%)
  local copies, waits for them, and re-layouts  42.6 us (6%)
  starting transfers between devices  32.1 us (4%)
  other arithmetic  19.6 us (3%)
  between operations  14.5 us (2%)
    unnamed x10, waiting for transfers between devices  87.6 us
    reduce_scatter x2, waiting for transfers between devices, on_device(): gins.append(lax.psum_scatter(gin, 'dp', scatter_dimension=0, tiled=True))  86.4 us
    psum x1, blocking collectives, on_device(): sums = lax.psum(sums, both)  62.7 us
    pallas_call x2, Pallas kernels, expert_b_call(): pl.pallas_call(functools.partial(expert_b_body, nz=nz), grid=(count,), in...  57.1 us
    pallas_call x2, Pallas kernels, attn_bwd_call(): pl.pallas_call(functools.partial(attn_bwd_body, blk=blk, hs=hs, scale=hs...  48 us
    pallas_call x1, Pallas kernels, expert_a_call(): pl.pallas_call(functools.partial(expert_a_body, nz=nz), grid=(chunks,), i...  35.7 us
    pallas_call x2, Pallas kernels, norm_one_call(): pl.pallas_call(body, in_specs=[VM] * len(args), out_specs=[VM] * 3, out_s...  33.1 us
    all_to_all x7, starting transfers between devices, exchange(): lax.all_to_all(parts, 'expert', split_axis=0, concat_axis=0, tiled=True)  31.8 us
  transfers between devices with their start and end apart: 16, of which 8 were waited for; matrix products, arithmetic and copies ran while one was open for 3% of the time, Pallas kernels for 26%

profile of v1, /device:TPU:0, one launch (start us, length us, event | category | flops | bytes accessed | tf_op | source)
XLA Modules:
  0.0 752.9 jit_solution(16138874543807459614)
XLA Ops:
  24.8 21.1 %all-to-all-done.1 = bf16[8,160,768]{2,1,0:T(8,128)(2,1)} async-done(((bf16[8,160,768]{2,1,0:T(8,128)(2,1)}), bf16[8,160,768]{2,1,0:T(8,128)(2,1)}, u32[]{:S(2)}, u32[]{:S(2)}) %all-to-all-start.1) | async-done | bytes 1966112 | tf_op jit(solution)/shard_map/all_to_all | solution.py:629
  55.5 26.8 %all-gather.4.cloned.1.call-done.w_ref.refs_4_ = bf16[768,2304]{1,0:T(8,128)(2,1)} async-done(((bf16[192,2304]{1,0:T(8,128)(2,1)}), bf16[768,2304]{1,0:T(8,128)(2,1)}) %all-gather.4.cloned.1.call-update) | async-done | bytes 3538960 | tf_op jit(solution)/shard_map/all_gather | solution.py:666
  82.3 8.5 %shard_map.186.q_ref.k_ref.v_ref = bf16[1,1024,2304]{2,1,0:T(8,128)(2,1)} custom-call(bf16[1,1024,768]{2,1,0:T(8,128)(2,1)} %get-tuple-element.92.x_ref, f32[1,768]{1,0:T(1,128)} %reshape.166.g_ref.refs_5_, f32[1,768]{1,0:T(1,128)} %reshape.167.b_ref.refs_6_, bf16[768,2304]{1,0:T(8,128)(2,1)} %all-gather.4.cloned.1.call-done.w_ref.refs_4_), custom_call_target="tpu_custom_call" | custom-call | flops 3623878656 | bytes 6291456 | tf_op jit(solution)/shard_map/pallas_call | solution.py:62
  90.8 12.0 %shard_map.187 = (bf16[1,1024,768]{2,1,0:T(8,128)(2,1)S(1)}, f32[1,6,2,1024]{3,2,1,0:T(2,128)S(1)}) custom-call(bf16[1,1024,2304]{2,1,0:T(8,128)(2,1)} %shard_map.186.q_ref.k_ref.v_ref, bf16[1,1024,2304]{2,1,0:T(8,128)(2,1)} %shard_map.186.q_ref.k_ref.v_ref, bf16[1,1024,2304]{2,1,0:T(8,128)(2,1)} %shard_map.186.q_ref.k_ref.v_ref), custom_call_target="tpu_custom_call" | custom-call | flops 6442450944 | bytes 6291456 | tf_op jit(solution)/shard_map/pallas_call | solution.py:128
  103.9 9.1 %all-gather.6.cloned.1.call-done.w_ref = bf16[768,768]{1,0:T(8,128)(2,1)} async-done(((bf16[192,768]{1,0:T(8,128)(2,1)}), bf16[768,768]{1,0:T(8,128)(2,1)}) %all-gather.6.cloned.1.call-update) | async-done | bytes 1179664 | tf_op jit(solution)/shard_map/all_gather | solution.py:667
  135.6 12.1 %shard_map.193 = (bf16[1,1024,768]{2,1,0:T(8,128)(2,1)S(1)}, f32[1,6,2,1024]{3,2,1,0:T(2,128)S(1)}) custom-call(bf16[1,1024,2304]{2,1,0:T(8,128)(2,1)} %shard_map.192.q_ref.k_ref.v_ref, bf16[1,1024,2304]{2,1,0:T(8,128)(2,1)} %shard_map.192.q_ref.k_ref.v_ref, bf16[1,1024,2304]{2,1,0:T(8,128)(2,1)} %shard_map.192.q_ref.k_ref.v_ref), custom_call_target="tpu_custom_call" | custom-call | flops 6442450944 | bytes 6291456 | tf_op jit(solution)/shard_map/pallas_call | solution.py:128
  160.5 35.7 %shard_map.190 = (bf16[3,1280,1024]{2,1,0:T(8,128)(2,1)}, bf16[3,1280,1024]{2,1,0:T(8,128)(2,1)}, bf16[1280,768]{1,0:T(8,128)(2,1)}, bf16[1280,768]{1,0:T(8,128)(2,1)}) custom-call(bf16[1280,768]{1,0:T(8,128)(2,1)} %bitcast.4.refs_0_, bf16[1280,768]{1,0:T(8,128)(2,1)} %bitcast.7.refs_1_, bf16[768,3072]{1,0:T(8,128)(2,1)} %bitcast.90, ...), custom_call_target="tpu_custom_call" | custom-call | flops 24159191040 | bytes 31457280 | tf_op jit(solution)/shard_map/pallas_call | solution.py:398
  200.6 36.5 %shard_map.197 = (bf16[2,1280,1024]{2,1,0:T(8,128)(2,1)}, bf16[2,1280,1024]{2,1,0:T(8,128)(2,1)}, bf16[4,2,256,768]{3,2,1,0:T(8,128)(2,1)}, bf16[4,2,768,256]{3,2,1,0:T(8,128)(2,1)}) custom-call(bf16[1280,768]{1,0:T(8,128)(2,1)} %bitcast.4.refs_0_, bf16[1280,768]{1,0:T(8,128)(2,1)} %bitcast.7.refs_1_, bf16[3,1280,1024]{2,1,0:T(8,128)(2,1)} %get-tuple-element.56.refs_2_, ...), custom_call_target="tpu_custom_call" | custom-call | flops 24159191040 | bytes 31457280 | tf_op jit(solution)/shard_map/pallas_call | solution.py:431
  237.1 20.6 %shard_map.196 = (bf16[1,1280,1024]{2,1,0:T(8,128)(2,1)}, bf16[1,1280,1024]{2,1,0:T(8,128)(2,1)}, bf16[4,1,256,768]{3,2,1,0:T(8,128)(2,1)}, bf16[4,1,768,256]{3,2,1,0:T(8,128)(2,1)}) custom-call(bf16[1280,768]{1,0:T(8,128)(2,1)} %bitcast.4.refs_0_, bf16[1280,768]{1,0:T(8,128)(2,1)} %bitcast.7.refs_1_, bf16[3,1280,1024]{2,1,0:T(8,128)(2,1)} %get-tuple-element.56.refs_2_, ...), custom_call_target="tpu_custom_call" | custom-call | flops 12079595520 | bytes 31457280 | tf_op jit(solution)/shard_map/pallas_call | solution.py:431
  257.7 12.5 %shard_map.203 = bf16[1280,768]{1,0:T(8,128)(2,1)} custom-call(bf16[1,1280,1024]{2,1,0:T(8,128)(2,1)} %get-tuple-element.69.refs_0_, bf16[2,1280,1024]{2,1,0:T(8,128)(2,1)} %get-tuple-element.70.refs_1_, bf16[768,3072]{1,0:T(8,128)(2,1)} %bitcast.102, bf16[768,3072]{1,0:T(8,128)(2,1)} %bitcast.103, bf16[768,3072]{1,0:T(8,128)(2,1)} %bitcast.104, ...), custom_call_target="tpu_custom_call" | custom-call | flops 6039797760 | bytes 14680064 | tf_op jit(solution)/shard_map/pallas_call | solution.py:487
  278.0 13.0 %shard_map.200 = (f32[1024,768]{1,0:T(8,128)}, bf16[1024,768]{1,0:T(8,128)(2,1)}, f32[768,768]{1,0:T(8,128)}, f32[2,768]{1,0:T(2,128)}) custom-call(bf16[1280,768]{1,0:T(8,128)(2,1)} %bitcast.26.back_ref, s32[1024,1]{1,0:T(8,128)} %copy.25.slot_ref, f32[1024,768]{1,0:T(8,128)} %copy-done.1, bf16[1024,768]{1,0:T(8,128)(2,1)} %copy-done.10, ...), custom_call_target="tpu_custom_call" | custom-call | flops 4429185024 | bytes 15728640 | tf_op jit(solution)/shard_map/pallas_call | solution.py:530
  291.1 8.5 %all-to-all-done.7 = bf16[8,160,768]{2,1,0:T(8,128)(2,1)S(1)} async-done(((bf16[8,160,768]{2,1,0:T(8,128)(2,1)}), bf16[8,160,768]{2,1,0:T(8,128)(2,1)S(1)}, u32[]{:S(2)}, u32[]{:S(2)}) %all-to-all-start.7) | async-done | bytes 1966112 | tf_op jit(solution)/shard_map/all_to_all | solution.py:629
  300.9 13.5 %shard_map.204 = (f32[1024,768]{1,0:T(8,128)}, bf16[1024,768]{1,0:T(8,128)(2,1)}, f32[768,768]{1,0:T(8,128)}, f32[2,768]{1,0:T(2,128)}) custom-call(bf16[1280,768]{1,0:T(8,128)(2,1)} %bitcast.130, s32[1024,1]{1,0:T(8,128)} %copy.26.slot_ref, f32[1024,768]{1,0:T(8,128)} %copy-done.3, bf16[1024,768]{1,0:T(8,128)(2,1)} %copy-done.9, ...), custom_call_target="tpu_custom_call" | custom-call | flops 4429185024 | bytes 15728640 | tf_op jit(solution)/shard_map/pallas_call | solution.py:530
  316.1 24.0 %shard_map.201 = (bf16[1,1024,768]{2,1,0:T(8,128)(2,1)S(1)}, bf16[1,1024,768]{2,1,0:T(8,128)(2,1)S(1)}, bf16[1,1024,768]{2,1,0:T(8,128)(2,1)S(1)}) custom-call(bf16[1,1024,2304]{2,1,0:T(8,128)(2,1)} %shard_map.186.q_ref.k_ref.v_ref, bf16[1,1024,2304]{2,1,0:T(8,128)(2,1)} %shard_map.186.q_ref.k_ref.v_ref, ...), custom_call_target="tpu_custom_call" | custom-call | flops 16106127360 | bytes 12582912 | tf_op jit(solution)/shard_map/pallas_call | solution.py:219
  343.7 24.1 %shard_map.205 = (bf16[1,1024,768]{2,1,0:T(8,128)(2,1)S(1)}, bf16[1,1024,768]{2,1,0:T(8,128)(2,1)S(1)}, bf16[1,1024,768]{2,1,0:T(8,128)(2,1)S(1)}) custom-call(bf16[1,1024,2304]{2,1,0:T(8,128)(2,1)} %shard_map.192.q_ref.k_ref.v_ref, bf16[1,1024,2304]{2,1,0:T(8,128)(2,1)} %shard_map.192.q_ref.k_ref.v_ref, ...), custom_call_target="tpu_custom_call" | custom-call | flops 16106127360 | bytes 12582912 | tf_op jit(solution)/shard_map/pallas_call | solution.py:219
  371.2 15.9 %shard_map.202 = (f32[1024,768]{1,0:T(8,128)}, f32[768,2304]{1,0:T(8,128)}, f32[2,768]{1,0:T(2,128)}) custom-call(bf16[1024,768]{1,0:T(8,128)(2,1)} %bitcast.87, bf16[1024,768]{1,0:T(8,128)(2,1)} %bitcast.88, bf16[1024,768]{1,0:T(8,128)(2,1)} %bitcast.89, bf16[1024,768]{1,0:T(8,128)(2,1)} %copy-done.8, ...), custom_call_target="tpu_custom_call" | custom-call | flops 7247757312 | bytes 23592960 | tf_op jit(solution)/shard_map/pallas_call | solution.py:593
  387.1 17.2 %shard_map.206 = (f32[1024,768]{1,0:T(8,128)}, bf16[768,2304]{1,0:T(8,128)(2,1)}, f32[2,768]{1,0:T(2,128)}) custom-call(bf16[1024,768]{1,0:T(8,128)(2,1)} %bitcast.84, bf16[1024,768]{1,0:T(8,128)(2,1)} %bitcast.85, bf16[1024,768]{1,0:T(8,128)(2,1)} %bitcast.86, bf16[1024,768]{1,0:T(8,128)(2,1)} %copy-done.7, ...), custom_call_target="tpu_custom_call" | custom-call | flops 7247757312 | bytes 23592960 | tf_op jit(solution)/shard_map/pallas_call | solution.py:593
  410.3 83.1 %all-reduce.3.cloned.1.call-done = bf16[8,4,24,3072]{3,2,0,1:T(8,128)(2,1)} async-done(((bf16[8,4,24,3072]{3,2,0,1:T(8,128)(2,1)}), bf16[8,4,24,3072]{3,2,0,1:T(8,128)(2,1)}) %all-reduce.3.cloned.1.call-update) | async-done | bytes 4718608
  498.7 12.5 %shard_map.198 = bf16[1280,768]{1,0:T(8,128)(2,1)} custom-call(bf16[1,1280,1024]{2,1,0:T(8,128)(2,1)} %get-tuple-element.59.refs_0_, bf16[2,1280,1024]{2,1,0:T(8,128)(2,1)} %get-tuple-element.60.refs_1_, bf16[3072,768]{1,0:T(8,128)(2,1)} %bitcast.118, bf16[3072,768]{1,0:T(8,128)(2,1)} %bitcast.119, bf16[3072,768]{1,0:T(8,128)(2,1)} %bitcast.120, ...), custom_call_target="tpu_custom_call" | custom-call | flops 6039797760 | bytes 14680064 | tf_op jit(solution)/shard_map/pallas_call | solution.py:487
  511.2 29.5 %all_to_all.40 = bf16[8,160,768]{2,1,0:T(8,128)(2,1)} all-to-all(bf16[8,160,768]{2,1,0:T(8,128)(2,1)} %bitcast.124), channel_id=1, replica_groups=mesh['dp'=4,'expert'=8] {'expert'}, dimensions={0} | all-to-all | bytes 3932160 | tf_op jit(solution)/shard_map/all_to_all | solution.py:629
  546.0 62.7 %psum.7 = f32[4,768]{1,0:T(4,128)S(1)} all-reduce(f32[4,768]{1,0:T(4,128)S(1)} %maximum_add_fusion), channel_id=1, replica_groups=mesh['dp'=4,'expert'=8] {'expert','dp'}, use_global_device_ids=true, to_apply=%region_1.0 | all-reduce | flops 3072 | bytes 24576 | tf_op jit(solution)/shard_map/psum | solution.py:729
  629.7 49.8 %reduce-scatter.11.cloned.1.call-done = bf16[1,2,768,256]{3,2,1,0:T(8,128)(2,1)} async-done(((bf16[4,2,768,256]{3,2,1,0:T(8,128)(2,1)}), bf16[1,2,768,256]{3,2,1,0:T(8,128)(2,1)}) %reduce-scatter.11.cloned.1.call-update) | async-done | bytes 786448 | tf_op jit(solution)/shard_map/reduce_scatter | solution.py:696
  680.7 36.6 %reduce-scatter.9.cloned.1.call-done = bf16[1,1,768,256]{3,2,1,0:T(8,128)(2,1)} async-done(((bf16[4,1,768,256]{3,2,1,0:T(8,128)(2,1)}), bf16[1,1,768,256]{3,2,1,0:T(8,128)(2,1)}) %reduce-scatter.9.cloned.1.call-update) | async-done | bytes 393232 | tf_op jit(solution)/shard_map/reduce_scatter | solution.py:696
  721.4 21.0 %all-gather.8.cloned.1.call-done = bf16[8,24,3072]{2,1,0:T(8,128)(2,1)} async-done(((bf16[1,24,3072]{2,1,0:T(8,128)(2,1)}), bf16[8,24,3072]{2,1,0:T(8,128)(2,1)}) %all-gather.8.cloned.1.call-update) | async-done | bytes 1179664 | tf_op jit(solution)/shard_map/all_gather | solution.py:727
  (138 shorter events, 132.4 us)
Async XLA Ops:
  7.2 75.1 %all-gather.4.cloned.1.call-start = ((), (), s32[]{:S(2)}) async-start(), calls=%async_computation.13 | async-start | bytes 4423680 | tf_op jit(solution)/shard_map/all_gather | solution.py:666
  15.4 30.5 %all-to-all-start.1 = ((bf16[8,160,768]{2,1,0:T(8,128)(2,1)}), bf16[8,160,768]{2,1,0:T(8,128)(2,1)}, u32[]{:S(2)}, u32[]{:S(2)}) async-start(bf16[8,160,768]{2,1,0:T(8,128)(2,1)} %bitcast.6), calls=%async_computation.1 | async-start | bytes 3932160 | tf_op jit(solution)/shard_map/all_to_all | solution.py:629
  20.5 92.4 %all-gather.6.cloned.1.call-start = ((), (), s32[]{:S(2)}) async-start(), calls=%async_computation.14 | async-start | bytes 1474560 | tf_op jit(solution)/shard_map/all_gather | solution.py:667
  24.8 25.6 %copy-start.31 = (f32[768]{0:T(1024)S(1)}, f32[768]{0:T(1024)}, u32[]{:S(2)}) copy-start(f32[768]{0:T(1024)} %param.13) | copy-start | bytes 9220
  24.8 26.2 %copy-start.32 = (f32[768]{0:T(1024)S(1)}, f32[768]{0:T(1024)}, u32[]{:S(2)}) copy-start(f32[768]{0:T(1024)} %param.14) | copy-start | bytes 9220
  24.8 26.8 %copy-start.33 = (f32[768]{0:T(1024)S(1)}, f32[768]{0:T(1024)}, u32[]{:S(2)}) copy-start(f32[768]{0:T(1024)} %param.17) | copy-start | bytes 9220
  24.8 26.8 %copy-start.34 = (f32[768]{0:T(1024)S(1)}, f32[768]{0:T(1024)}, u32[]{:S(2)}) copy-start(f32[768]{0:T(1024)} %param.18) | copy-start | bytes 9220
  45.9 76.7 %all-to-all-start.4 = ((bf16[8,160,768]{2,1,0:T(8,128)(2,1)}), bf16[8,160,768]{2,1,0:T(8,128)(2,1)}, u32[]{:S(2)}, u32[]{:S(2)}) async-start(bf16[8,160,768]{2,1,0:T(8,128)(2,1)} %bitcast.19), calls=%async_computation.4 | async-start | bytes 3932160 | tf_op jit(solution)/shard_map/all_to_all | solution.py:629
  51.6 96.1 %copy-start.11 = (f32[1,768]{1,0:T(1,128)}, f32[1,768]{1,0:T(1,128)S(1)}, u32[]{:S(2)}) copy-start(f32[1,768]{1,0:T(1,128)S(1)} %reshape.168.g_ref) | copy-start | bytes 9220
  55.5 57.4 %copy-start.8 = (bf16[1024,768]{1,0:T(8,128)(2,1)}, bf16[1024,768]{1,0:T(8,128)(2,1)S(1)}, u32[]{:S(2)}) copy-start(bf16[1024,768]{1,0:T(8,128)(2,1)S(1)} %get-tuple-element.93.x_ref.refs_3_) | copy-start | bytes 4718596
  55.5 92.1 %copy-start.7 = (bf16[1024,768]{1,0:T(8,128)(2,1)}, bf16[1024,768]{1,0:T(8,128)(2,1)S(1)}, u32[]{:S(2)}) copy-start(bf16[1024,768]{1,0:T(8,128)(2,1)S(1)} %get-tuple-element.94.x_ref) | copy-start | bytes 4718596
  122.6 33.2 %all-to-all-start = ((bf16[8,160,768]{2,1,0:T(8,128)(2,1)}), bf16[8,160,768]{2,1,0:T(8,128)(2,1)}, u32[]{:S(2)}, u32[]{:S(2)}) async-start(bf16[8,160,768]{2,1,0:T(8,128)(2,1)} %bitcast.3), calls=%async_computation | async-start | bytes 3932160 | tf_op jit(solution)/shard_map/all_to_all | solution.py:629
  135.6 12.1 %copy-start.13 = (bf16[768,768]{1,0:T(8,128)(2,1)S(1)}, bf16[768,768]{1,0:T(8,128)(2,1)}, u32[]{:S(2)}) copy-start(bf16[768,768]{1,0:T(8,128)(2,1)} %all-gather.6.cloned.1.call-done.w_ref) | copy-start | bytes 3538948
  155.9 40.3 %all-to-all-start.3 = ((bf16[8,160,768]{2,1,0:T(8,128)(2,1)}), bf16[8,160,768]{2,1,0:T(8,128)(2,1)S(1)}, u32[]{:S(2)}, u32[]{:S(2)}) async-start(bf16[8,160,768]{2,1,0:T(8,128)(2,1)} %bitcast.16), calls=%async_computation.3 | async-start | bytes 3932160 | tf_op jit(solution)/shard_map/all_to_all | solution.py:629
  196.2 74.0 %all-to-all-start.6 = ((bf16[8,160,768]{2,1,0:T(8,128)(2,1)}), bf16[8,160,768]{2,1,0:T(8,128)(2,1)}, u32[]{:S(2)}, u32[]{:S(2)}) async-start(bf16[8,160,768]{2,1,0:T(8,128)(2,1)} %bitcast.131), calls=%async_computation.6 | async-start | bytes 3932160 | tf_op jit(solution)/shard_map/all_to_all | solution.py:629
  270.2 29.4 %all-to-all-start.7 = ((bf16[8,160,768]{2,1,0:T(8,128)(2,1)}), bf16[8,160,768]{2,1,0:T(8,128)(2,1)S(1)}, u32[]{:S(2)}, u32[]{:S(2)}) async-start(bf16[8,160,768]{2,1,0:T(8,128)(2,1)} %bitcast.123), calls=%async_computation.7 | async-start | bytes 3932160 | tf_op jit(solution)/shard_map/all_to_all | solution.py:629
  274.3 219.1 %all-reduce.3.cloned.1.call-start = ((), (), s32[]{:S(2)}) async-start(), calls=%async_computation.21 | async-start | bytes 9437184
  409.1 136.2 %reduce-scatter.7.cloned.1.call-start = ((), (), s32[]{:S(2)}) async-start(), calls=%async_computation.15 | async-start | bytes 737280 | tf_op jit(solution)/shard_map/reduce_scatter | solution.py:726
  496.0 132.4 %reduce-scatter.13.cloned.1.call-start = ((), (), s32[]{:S(2)}) async-start(), calls=%async_computation.19 | async-start | bytes 1966080 | tf_op jit(solution)/shard_map/reduce_scatter | solution.py:695
  496.6 131.8 %reduce-scatter.15.cloned.1.call-start = ((), (), s32[]{:S(2)}) async-start(), calls=%async_computation.20 | async-start | bytes 3932160 | tf_op jit(solution)/shard_map/reduce_scatter | solution.py:695
  497.2 182.4 %reduce-scatter.11.cloned.1.call-start = ((), (), s32[]{:S(2)}) async-start(), calls=%async_computation.18 | async-start | bytes 3932160 | tf_op jit(solution)/shard_map/reduce_scatter | solution.py:696
  497.9 219.4 %reduce-scatter.9.cloned.1.call-start = ((), (), s32[]{:S(2)}) async-start(), calls=%async_computation.17 | async-start | bytes 1966080 | tf_op jit(solution)/shard_map/reduce_scatter | solution.py:696
  540.7 75.4 %all-to-all-start.2 = ((bf16[8,160,768]{2,1,0:T(8,128)(2,1)}), bf16[8,160,768]{2,1,0:T(8,128)(2,1)}, u32[]{:S(2)}, u32[]{:S(2)}) async-start(bf16[8,160,768]{2,1,0:T(8,128)(2,1)} %bitcast.10), calls=%async_computation.2 | async-start | bytes 3932160 | tf_op jit(solution)/shard_map/all_to_all | solution.py:629
  545.2 197.2 %all-gather.8.cloned.1.call-start = ((), (), s32[]{:S(2)}) async-start(), calls=%async_computation.16 | async-start | bytes 1327104 | tf_op jit(solution)/shard_map/all_gather | solution.py:727
  (28 other events, 70.9 us)
Sparse Core Ops, SparseCore 0:
  9.6 72.6 all-gather.3
  83.9 29.0 all-gather.5
  409.2 84.1 all-reduce.2
  496.2 21.9 reduce-scatter.6
  520.5 33.7 reduce-scatter.12
  556.5 60.2 reduce-scatter.14
  619.3 60.2 reduce-scatter.10
  681.9 35.2 reduce-scatter.8
  719.3 23.0 all-gather.7

commit v2 on v1

--- a/solution.py
+++ b/solution.py
@@ -38,6 +38,17 @@
 
 
 VM = pl.BlockSpec(memory_space=pltpu.VMEM)
+ANY = pl.BlockSpec(memory_space=pl.ANY)
+
+
+def kernel_call(body, in_specs, args, deps=(), **options):
+    count = len(args)
+    extra = len(deps)
+
+    def wrapped(*refs):
+        body(*refs[:count], *refs[count + extra :])
+
+    return pl.pallas_call(wrapped, in_specs=list(in_specs) + [ANY] * extra, **options)(*args, *deps)
 
 
 def norm_parts(v):
@@ -48,31 +59,207 @@
     return shifted * r, r
 
 
-def qkv_body(x_ref, g_ref, b_ref, w_ref, o_ref):
-    hat, _ = norm_parts(x_ref[0].astype(f32))
-    low = (hat * g_ref[...] + b_ref[...]).astype(bf16)
-    o_ref[0] = dot(low, w_ref[...]).astype(bf16)
-
-
-def qkv_call(x, gain, bias, w):
-    n, length, width = x.shape
-    triple = w.shape[1]
-    rows = min(512, length)
-    row = pl.BlockSpec((1, width), lambda s, r: (0, 0))
+MESH = pl.DeviceIdType.MESH
+
+
+def greet(peers):
+    barrier = pltpu.get_barrier_semaphore()
+    for peer in peers:
+        pl.semaphore_signal(barrier, inc=1, device_id=peer, device_id_type=MESH)
+    return barrier
+
+
+def qkv_body(
+    x_ref, g_ref, b_ref, wq_ref, wo_ref, qkv_ref, fq_ref, fo_ref, low, acc, up_s, dn_s, core_s, z_r, core_r, loc
+):
+    nz = lax.axis_size("dp")
+    z = lax.axis_index("dp")
+    e = lax.axis_index("expert")
+    core = e % 2
+    seqs, length, width = x_ref.shape
+    per = width // nz
+    half = per // 2
+    above = (jnp.minimum(z + 1, nz - 1), e)
+    below = (jnp.maximum(z - 1, 0), e)
+    mate = (z, e + 1 - 2 * core)
+    full = (fq_ref, fo_ref)
+
+    barrier = pltpu.get_barrier_semaphore()
+
+    @pl.when(z + 1 < nz)
+    def _():
+        pl.semaphore_signal(barrier, inc=1, device_id=above, device_id_type=MESH)
+
+    @pl.when(z > 0)
+    def _():
+        pl.semaphore_signal(barrier, inc=1, device_id=below, device_id_type=MESH)
+
+    pl.semaphore_signal(barrier, inc=1, device_id=mate, device_id_type=MESH)
+
+    @pl.when((z + 1 < nz) & (z > 0))
+    def _():
+        pl.semaphore_wait(barrier, 3)
+
+    @pl.when((z + 1 >= nz) | (z <= 0))
+    def _():
+        pl.semaphore_wait(barrier, 2)
+
+    def rows_of(ref, p, c):
+        return ref.at[pl.ds(pl.multiple_of(p * per + c * half, 16), half)]
+
+    def hop(t, p, c, src, sem, r_sem, peer):
+        return pltpu.make_async_remote_copy(
+            src_ref=src,
+            dst_ref=rows_of(full[t], p, c),
+            send_sem=sem.at[t, p],
+            recv_sem=r_sem.at[t, p],
+            device_id=peer,
+            device_id_type=MESH,
+        )
+
+    shard = (wq_ref, wo_ref)
+    for t in range(2):
+        mine = shard[t].at[pl.ds(pl.multiple_of(core * half, 16), half)]
+
+        @pl.when(z + 1 < nz)
+        def _(t=t, mine=mine):
+            hop(t, z, core, mine, up_s, z_r, above).start()
+
+        @pl.when(z > 0)
+        def _(t=t, mine=mine):
+            hop(t, z, core, mine, dn_s, z_r, below).start()
+
+    own = [
+        pltpu.make_async_copy(
+            shard[t], full[t].at[pl.ds(pl.multiple_of(z * per, 16), per)], loc.at[t]
+        )
+        for t in range(2)
+    ]
+    for c in own:
+        c.start()
+
+    blk = min(BLK, length)
+    for s in range(seqs):
+        for a in range(0, length, blk):
+            hat, _ = norm_parts(x_ref[s, a : a + blk].astype(f32))
+            v = (hat * g_ref[...] + b_ref[...]).astype(bf16)
+            for p in range(nz):
+                low[p, s * length + a : s * length + a + blk] = v[:, p * per : (p + 1) * per]
+    total = seqs * length
+    step = min(512, length)
+
+    def product(p, first):
+        w = fq_ref[pl.ds(pl.multiple_of(p * per, 16), per)]
+        for a in range(0, total, step):
+            term = dot(low[p, a : a + step], w)
+            if first:
+                acc[a : a + step] = term
+            else:
+                acc[a : a + step] += term
+
+    def arrive(t, p, forward, sem, peer):
+        hop(t, p, core, rows_of(full[t], p, core), sem, z_r, peer).wait_recv()
+        hop(t, p, core, rows_of(full[t], p, core), core_s, core_r, mate).start()
+
+        @pl.when(forward)
+        def _():
+            hop(t, p, core, rows_of(full[t], p, core), sem, z_r, peer).start()
+
+    def got(t, p):
+        hop(t, p, 1 - core, rows_of(full[t], p, 1 - core), core_s, core_r, mate).wait_recv()
+
+    own[0].wait()
+    own[1].wait()
+    product(z, True)
+    for d in range(1, nz):
+
+        @pl.when(z - d >= 0)
+        def _(d=d):
+            arrive(0, z - d, z + 1 < nz, up_s, above)
+
+        @pl.when(z + d < nz)
+        def _(d=d):
+            arrive(0, z + d, z > 0, dn_s, below)
+
+        @pl.when(z - d >= 0)
+        def _(d=d):
+            got(0, z - d)
+            product(z - d, False)
+
+        @pl.when(z + d < nz)
+        def _(d=d):
+            got(0, z + d)
+            product(z + d, False)
+
+    for a in range(0, total, step):
+        qkv_ref[a // length, a % length : a % length + step] = acc[a : a + step].astype(bf16)
+    for d in range(1, nz):
+
+        @pl.when(z - d >= 0)
+        def _(d=d):
+            arrive(1, z - d, z + 1 < nz, up_s, above)
+
+        @pl.when(z + d < nz)
+        def _(d=d):
+            arrive(1, z + d, z > 0, dn_s, below)
+
+    for d in range(1, nz):
+        for ok, p in ((z - d >= 0, z - d), (z + d < nz, z + d)):
+
+            @pl.when(ok)
+            def _(p=p):
+                got(1, p)
+
+    for t in range(2):
+        mine = shard[t].at[pl.ds(pl.multiple_of(core * half, 16), half)]
+
+        @pl.when(z + 1 < nz)
+        def _(t=t, mine=mine):
+            hop(t, z, core, mine, up_s, z_r, above).wait_send()
+
+        @pl.when(z > 0)
+        def _(t=t, mine=mine):
+            hop(t, z, core, mine, dn_s, z_r, below).wait_send()
+
+        for d in range(1, nz):
+            for ok, p, more, sem, peer in (
+                (z - d >= 0, z - d, z + 1 < nz, up_s, above),
+                (z + d < nz, z + d, z > 0, dn_s, below),
+            ):
+
+                @pl.when(ok)
+                def _(t=t, p=p):
+                    hop(t, p, core, rows_of(full[t], p, core), core_s, core_r, mate).wait_send()
+
+                @pl.when(ok & more)
+                def _(t=t, p=p, sem=sem, peer=peer):
+                    hop(t, p, core, rows_of(full[t], p, core), sem, z_r, peer).wait_send()
+
+
+def qkv_call(x, gain, bias, wq, wo, nz):
+    seqs, length, width = x.shape
+    triple = wq.shape[1]
+    dma = pltpu.SemaphoreType.DMA
     return pl.pallas_call(
         qkv_body,
-        grid=(n, length // rows),
-        in_specs=[
-            pl.BlockSpec((1, rows, width), lambda s, r: (s, r, 0)),
-            row,
-            row,
-            pl.BlockSpec((width, triple), lambda s, r: (0, 0)),
+        in_specs=[VM] * 5,
+        out_specs=[VM] * 3,
+        out_shape=[
+            sds((seqs, length, triple), bf16),
+            sds((width, triple), bf16),
+            sds((width, width), bf16),
         ],
-        out_specs=pl.BlockSpec((1, rows, triple), lambda s, r: (s, r, 0)),
-        out_shape=sds((n, length, triple), bf16),
-        compiler_params=params(),
-        cost_estimate=cost(2 * n * length * width * triple, n * length * (width + triple) * 2),
-    )(x, gain.reshape(1, -1), bias.reshape(1, -1), w)
+        scratch_shapes=[
+            pltpu.VMEM((nz, seqs * length, width // nz), bf16),
+            pltpu.VMEM((seqs * length, triple), f32),
+        ]
+        + [dma((2, nz))] * 5
+        + [dma((2,))],
+        compiler_params=pltpu.CompilerParams(
+            vmem_limit_bytes=58 << 20, collective_id=0, has_side_effects=True
+        ),
+        cost_estimate=cost(2 * seqs * length * width * triple * 4, 30 << 20),
+    )(x, gain.reshape(1, -1), bias.reshape(1, -1), wq, wo)
 
 
 def attn_fwd_body(q_ref, k_ref, v_ref, o_ref, lse_ref, *, blk, hs, scale, depth):
@@ -114,26 +301,28 @@
             o_ref[0, i * blk : top, :] = both.T.astype(bf16)
 
 
-def attn_fwd_call(qkv, heads):
-    n, length, triple = qkv.shape
+def attn_fwd_call(qkv, heads, at, deps=()):
+    n, length, triple = 1, *qkv.shape[1:]
     width = triple // 3
     hs = width // heads
     pairs = heads // 2
     blk = min(BLK, length)
 
-    def spec(o):
-        return pl.BlockSpec((1, length, 2 * hs), lambda s, p, o=o: (s, 0, o * pairs + p))
+    def spec(o, at=0):
+        return pl.BlockSpec((1, length, 2 * hs), lambda s, p: (s + at, 0, o * pairs + p))
 
     half = n * heads * length * length // 2
-    return pl.pallas_call(
+    return kernel_call(
         functools.partial(attn_fwd_body, blk=blk, hs=hs, scale=hs**-0.5, depth=3),
+        args=[qkv, qkv, qkv],
+        deps=deps,
         grid=(n, pairs),
-        in_specs=[spec(0), spec(1), spec(2)],
+        in_specs=[spec(0, at), spec(1, at), spec(2, at)],
         out_specs=[spec(0), pl.BlockSpec((1, 1, 2, length), lambda s, p: (s, p, 0, 0))],
         out_shape=[sds((n, length, width), bf16), sds((n, pairs, 2, length), f32)],
         compiler_params=params(48),
         cost_estimate=cost(half * 2 * 2 * 256, n * length * width * 8, half),
-    )(qkv, qkv, qkv)
+    )
 
 
 def attn_bwd_body(
@@ -205,21 +394,23 @@
             dq_ref[0, a : a + blk, :] = dqa[:, a : a + blk].T.astype(bf16)
 
 
-def attn_bwd_call(qkv, o, do, lse, heads):
-    n, length, triple = qkv.shape
+def attn_bwd_call(qkv, o, do, lse, heads, at, deps=()):
+    n, length, triple = 1, *qkv.shape[1:]
     width = triple // 3
     hs = width // heads
     pairs = heads // 2
     blk = min(BLK, length)
 
-    def spec(o):
-        return pl.BlockSpec((1, length, 2 * hs), lambda s, p, o=o: (s, 0, o * pairs + p))
+    def spec(o, at=0):
+        return pl.BlockSpec((1, length, 2 * hs), lambda s, p: (s + at, 0, o * pairs + p))
 
     half = n * heads * length * length // 2
-    return pl.pallas_call(
+    return kernel_call(
         functools.partial(attn_bwd_body, blk=blk, hs=hs, scale=hs**-0.5, depth=2),
+        args=[qkv, qkv, qkv, o, do, lse],
+        deps=deps,
         grid=(n, pairs),
-        in_specs=[spec(0), spec(1), spec(2), spec(0), spec(0)]
+        in_specs=[spec(0, at), spec(1, at), spec(2, at), spec(0), spec(0)]
         + [pl.BlockSpec((1, 1, 2, length), lambda s, p: (s, p, 0, 0))],
         out_specs=[spec(0)] * 3,
         out_shape=[sds((n, length, width), bf16)] * 3,
@@ -229,7 +420,7 @@
         ],
         compiler_params=params(48),
         cost_estimate=cost(half * 5 * 2 * 256, n * length * width * 16, half),
-    )(qkv, qkv, qkv, o, do, lse)
+    )
 
 
 def slot_chunk(total):
@@ -256,16 +447,18 @@
     place_rows(rows_ref[...], slot_ref[...], out_ref)
 
 
-def send_call(rows, slot_row, total):
+def send_call(rows, slot_row, total, deps=()):
     length, width = rows.shape
-    return pl.pallas_call(
+    return kernel_call(
         send_body,
+        args=[rows, slot_row],
+        deps=deps,
         in_specs=[VM, VM],
         out_specs=VM,
         out_shape=sds((total, width), bf16),
         compiler_params=params(32),
         cost_estimate=cost(2 * length * total * width, (length + total) * width * 2),
-    )(rows, slot_row)
+    )
 
 
 def out_body(x_ref, mixed_ref, w_ref, g_ref, b_ref, slot_ref, after_ref, sent_ref, toks):
@@ -280,17 +473,19 @@
     place_rows(toks[...], slot_ref[...], sent_ref)
 
 
-def out_call(x, mixed, w, gain, bias, slot_row, total):
+def out_call(x, mixed, w, gain, bias, slot_row, total, deps=()):
     length, width = x.shape
-    return pl.pallas_call(
+    return kernel_call(
         out_body,
+        args=[x, mixed, w, gain.reshape(1, -1), bias.reshape(1, -1), slot_row],
+        deps=deps,
         in_specs=[VM] * 6,
         out_specs=[VM] * 2,
         out_shape=[sds((length, width), f32), sds((total, width), bf16)],
         scratch_shapes=[pltpu.VMEM((length, width), bf16)],
         compiler_params=params(40),
         cost_estimate=cost(2 * length * width * (width + total), length * width * 12),
-    )(x, mixed, w, gain.reshape(1, -1), bias.reshape(1, -1), slot_row)
+    )
 
 
 def add_back_body(after_ref, back_ref, slot_ref, out_ref):
@@ -301,17 +496,19 @@
         out_ref[rows] = after_ref[rows] + take_rows(back_ref[...], slot_ref[rows])
 
 
-def add_back_call(after, back, slot_col):
+def add_back_call(after, back, slot_col, deps=()):
     length, width = after.shape
     total = back.shape[0]
-    return pl.pallas_call(
+    return kernel_call(
         add_back_body,
+        args=[after, back, slot_col],
+        deps=deps,
         in_specs=[VM] * 3,
         out_specs=VM,
         out_shape=sds((length, width), f32),
         compiler_params=params(40),
         cost_estimate=cost(2 * length * width * total, length * width * 12),
-    )(after, back, slot_col)
+    )
 
 
 def gelu_parts(pre):
@@ -388,15 +585,17 @@
     return ins + downs
 
 
-def expert_a_call(rows, cot, w_in, w_down, nz):
+def expert_a_call(rows, cot, w_in, w_down, nz, deps=()):
     total, width = rows.shape
     hidden = w_in.shape[1]
     chunks = hidden // (nz * FFT)
     tile = nz * FFT
     keep = pl.BlockSpec((total, width), lambda c: (0, 0))
     mid = pl.BlockSpec((1, total, tile), lambda c: (c, 0, 0))
-    return pl.pallas_call(
+    return kernel_call(
         functools.partial(expert_a_body, nz=nz),
+        args=[rows, cot, *([w_in] * nz), *([w_down] * nz)],
+        deps=deps,
         grid=(chunks,),
         in_specs=[keep, keep] + weight_specs(width, hidden, nz),
         out_specs=[mid, mid, keep, keep],
@@ -404,7 +603,7 @@
         scratch_shapes=[pltpu.VMEM((total, width), f32)] * 2,
         compiler_params=params(60),
         cost_estimate=cost(8 * total * width * hidden, 30 << 20),
-    )(rows, cot, *([w_in] * nz), *([w_down] * nz))
+    )
 
 
 def expert_b_body(*refs, nz):
@@ -421,15 +620,17 @@
         gin_ref[z, 0] = gin.astype(bf16)
 
 
-def expert_b_call(rows_a, cot_a, act_a, gpre_a, rows_b, cot_b, w_in, w_down, nz, first, count):
+def expert_b_call(rows_a, cot_a, act_a, gpre_a, rows_b, cot_b, w_in, w_down, nz, first, count, deps=()):
     total, width = rows_a.shape
     hidden = w_in.shape[1]
     tile = nz * FFT
     keep = pl.BlockSpec((total, width), lambda c: (0, 0))
     mid = pl.BlockSpec((1, total, tile), lambda c: (c + first, 0, 0))
     mid_out = pl.BlockSpec((1, total, tile), lambda c: (c, 0, 0))
-    return pl.pallas_call(
+    return kernel_call(
         functools.partial(expert_b_body, nz=nz),
+        args=[rows_a, cot_a, act_a, gpre_a, rows_b, cot_b, *([w_in] * nz), *([w_down] * nz)],
+        deps=deps,
         grid=(count,),
         in_specs=[keep, keep, mid, mid, keep, keep] + weight_specs(width, hidden, nz, first),
         out_specs=[
@@ -446,7 +647,7 @@
         ],
         compiler_params=params(60),
         cost_estimate=cost(12 * total * width * tile * count, 30 << 20),
-    )(rows_a, cot_a, act_a, gpre_a, rows_b, cot_b, *([w_in] * nz), *([w_down] * nz))
+    )
 
 
 def expert_c_body(*refs, nz, parts, dims):
@@ -477,15 +678,17 @@
         out_ref[...] = acc[...].astype(bf16)
 
 
-def expert_c_call(mids, w, nz, dims):
+def expert_c_call(mids, w, nz, dims, deps=()):
     total, tile = mids[0].shape[1:]
     hidden = tile * sum(m.shape[0] for m in mids)
     width = w.shape[0] if dims is NT else w.shape[1]
     chunks = hidden // tile
     specs = weight_specs(width, hidden, nz)
     specs = specs[:nz] if dims is NT else specs[nz:]
-    return pl.pallas_call(
+    return kernel_call(
         functools.partial(expert_c_body, nz=nz, parts=len(mids), dims=dims),
+        args=[*mids, *([w] * nz)],
+        deps=deps,
         grid=(chunks,),
         in_specs=[pl.BlockSpec(m.shape, lambda c: (0, 0, 0)) for m in mids] + specs,
         out_specs=pl.BlockSpec((total, width), lambda c: (0, 0)),
@@ -493,7 +696,7 @@
         scratch_shapes=[pltpu.VMEM((total, width), f32)],
         compiler_params=params(60),
         cost_estimate=cost(2 * total * width * hidden, 14 << 20),
-    )(*mids, *([w] * nz))
+    )
 
 
 def norm_two_body(
@@ -524,11 +727,13 @@
     sums_ref[1:2] = bias_sum
 
 
-def norm_two_call(back, slot_col, after, cot, mixed, w, gain, seed):
+def norm_two_call(back, slot_col, after, cot, mixed, w, gain, seed, deps=()):
     length, width = after.shape
     total = back.shape[0]
-    return pl.pallas_call(
+    return kernel_call(
         norm_two_body,
+        args=[back, slot_col, after, cot, mixed, w, gain.reshape(1, -1), seed],
+        deps=deps,
         in_specs=[VM] * 8,
         out_specs=[VM] * 4,
         out_shape=[
@@ -540,11 +745,22 @@
         scratch_shapes=[pltpu.VMEM((length, width), bf16)],
         compiler_params=params(56),
         cost_estimate=cost(2 * length * width * (total + 2 * width), length * width * 20),
-    )(back, slot_col, after, cot, mixed, w, gain.reshape(1, -1), seed)
+    )
+
+
+def pack(out_ref, value, block):
+    nz, _, lanes = out_ref.shape
+    width = value.shape[1]
+    per = value.shape[0] // nz
+    low = value.astype(bf16)
+    for c in range(width // lanes):
+        at = (block * (width // lanes) + c) * per
+        for z in range(nz):
+            out_ref[z, at : at + per] = low[z * per : (z + 1) * per, c * lanes : (c + 1) * lanes]
 
 
 def norm_one_body(
-    dq_ref, dk_ref, dv_ref, x_ref, w_ref, g_ref, b_ref, ga_ref, seed_ref, gx_ref, gw_ref, sums_ref, low
+    dq_ref, dk_ref, dv_ref, x_ref, w_ref, g_ref, b_ref, ga_ref, seed_ref, gwo_ref, gx_ref, gw_ref, sums_ref, low
 ):
     length, width = x_ref.shape
     blk = min(BLK, length)
@@ -570,58 +786,170 @@
         cols = slice(t * width, (t + 1) * width)
         term = dot(low[...], ref[...], TN)
         if seed_ref is None:
-            gw_ref[:, cols] = term.astype(gw_ref.dtype)
+            gw_ref[:, cols] = term
         else:
-            gw_ref[:, cols] = (seed_ref[:, cols] + term).astype(gw_ref.dtype)
+            pack(gw_ref, seed_ref[:, cols] + term, t)
+    if seed_ref is not None:
+        pack(gw_ref, gwo_ref[...], len(parts))
     sums_ref[0:1] = gain_sum
     sums_ref[1:2] = bias_sum
 
 
-def norm_one_call(dq, dk, dv, x, w, gain, bias, ga, seed):
+def norm_one_call(dq, dk, dv, x, w, gain, bias, ga, seed, gwo, nz, deps=()):
     length, width = x.shape
     args = [dq, dk, dv, x, w, gain.reshape(1, -1), bias.reshape(1, -1), ga]
     if seed is None:
 
         def body(*refs):
-            norm_one_body(*refs[:8], None, *refs[8:])
-
-        kind = f32
+            norm_one_body(*refs[:8], None, None, *refs[8:])
+
+        gw = sds((width, 3 * width), f32)
     else:
-        args.append(seed)
+        args += [seed, gwo]
         body = norm_one_body
-        kind = bf16
-    return pl.pallas_call(
+        gw = sds((nz, 4 * width * width // nz // 128, 128), bf16)
+    return kernel_call(
         body,
+        args=args,
+        deps=deps,
         in_specs=[VM] * len(args),
         out_specs=[VM] * 3,
-        out_shape=[sds((length, width), f32), sds((width, 3 * width), kind), sds((2, width), f32)],
+        out_shape=[sds((length, width), f32), gw, sds((2, width), f32)],
         scratch_shapes=[pltpu.VMEM((length, width), bf16)],
         compiler_params=params(60),
         cost_estimate=cost(12 * length * width * width, length * width * 30),
-    )(*args)
-
-
-def gather_line(x, axis):
-    size = lax.axis_size(axis)
-    me = lax.axis_index(axis)
-    up = [(i, i + 1) for i in range(size - 1)]
-    down = [(i + 1, i) for i in range(size - 1)]
-    full = jnp.zeros((size,) + x.shape, x.dtype)
-    full = lax.dynamic_update_index_in_dim(full, x, me, 0)
-    from_below = from_above = x
-    for step in range(1, size):
-        from_below = lax.ppermute(from_below, axis, up)
-        from_above = lax.ppermute(from_above, axis, down)
-        low = jnp.where(me >= step, me - step, me)
-        high = jnp.where(me + step < size, me + step, me)
-        own = lax.dynamic_index_in_dim(full, me, 0, keepdims=False)
-        full = lax.dynamic_update_index_in_dim(
-            full, jnp.where(me >= step, from_below, own), low, 0
+    )
+
+
+def reduce_body(
+    g_ref, sums_ref, gq_ref, go_ref, tot_ref, r1, s1, r2, s2, r3, fin, v1, v2, v3, w1, w2, *sems
+):
+    nz = lax.axis_size("dp")
+    experts = lax.axis_size("expert")
+    z = lax.axis_index("dp")
+    e = lax.axis_index("expert")
+    chips = experts // 2
+    core = e % 2
+    chip = e // 2
+    mate = (z, chip * 2 + 1 - core)
+    others = [(z, lax.rem(chip + j, chips) * 2 + core) for j in range(1, chips)]
+    layers = [(lax.rem(z + j, nz), e) for j in range(1, nz)]
+    peers = [mate] + others + layers
+    pl.semaphore_wait(greet(peers), len(peers))
+    big, small = sems[:2], sems[2:]
+    whole = g_ref.shape[1]
+    half = whole // 2
+    piece = half // chips
+
+    def copy(src, dst, sem, at, peer):
+        return pltpu.make_async_remote_copy(
+            src_ref=src,
+            dst_ref=dst,
+            send_sem=sem[0].at[at],
+            recv_sem=sem[1].at[at],
+            device_id=peer,
+            device_id_type=MESH,
         )
-        full = lax.dynamic_update_index_in_dim(
-            full, jnp.where(me + step < size, from_above, own), high, 0
-        )
-    return full
+
+    def rows(start, size):
+        return pl.ds(pl.multiple_of(start, 16), size)
+
+    first = [
+        copy(g_ref.at[:, rows((1 - core) * half, half)], r1, big, 0, mate),
+        copy(sums_ref, v1, small, 0, mate),
+    ]
+    for c in first:
+        c.start()
+    for c in first:
+        c.wait()
+    s1[...] = (g_ref[:, rows(core * half, half)].astype(f32) + r1[...].astype(f32)).astype(bf16)
+    w1[...] = sums_ref[...] + v1[...]
+    second = []
+    for j in range(1, chips):
+        k = lax.rem(chip + j, chips)
+        second.append(copy(s1.at[:, rows(k * piece, piece)], r2.at[j - 1], big, j, others[j - 1]))
+        second.append(copy(w1, v2.at[j - 1], small, j, others[j - 1]))
+    for c in second:
+        c.start()
+    for c in second:
+        c.wait()
+    part = s1[:, rows(chip * piece, piece)].astype(f32)
+    line = w1[...]
+    for j in range(1, chips):
+        part = part + r2[j - 1].astype(f32)
+        line = line + v2[j - 1]
+    s2[...] = part.astype(bf16)
+    w2[...] = line
+    third = []
+    for j in range(1, nz):
+        k = lax.rem(z + j, nz)
+        third.append(copy(s2.at[k], r3.at[j - 1], big, chips + j, layers[j - 1]))
+        third.append(copy(w2, v3.at[j - 1], small, chips + j, layers[j - 1]))
+    for c in third:
+        c.start()
+    for c in third:
+        c.wait()
+    part = s2[z].astype(f32)
+    line = w2[...]
+    for j in range(1, nz):
+        part = part + r3[j - 1].astype(f32)
+        line = line + v3[j - 1]
+    tot_ref[...] = line
+    here = fin.at[rows(core * half + chip * piece, piece)]
+    fin[rows(core * half + chip * piece, piece)] = part.astype(bf16)
+    fourth = [copy(here, here, big, chips + nz + j, others[j - 1]) for j in range(1, chips)]
+    for c in fourth:
+        c.start()
+    for c in fourth:
+        c.wait()
+    side = fin.at[rows(core * half, half)]
+    last = copy(side, side, big, 2 * chips + nz, mate)
+    last.start()
+    last.wait()
+    per, wide = gq_ref.shape
+    lanes = g_ref.shape[2]
+    for c in range(whole // per):
+        value = fin[c * per : (c + 1) * per].astype(f32)
+        at = c * lanes
+        if at < wide:
+            gq_ref[:, at : at + lanes] = value
+        else:
+            go_ref[:, at - wide : at - wide + lanes] = value
+
+
+def reduce_call(g, sums, width, experts, nz):
+    whole = g.shape[1]
+    chips = experts // 2
+    half = whole // 2
+    piece = half // chips
+    per = width // nz
+    count = 2 * chips + nz + 1
+    dma = pltpu.SemaphoreType.DMA
+    vec = sums.shape
+    return pl.pallas_call(
+        reduce_body,
+        in_specs=[VM] * 2,
+        out_specs=[VM] * 3,
+        out_shape=[sds((per, 3 * width), f32), sds((per, width), f32), sds(vec, f32)],
+        scratch_shapes=[
+            pltpu.VMEM((nz, half, 128), bf16),
+            pltpu.VMEM((nz, half, 128), bf16),
+            pltpu.VMEM((chips - 1, nz, piece, 128), bf16),
+            pltpu.VMEM((nz, piece, 128), bf16),
+            pltpu.VMEM((nz - 1, piece, 128), bf16),
+            pltpu.VMEM((whole, 128), bf16),
+            pltpu.VMEM(vec, f32),
+            pltpu.VMEM((chips - 1,) + vec, f32),
+            pltpu.VMEM((nz - 1,) + vec, f32),
+            pltpu.VMEM(vec, f32),
+            pltpu.VMEM(vec, f32),
+        ]
+        + [dma((count,))] * 4,
+        compiler_params=pltpu.CompilerParams(
+            vmem_limit_bytes=48 << 20, collective_id=1, has_side_effects=True
+        ),
+        cost_estimate=cost(1 << 24, 150 << 20),
+    )(g, sums)
 
 
 def exchange(x, experts, capacity):
@@ -663,39 +991,58 @@
     slot_row = slot[:, None, :]
     slot_col = slot[:, :, None]
 
-    full_qkv = lax.all_gather(w_qkv, "dp", axis=0, tiled=True)
-    full_out = lax.all_gather(w_out, "dp", axis=0, tiled=True)
-
-    cots = [
-        exchange(send_call(cotangent[s], slot_row[s], total), experts, capacity)
-        for s in range(seqs)
-    ]
+    sends = []
+    last = ()
+    for s in range(seqs):
+        sends.append(send_call(cotangent[s], slot_row[s], total, deps=last))
+        last = (sends[-1],)
+    cots = [exchange(v, experts, capacity) for v in sends]
+    qkv, full_qkv, full_out = qkv_call(tokens_in, ln1_gain, ln1_bias, w_qkv, w_out, nz)
     saved = []
     rows = []
+    last = (sends[-1],)
     for s in range(seqs):
-        qkv = qkv_call(tokens_in[s : s + 1], ln1_gain, ln1_bias, full_qkv)
-        mixed, lse = attn_fwd_call(qkv, HEADS)
+        mixed, lse = attn_fwd_call(qkv, HEADS, s, deps=last)
         after, sent = out_call(
             tokens_in[s], mixed[0], full_out, ln2_gain, ln2_bias, slot_row[s], total
         )
+        last = (sent,)
         rows.append(exchange(sent, experts, capacity))
-        saved.append((qkv, mixed, lse, after))
-
-    act_a, gpre_a, out_a, gtok_a = expert_a_call(rows[0], cots[0], w_in_local, w_down_local, nz)
+        saved.append((mixed, lse, after))
+
+    act_a, gpre_a, out_a, gtok_a = expert_a_call(
+        rows[0], cots[0], w_in_local, w_down_local, nz, deps=last
+    )
+    last = (gtok_a,)
     outs = [exchange(out_a, experts, capacity)]
     gtoks = [exchange(gtok_a, experts, capacity)]
 
     acts, gpres, gdowns, gins = [], [], [], []
     for first, many in ((0, 1), (1, chunks - 1)):
         act_b, gpre_b, gdown, gin = expert_b_call(
-            rows[0], cots[0], act_a, gpre_a, rows[1], cots[1], w_in_local, w_down_local, nz, first, many
+            rows[0],
+            cots[0],
+            act_a,
+            gpre_a,
+            rows[1],
+            cots[1],
+            w_in_local,
+            w_down_local,
+            nz,
+            first,
+            many,
+            deps=last,
         )
+        last = (act_b,)
         acts.append(act_b)
         gpres.append(gpre_b)
         gdowns.append(lax.psum_scatter(gdown, "dp", scatter_dimension=0, tiled=True))
         gins.append(lax.psum_scatter(gin, "dp", scatter_dimension=0, tiled=True))
-    gtoks.append(exchange(expert_c_call(gpres, w_in_local, nz, NT), experts, capacity))
-    outs.append(exchange(expert_c_call(acts, w_down_local, nz, NN), experts, capacity))
+    gtok_b = expert_c_call(gpres, w_in_local, nz, NT, deps=last)
+    gtoks.append(exchange(gtok_b, experts, capacity))
+    out_b = expert_c_call(acts, w_down_local, nz, NN, deps=(gtok_b,))
+    outs.append(exchange(out_b, experts, capacity))
+    last = (out_b,)
 
     results = []
     gxs = []
@@ -703,30 +1050,40 @@
     gw_qkv = None
     sums = 0.0
     for s in range(seqs):
-        qkv, mixed, lse, after = saved[s]
+        mixed, lse, after = saved[s]
         ga, gmix, gw_out, sums_two = norm_two_call(
-            gtoks[s], slot_col[s], after, cotangent[s], mixed[0], full_out, ln2_gain, gw_out
+            gtoks[s],
+            slot_col[s],
+            after,
+            cotangent[s],
+            mixed[0],
+            full_out,
+            ln2_gain,
+            gw_out,
+            deps=last,
         )
-        dq, dk, dv = attn_bwd_call(qkv, mixed, gmix[None], lse, HEADS)
+        dq, dk, dv = attn_bwd_call(qkv, mixed, gmix[None], lse, HEADS, s)
         gx, gw_qkv, sums_one = norm_one_call(
-            dq[0], dk[0], dv[0], tokens_in[s], full_qkv, ln1_gain, ln1_bias, ga, gw_qkv
+            dq[0],
+            dk[0],
+            dv[0],
+            tokens_in[s],
+            full_qkv,
+            ln1_gain,
+            ln1_bias,
+            ga,
+            gw_qkv,
+            gw_out,
+            nz,
         )
+        last = (gx,)
         gxs.append(gx)
-        sums = sums + jnp.concatenate([sums_one, sums_two], axis=0)
-        results.append(add_back_call(after, outs[s], slot_col[s]))
-
-    both = ("expert", "dp")
-    dense = jnp.concatenate([gw_qkv, gw_out.astype(bf16)], axis=1)
-    piece = lax.psum_scatter(
-        dense.reshape(nz, experts, width // nz // experts, 4 * width).swapaxes(0, 1),
-        "expert",
-        scatter_dimension=0,
-        tiled=True,
-    )
-    piece = lax.psum_scatter(piece[0], "dp", scatter_dimension=0, tiled=True)
-    dense = lax.all_gather(piece, "expert", axis=0, tiled=True).reshape(width // nz, 4 * width)
-    dense = dense.astype(f32)
-    sums = lax.psum(sums, both)
+        sums = sums + jnp.concatenate([sums_one, sums_two, sums_one, sums_two], axis=0)
+    for s in range(seqs):
+        results.append(add_back_call(saved[s][2], outs[s], slot_col[s], deps=last))
+        last = (results[-1],)
+
+    gq, go, sums = reduce_call(gw_qkv, sums, width, experts, nz)
     mine = lax.dynamic_slice_in_dim(
         sums, lax.axis_index("dp") * (width // nz), width // nz, axis=1
     )
@@ -737,8 +1094,8 @@
         jnp.stack(gxs),
         mine[0],
         mine[1],
-        dense[:, : 3 * width],
-        dense[:, 3 * width :],
+        gq,
+        go,
         mine[2],
         mine[3],
         gin.astype(f32),

time: 758 us -> 562 us (0.74)
  waiting for transfers between devices: 260 us -> 19 us
  Pallas kernels: 290 us -> 387 us
  blocking collectives: 92.2 us -> 57.2 us
  other arithmetic: 19.6 us -> 11.8 us
    pallas_call x21, Pallas kernels: 290 us -> 387 us  [the longest x19 271 us: kernel_call(): pl.pallas_call(wrapped, in_specs=list(in_specs) + [ANY] * extra, **options)]
    unnamed x10 -> x4, waiting for transfers between devices: 87.6 us -> 0.73 us
    reduce_scatter x2, waiting for transfers between devices: 86.4 us -> 0.02 us  [on_device(): gins.append(lax.psum_scatter(gin, 'dp', scatter_dimension=0, tiled=True))]
    psum x1 -> x0, blocking collectives: 62.7 us -> none  [on_device(): sums = lax.psum(sums, both)]
    all_gather x3 -> x0, waiting for transfers between devices: 56.8 us -> none  [the longest x1 26.8 us: on_device(): full_qkv = lax.all_gather(w_qkv, 'dp', axis=0, tiled=True)]
    all_to_all x1 -> x2, blocking collectives: 29.5 us -> 57.2 us  [exchange(): lax.all_to_all(parts, 'expert', split_axis=0, concat_axis=0, tiled=True)]
    all_to_all x7 -> x6, waiting for transfers between devices: 29.6 us -> 18.2 us  [exchange(): lax.all_to_all(parts, 'expert', split_axis=0, concat_axis=0, tiled=True)]
    all_to_all x7 -> x6, starting transfers between devices: 31.8 us -> 25.1 us  [exchange(): lax.all_to_all(parts, 'expert', split_axis=0, concat_axis=0, tiled=True)]
  transfers between devices with their start and end apart: 16 -> 10, of which waited for: 8 -> 2; matrix products, arithmetic and copies ran while one was open for 3% -> 3% of each run, Pallas kernels for 26% -> 53%
where the time goes in v2:
time: 562 us; the launch traced here: 552 us
  Pallas kernels  387 us (69%)
  blocking collectives  57.2 us (10%)
  local copies, waits for them, and re-layouts  36.8 us (7%)
  starting transfers between devices  25.3 us (5%)
  waiting for transfers between devices  19 us (3%)
  between operations  14.7 us (3%)
  other arithmetic  11.8 us (2%)
    pallas_call x19, Pallas kernels, kernel_call(): pl.pallas_call(wrapped, in_specs=list(in_specs) + [ANY] * extra, **options)  271 us
    pallas_call x1, Pallas kernels, reduce_call(): pl.pallas_call(reduce_body, in_specs=[VM] * 2, out_specs=[VM] * 3, out_sh...  62 us
    all_to_all x2, blocking collectives, exchange(): lax.all_to_all(parts, 'expert', split_axis=0, concat_axis=0, tiled=True)  57.2 us
    pallas_call x1, Pallas kernels, qkv_call(): pl.pallas_call(qkv_body, in_specs=[VM] * 5, out_specs=[VM] * 3, out_shape...  54.3 us
    unnamed x98, local copies, waits for them, and re-layouts  25.7 us
    all_to_all x6, starting transfers between devices, exchange(): lax.all_to_all(parts, 'expert', split_axis=0, concat_axis=0, tiled=True)  25.1 us
    all_to_all x6, waiting for transfers between devices, exchange(): lax.all_to_all(parts, 'expert', split_axis=0, concat_axis=0, tiled=True)  18.2 us
  transfers between devices with their start and end apart: 10, of which 2 were waited for; matrix products, arithmetic and copies ran while one was open for 3% of the time, Pallas kernels for 53%

profile of v2, /device:TPU:0, one launch (start us, length us, event | category | flops | bytes accessed | tf_op | source)
XLA Modules:
  0.0 552.4 jit_solution(5674848024636385148)
XLA Ops:
  19.5 54.3 %shard_map.186 = (bf16[2,1024,2304]{2,1,0:T(8,128)(2,1)}, bf16[768,2304]{1,0:T(8,128)(2,1)}, bf16[768,768]{1,0:T(8,128)(2,1)}) custom-call(bf16[2,1024,768]{2,1,0:T(8,128)(2,1)} %x_ref.1, f32[1,768]{1,0:T(1,128)} %reshape.158.g_ref.refs_5_, f32[1,768]{1,0:T(1,128)} %reshape.159.b_ref.refs_6_, bf16[192,2304]{1,0:T(8,128)(2,1)} %wq_ref.1, bf16[192,768]{1,0:T(8,128)(2,1)} %wo_ref.1), custom_call_target="tpu_custom_call" | custom-call | flops 28991029248 | bytes 31457280 | tf_op jit(solution)/shard_map/pallas_call | solution.py:243
  73.8 12.1 %shard_map.189 = (bf16[1,1024,768]{2,1,0:T(8,128)(2,1)S(1)}, f32[1,6,2,1024]{3,2,1,0:T(2,128)S(1)}) custom-call(bf16[2,1024,2304]{2,1,0:T(8,128)(2,1)} %get-tuple-element.56.refs_0_.refs_1_.refs_2_, bf16[2,1024,2304]{2,1,0:T(8,128)(2,1)} %get-tuple-element.56.refs_0_.refs_1_.refs_2_, bf16[2,1024,2304]{2,1,0:T(8,128)(2,1)} %get-tuple-element.56.refs_0_.refs_1_.refs_2_, ...), custom_call_target="tpu_custom_call" | custom-call | flops 6442450944 | bytes 6291456 | tf_op jit(solution)/shard_map/pallas_call | solution.py:51
  91.8 28.8 %all_to_all.40 = bf16[8,160,768]{2,1,0:T(8,128)(2,1)} all-to-all(bf16[8,160,768]{2,1,0:T(8,128)(2,1)S(1)} %bitcast.70), channel_id=1, replica_groups=mesh['dp'=4,'expert'=8] {'expert'}, dimensions={0} | all-to-all | bytes 3932160 | tf_op jit(solution)/shard_map/all_to_all | solution.py:957
  120.6 4.5 all-to-all-start.1
  125.1 12.1 %shard_map.191 = (bf16[1,1024,768]{2,1,0:T(8,128)(2,1)S(1)}, f32[1,6,2,1024]{3,2,1,0:T(2,128)S(1)}) custom-call(bf16[2,1024,2304]{2,1,0:T(8,128)(2,1)} %get-tuple-element.56.refs_0_.refs_1_.refs_2_, bf16[2,1024,2304]{2,1,0:T(8,128)(2,1)} %get-tuple-element.56.refs_0_.refs_1_.refs_2_, bf16[2,1024,2304]{2,1,0:T(8,128)(2,1)} %get-tuple-element.56.refs_0_.refs_1_.refs_2_, ...), custom_call_target="tpu_custom_call" | custom-call | flops 6442450944 | bytes 6291456 | tf_op jit(solution)/shard_map/pallas_call | solution.py:51
  144.6 5.7 %all-to-all-done.1 = bf16[8,160,768]{2,1,0:T(8,128)(2,1)} async-done(((bf16[8,160,768]{2,1,0:T(8,128)(2,1)}), bf16[8,160,768]{2,1,0:T(8,128)(2,1)}, u32[]{:S(2)}, u32[]{:S(2)}) %all-to-all-start.1) | async-done | bytes 1966112 | tf_op jit(solution)/shard_map/all_to_all | solution.py:957
  150.4 28.3 %all_to_all.41 = bf16[8,160,768]{2,1,0:T(8,128)(2,1)} all-to-all(bf16[8,160,768]{2,1,0:T(8,128)(2,1)S(1)} %bitcast.72), channel_id=1, replica_groups=mesh['dp'=4,'expert'=8] {'expert'}, dimensions={0} | all-to-all | bytes 3932160 | tf_op jit(solution)/shard_map/all_to_all | solution.py:957
  178.7 4.3 all-to-all-start.4
  183.1 36.1 %shard_map.193 = (bf16[3,1280,1024]{2,1,0:T(8,128)(2,1)}, bf16[3,1280,1024]{2,1,0:T(8,128)(2,1)}, bf16[1280,768]{1,0:T(8,128)(2,1)}, bf16[1280,768]{1,0:T(8,128)(2,1)}) custom-call(bf16[1280,768]{1,0:T(8,128)(2,1)} %bitcast.116, bf16[1280,768]{1,0:T(8,128)(2,1)} %bitcast.8.refs_1_, bf16[768,3072]{1,0:T(8,128)(2,1)} %bitcast.83, bf16[768,3072]{1,0:T(8,128)(2,1)} %bitcast.84, ...), custom_call_target="tpu_custom_call" | custom-call | flops 24159191040 | bytes 31457280 | tf_op jit(solution)/shard_map/pallas_call | solution.py:51
  219.3 20.3 %shard_map.194 = (bf16[1,1280,1024]{2,1,0:T(8,128)(2,1)}, bf16[1,1280,1024]{2,1,0:T(8,128)(2,1)}, bf16[4,1,256,768]{3,2,1,0:T(8,128)(2,1)}, bf16[4,1,768,256]{3,2,1,0:T(8,128)(2,1)}) custom-call(bf16[1280,768]{1,0:T(8,128)(2,1)} %bitcast.117, bf16[1280,768]{1,0:T(8,128)(2,1)} %bitcast.8.refs_1_, bf16[3,1280,1024]{2,1,0:T(8,128)(2,1)} %get-tuple-element.64.refs_2_, ...), custom_call_target="tpu_custom_call" | custom-call | flops 12079595520 | bytes 31457280 | tf_op jit(solution)/shard_map/pallas_call | solution.py:51
  239.7 36.8 %shard_map.195 = (bf16[2,1280,1024]{2,1,0:T(8,128)(2,1)}, bf16[2,1280,1024]{2,1,0:T(8,128)(2,1)}, bf16[4,2,256,768]{3,2,1,0:T(8,128)(2,1)}, bf16[4,2,768,256]{3,2,1,0:T(8,128)(2,1)}) custom-call(bf16[1280,768]{1,0:T(8,128)(2,1)} %bitcast.118, bf16[1280,768]{1,0:T(8,128)(2,1)} %bitcast.8.refs_1_, bf16[3,1280,1024]{2,1,0:T(8,128)(2,1)} %get-tuple-element.64.refs_2_, ...), custom_call_target="tpu_custom_call" | custom-call | flops 24159191040 | bytes 31457280 | tf_op jit(solution)/shard_map/pallas_call | solution.py:51
  281.2 12.7 %shard_map.196.refs_6_ = bf16[1280,768]{1,0:T(8,128)(2,1)} custom-call(bf16[1,1280,1024]{2,1,0:T(8,128)(2,1)} %get-tuple-element.67.refs_0_, bf16[2,1280,1024]{2,1,0:T(8,128)(2,1)} %get-tuple-element.69.refs_1_, bf16[768,3072]{1,0:T(8,128)(2,1)} %bitcast.95, bf16[768,3072]{1,0:T(8,128)(2,1)} %bitcast.96, bf16[768,3072]{1,0:T(8,128)(2,1)} %bitcast.97, ...), custom_call_target="tpu_custom_call" | custom-call | flops 6039797760 | bytes 14680064 | tf_op jit(solution)/shard_map/pallas_call | solution.py:51
  294.0 12.5 %all-to-all-done.6 = bf16[8,160,768]{2,1,0:T(8,128)(2,1)S(1)} async-done(((bf16[8,160,768]{2,1,0:T(8,128)(2,1)}), bf16[8,160,768]{2,1,0:T(8,128)(2,1)S(1)}, u32[]{:S(2)}, u32[]{:S(2)}) %all-to-all-start.6) | async-done | bytes 1966112 | tf_op jit(solution)/shard_map/all_to_all | solution.py:957
  313.5 12.6 %shard_map.197.refs_8_ = bf16[1280,768]{1,0:T(8,128)(2,1)} custom-call(bf16[1,1280,1024]{2,1,0:T(8,128)(2,1)} %get-tuple-element.68.refs_14_.refs_0_, bf16[2,1280,1024]{2,1,0:T(8,128)(2,1)} %get-tuple-element.70.refs_6_.refs_1_, bf16[3072,768]{1,0:T(8,128)(2,1)} %bitcast.111, bf16[3072,768]{1,0:T(8,128)(2,1)} %bitcast.112, bf16[3072,768]{1,0:T(8,128)(2,1)} %bitcast.113, ...), custom_call_target="tpu_custom_call" | custom-call | flops 6039797760 | bytes 14680064 | tf_op jit(solution)/shard_map/pallas_call | solution.py:51
  327.7 13.1 %shard_map.198 = (f32[1024,768]{1,0:T(8,128)}, bf16[1024,768]{1,0:T(8,128)(2,1)}, f32[768,768]{1,0:T(8,128)}, f32[2,768]{1,0:T(2,128)}) custom-call(bf16[1280,768]{1,0:T(8,128)(2,1)} %bitcast.126, s32[1024,1]{1,0:T(8,128)} %copy.23.refs_1_.refs_2_, f32[1024,768]{1,0:T(8,128)} %copy-done.4, bf16[1024,768]{1,0:T(8,128)(2,1)} %copy-done.17, ...), custom_call_target="tpu_custom_call" | custom-call | flops 4429185024 | bytes 15728640 | tf_op jit(solution)/shard_map/pallas_call | solution.py:51
  342.1 4.3 all-to-all-start.2
  346.4 23.9 %shard_map.199 = (bf16[1,1024,768]{2,1,0:T(8,128)(2,1)S(1)}, bf16[1,1024,768]{2,1,0:T(8,128)(2,1)S(1)}, bf16[1,1024,768]{2,1,0:T(8,128)(2,1)S(1)}) custom-call(bf16[2,1024,2304]{2,1,0:T(8,128)(2,1)} %get-tuple-element.56.refs_0_.refs_1_.refs_2_, bf16[2,1024,2304]{2,1,0:T(8,128)(2,1)} %get-tuple-element.56.refs_0_.refs_1_.refs_2_, ...), custom_call_target="tpu_custom_call" | custom-call | flops 16106127360 | bytes 12582912 | tf_op jit(solution)/shard_map/pallas_call | solution.py:51
  373.8 16.0 %shard_map.200 = (f32[1024,768]{1,0:T(8,128)}, f32[768,2304]{1,0:T(8,128)}, f32[2,768]{1,0:T(2,128)}) custom-call(bf16[1024,768]{1,0:T(8,128)(2,1)} %bitcast.80, bf16[1024,768]{1,0:T(8,128)(2,1)} %bitcast.81, bf16[1024,768]{1,0:T(8,128)(2,1)} %bitcast.82, bf16[1024,768]{1,0:T(8,128)(2,1)} %get-tuple-element.104.refs_0_.refs_3_, ...), custom_call_target="tpu_custom_call" | custom-call | flops 7247757312 | bytes 23592960 | tf_op jit(solution)/shard_map/pallas_call | solution.py:51
  389.8 13.3 %shard_map.201 = (f32[1024,768]{1,0:T(8,128)}, bf16[1024,768]{1,0:T(8,128)(2,1)}, f32[768,768]{1,0:T(8,128)}, f32[2,768]{1,0:T(2,128)}) custom-call(bf16[1280,768]{1,0:T(8,128)(2,1)} %bitcast.125, s32[1024,1]{1,0:T(8,128)} %copy.22.refs_1_.refs_2_, f32[1024,768]{1,0:T(8,128)} %copy-done.6, bf16[1024,768]{1,0:T(8,128)(2,1)} %copy-done.15, ...), custom_call_target="tpu_custom_call" | custom-call | flops 4429185024 | bytes 15728640 | tf_op jit(solution)/shard_map/pallas_call | solution.py:51
  403.1 4.4 all-to-all-start.7
  407.5 23.9 %shard_map.202 = (bf16[1,1024,768]{2,1,0:T(8,128)(2,1)S(1)}, bf16[1,1024,768]{2,1,0:T(8,128)(2,1)S(1)}, bf16[1,1024,768]{2,1,0:T(8,128)(2,1)S(1)}) custom-call(bf16[2,1024,2304]{2,1,0:T(8,128)(2,1)} %get-tuple-element.56.refs_0_.refs_1_.refs_2_, bf16[2,1024,2304]{2,1,0:T(8,128)(2,1)} %get-tuple-element.56.refs_0_.refs_1_.refs_2_, ...), custom_call_target="tpu_custom_call" | custom-call | flops 16106127360 | bytes 12582912 | tf_op jit(solution)/shard_map/pallas_call | solution.py:51
  434.9 18.1 %shard_map.203 = (f32[1024,768]{1,0:T(8,128)}, bf16[4,4608,128]{2,1,0:T(8,128)(2,1)}, f32[2,768]{1,0:T(2,128)}) custom-call(bf16[1024,768]{1,0:T(8,128)(2,1)} %bitcast.77, bf16[1024,768]{1,0:T(8,128)(2,1)} %bitcast.78, bf16[1024,768]{1,0:T(8,128)(2,1)} %bitcast.79, bf16[1024,768]{1,0:T(8,128)(2,1)} %copy-done.14, ...), custom_call_target="tpu_custom_call" | custom-call | flops 7247757312 | bytes 23592960 | tf_op jit(solution)/shard_map/pallas_call | solution.py:51
  453.8 62.0 %shard_map.206 = (f32[192,2304]{1,0:T(8,128)S(1)}, f32[192,768]{1,0:T(8,128)S(1)}, f32[8,768]{1,0:T(8,128)S(1)}) custom-call(bf16[4,4608,128]{2,1,0:T(8,128)(2,1)} %get-tuple-element.90.g_ref, f32[8,768]{1,0:T(8,128)S(1)} %maximum_add_fusion.sums_ref), custom_call_target="tpu_custom_call" | custom-call | flops 16777216 | bytes 157286400 | tf_op jit(solution)/shard_map/pallas_call | solution.py:929
  531.1 5.3 pad_maximum_fusion
  (140 shorter events, 72.1 us)
Async XLA Ops:
  10.6 127.3 %copy-start.14 = (bf16[1024,768]{1,0:T(8,128)(2,1)}, bf16[1024,768]{1,0:T(8,128)(2,1)S(1)}, u32[]{:S(2)}) copy-start(bf16[1024,768]{1,0:T(8,128)(2,1)S(1)} %get-tuple-element.105.refs_0_.refs_3_) | copy-start | bytes 4718596
  13.8 124.1 %copy-start.20 = (f32[1,768]{1,0:T(1,128)}, f32[1,768]{1,0:T(1,128)S(1)}, u32[]{:S(2)}) copy-start(f32[1,768]{1,0:T(1,128)S(1)} %reshape.160.refs_3_.refs_6_) | copy-start | bytes 9220
  73.8 12.2 %copy-start.16 = (bf16[1024,768]{1,0:T(8,128)(2,1)S(1)}, bf16[1024,768]{1,0:T(8,128)(2,1)}, u32[]{:S(2)}) copy-start(bf16[1024,768]{1,0:T(8,128)(2,1)} %get-tuple-element.104.refs_0_.refs_3_) | copy-start | bytes 4718596
  73.8 12.2 %copy-start.33 = (bf16[768,768]{1,0:T(8,128)(2,1)S(1)}, bf16[768,768]{1,0:T(8,128)(2,1)}, u32[]{:S(2)}) copy-start(bf16[768,768]{1,0:T(8,128)(2,1)} %get-tuple-element.58.refs_2_.refs_5_) | copy-start | bytes 3538948
  120.6 29.8 %all-to-all-start.1 = ((bf16[8,160,768]{2,1,0:T(8,128)(2,1)}), bf16[8,160,768]{2,1,0:T(8,128)(2,1)}, u32[]{:S(2)}, u32[]{:S(2)}) async-start(bf16[8,160,768]{2,1,0:T(8,128)(2,1)} %bitcast.71), calls=%async_computation.1 | async-start | bytes 3932160 | tf_op jit(solution)/shard_map/all_to_all | solution.py:957
  125.1 12.7 %copy-start.34 = (bf16[768,768]{1,0:T(8,128)(2,1)S(1)}, bf16[768,768]{1,0:T(8,128)(2,1)}, u32[]{:S(2)}) copy-start(bf16[768,768]{1,0:T(8,128)(2,1)} %get-tuple-element.58.refs_2_.refs_5_) | copy-start | bytes 3538948
  144.6 34.1 %copy-start.11 = (bf16[1280,768]{1,0:T(8,128)(2,1)}, bf16[1280,768]{1,0:T(8,128)(2,1)S(1)}, u32[]{:S(2)}) copy-start(bf16[1280,768]{1,0:T(8,128)(2,1)S(1)} %get-tuple-element.62.refs_10_) | copy-start | bytes 5898244
  178.7 40.5 %all-to-all-start.4 = ((bf16[8,160,768]{2,1,0:T(8,128)(2,1)}), bf16[8,160,768]{2,1,0:T(8,128)(2,1)}, u32[]{:S(2)}, u32[]{:S(2)}) async-start(bf16[8,160,768]{2,1,0:T(8,128)(2,1)} %bitcast.18), calls=%async_computation.4 | async-start | bytes 3932160 | tf_op jit(solution)/shard_map/all_to_all | solution.py:957
  183.1 353.4 %reduce-scatter.9.cloned.1.call-start = ((), (), s32[]{:S(2)}) async-start(), calls=%async_computation.14 | async-start | bytes 1966080 | tf_op jit(solution)/shard_map/reduce_scatter | solution.py:1039
  239.6 296.9 %reduce-scatter.11.cloned.1.call-start = ((), (), s32[]{:S(2)}) async-start(), calls=%async_computation.15 | async-start | bytes 3932160 | tf_op jit(solution)/shard_map/reduce_scatter | solution.py:1039
  276.5 261.3 %reduce-scatter.7.cloned.1.call-start = ((), (), s32[]{:S(2)}) async-start(), calls=%async_computation.13 | async-start | bytes 3932160 | tf_op jit(solution)/shard_map/reduce_scatter | solution.py:1040
  277.2 29.3 %all-to-all-start.6 = ((bf16[8,160,768]{2,1,0:T(8,128)(2,1)}), bf16[8,160,768]{2,1,0:T(8,128)(2,1)S(1)}, u32[]{:S(2)}, u32[]{:S(2)}) async-start(bf16[8,160,768]{2,1,0:T(8,128)(2,1)} %bitcast.23), calls=%async_computation.6 | async-start | bytes 3932160 | tf_op jit(solution)/shard_map/all_to_all | solution.py:957
  294.0 17.4 %copy-start.39 = (s32[1024,1]{0,1:T(1,128)S(1)}, s32[1024,1]{0,1:T(1,128)}, u32[]{:S(2)}) copy-start(s32[1024,1]{0,1:T(1,128)} %get-tuple-element.113) | copy-start | bytes 12292
  307.8 33.0 %all-to-all-start.5 = ((bf16[8,160,768]{2,1,0:T(8,128)(2,1)}), bf16[8,160,768]{2,1,0:T(8,128)(2,1)S(1)}, u32[]{:S(2)}, u32[]{:S(2)}) async-start(bf16[8,160,768]{2,1,0:T(8,128)(2,1)} %bitcast.115), calls=%async_computation.5 | async-start | bytes 3932160 | tf_op jit(solution)/shard_map/all_to_all | solution.py:957
  311.4 229.2 %reduce-scatter.5.cloned.1.call-start = ((), (), s32[]{:S(2)}) async-start(), calls=%async_computation.12 | async-start | bytes 1966080 | tf_op jit(solution)/shard_map/reduce_scatter | solution.py:1040
  340.8 5.6 %copy-start.26 = (f32[1,6,2,1024]{3,2,1,0:T(2,128)S(1)}, f32[1,6,2,1024]{3,2,1,0:T(2,128)}, u32[]{:S(2)}) copy-start(f32[1,6,2,1024]{3,2,1,0:T(2,128)} %copy-done.25) | copy-start | bytes 147460
  342.1 61.0 %all-to-all-start.2 = ((bf16[8,160,768]{2,1,0:T(8,128)(2,1)}), bf16[8,160,768]{2,1,0:T(8,128)(2,1)S(1)}, u32[]{:S(2)}, u32[]{:S(2)}) async-start(bf16[8,160,768]{2,1,0:T(8,128)(2,1)} %bitcast.124), calls=%async_computation.2 | async-start | bytes 3932160 | tf_op jit(solution)/shard_map/all_to_all | solution.py:957
  403.1 28.3 %copy-start.2 = (bf16[8,160,768]{2,1,0:T(8,128)(2,1)}, bf16[8,160,768]{2,1,0:T(8,128)(2,1)S(1)}, u32[]{:S(2)}) copy-start(bf16[8,160,768]{2,1,0:T(8,128)(2,1)S(1)} %all-to-all-done.2) | copy-start | bytes 5898244
  403.1 121.1 %all-to-all-start.7 = ((bf16[8,160,768]{2,1,0:T(8,128)(2,1)}), bf16[8,160,768]{2,1,0:T(8,128)(2,1)}, u32[]{:S(2)}, u32[]{:S(2)}) async-start(bf16[8,160,768]{2,1,0:T(8,128)(2,1)} %bitcast.121), calls=%async_computation.7 | async-start | bytes 3932160 | tf_op jit(solution)/shard_map/all_to_all | solution.py:957
  434.9 18.1 %copy-start.41 = (f32[2,768]{1,0:T(2,128)S(1)}, f32[2,768]{1,0:T(2,128)}, u32[]{:S(2)}) copy-start(f32[2,768]{1,0:T(2,128)} %get-tuple-element.92) | copy-start | bytes 18436
  434.9 18.1 %copy-start.42 = (f32[2,768]{1,0:T(2,128)S(1)}, f32[2,768]{1,0:T(2,128)}, u32[]{:S(2)}) copy-start(f32[2,768]{1,0:T(2,128)} %get-tuple-element.91) | copy-start | bytes 18436
  434.9 18.1 %copy-start.43 = (f32[2,768]{1,0:T(2,128)S(1)}, f32[2,768]{1,0:T(2,128)}, u32[]{:S(2)}) copy-start(f32[2,768]{1,0:T(2,128)} %get-tuple-element.94) | copy-start | bytes 18436
  453.8 64.7 %copy-start = (f32[1024,768]{1,0:T(8,128)S(1)}, f32[1024,768]{1,0:T(8,128)}, u32[]{:S(2)}) copy-start(f32[1024,768]{1,0:T(8,128)} %get-tuple-element.89.refs_3_) | copy-start | bytes 9437188
  453.8 64.7 %copy-start.9 = (s32[1024,1]{1,0:T(8,128)S(1)}, s32[1024,1]{1,0:T(8,128)}, u32[]{:S(2)}) copy-start(s32[1024,1]{1,0:T(8,128)} %copy.23.refs_1_.refs_2_) | copy-start | bytes 12292
  (34 other events, 74.9 us)
Sparse Core Ops, SparseCore 0:
  239.7 34.3 reduce-scatter.8
  276.6 59.0 reduce-scatter.10
  338.0 60.2 reduce-scatter.6
  400.5 35.3 reduce-scatter.4

commit v3 on v2

v3 whole, which is shorter than its diff:
```python
import functools

import jax
import jax.numpy as jnp
from jax import lax
from jax.experimental import pallas as pl
from jax.experimental.pallas import tpu as pltpu
from jax.sharding import PartitionSpec as P

HEADS = 12
EPS = 1e-5
NEG = -1e30
bf16 = jnp.bfloat16
f32 = jnp.float32
NN = (((1,), (0,)), ((), ()))
NT = (((1,), (1,)), ((), ()))
TN = (((0,), (0,)), ((), ()))
GELU_A = 0.7978845608028654
GELU_B = 0.044715
BLK = 256
FFT = 256


def dot(a, b, dims=NN):
    return lax.dot_general(a, b, dims, preferred_element_type=f32)


def params(mib=56):
    return pltpu.CompilerParams(vmem_limit_bytes=mib << 20)


def cost(flops, nbytes, trans=0):
    return pl.CostEstimate(flops=int(flops), bytes_accessed=int(nbytes), transcendentals=int(trans))


def sds(shape, dtype):
    return jax.ShapeDtypeStruct(shape, dtype)


VM = pl.BlockSpec(memory_space=pltpu.VMEM)
ANY = pl.BlockSpec(memory_space=pl.ANY)


def kernel_call(body, in_specs, args, deps=(), into=None, **options):
    into = into or {}
    count = len(args)
    extra = len(into) + len(deps)

    def wrapped(*refs):
        body(*refs[:count], *refs[count + extra :])

    return pl.pallas_call(
        wrapped,
        in_specs=list(in_specs) + [ANY] * extra,
        input_output_aliases={count + n: out for n, out in enumerate(into)},
        **options,
    )(*args, *into.values(), *deps)


def norm_parts(v):
    centre = jnp.mean(v, axis=-1, keepdims=True)
    shifted = v - centre
    spread = jnp.mean(shifted * shifted, axis=-1, keepdims=True)
    r = lax.rsqrt(spread + EPS)
    return shifted * r, r


MESH = pl.DeviceIdType.MESH


def greet(peers):
    barrier = pltpu.get_barrier_semaphore()
    for peer in peers:
        pl.semaphore_signal(barrier, inc=1, device_id=peer, device_id_type=MESH)
    return barrier


def find_slots(bucket, experts, capacity):
    length = bucket.shape[1]
    hot = (lax.broadcasted_iota(jnp.int32, (experts, length), 0) == bucket).astype(f32)
    upto = lax.broadcasted_iota(jnp.int32, (length, length), 0) <= lax.broadcasted_iota(
        jnp.int32, (length, length), 1
    )
    count = dot(hot.astype(bf16), upto.astype(bf16))
    rank = jnp.sum(hot * count, axis=0, keepdims=True) - 1.0
    return bucket * capacity + rank.astype(jnp.int32)


def qkv_body(
    x_ref,
    g_ref,
    b_ref,
    wq_ref,
    wo_ref,
    buckets_ref,
    cot_ref,
    qkv_ref,
    fq_ref,
    fo_ref,
    row_ref,
    col_ref,
    cots_ref,
    low,
    acc,
    stage,
    sent,
    up_s,
    dn_s,
    core_s,
    z_r,
    core_r,
    loc,
    a2a_s,
    a2a_r,
    out_s,
    stay_s,
):
    nz = lax.axis_size("dp")
    experts = lax.axis_size("expert")
    z = lax.axis_index("dp")
    e = lax.axis_index("expert")
    core = e % 2
    seqs, length, width = x_ref.shape
    per = width // nz
    half = per // 2
    above = (jnp.minimum(z + 1, nz - 1), e)
    below = (jnp.maximum(z - 1, 0), e)
    mate = (z, e + 1 - 2 * core)
    full = (fq_ref, fo_ref)

    barrier = pltpu.get_barrier_semaphore()

    @pl.when(z + 1 < nz)
    def _():
        pl.semaphore_signal(barrier, inc=1, device_id=above, device_id_type=MESH)

    @pl.when(z > 0)
    def _():
        pl.semaphore_signal(barrier, inc=1, device_id=below, device_id_type=MESH)

    plane = [(z, (e + j) % experts) for j in range(1, experts)]
    plane_back = [(e + experts - j) % experts for j in range(1, experts)]
    for peer in plane:
        pl.semaphore_signal(barrier, inc=1, device_id=peer, device_id_type=MESH)

    @pl.when((z + 1 < nz) & (z > 0))
    def _():
        pl.semaphore_wait(barrier, experts + 1)

    @pl.when((z + 1 >= nz) | (z <= 0))
    def _():
        pl.semaphore_wait(barrier, experts)

    def rows_of(ref, p, c):
        return ref.at[pl.ds(pl.multiple_of(p * per + c * half, 16), half)]

    def hop(t, p, c, src, sem, r_sem, peer):
        return pltpu.make_async_remote_copy(
            src_ref=src,
            dst_ref=rows_of(full[t], p, c),
            send_sem=sem.at[t, p],
            recv_sem=r_sem.at[t, p],
            device_id=peer,
            device_id_type=MESH,
        )

    shard = (wq_ref, wo_ref)
    for t in range(2):
        mine = shard[t].at[pl.ds(pl.multiple_of(core * half, 16), half)]

        @pl.when(z + 1 < nz)
        def _(t=t, mine=mine):
            hop(t, z, core, mine, up_s, z_r, above).start()

        @pl.when(z > 0)
        def _(t=t, mine=mine):
            hop(t, z, core, mine, dn_s, z_r, below).start()

    own = [
        pltpu.make_async_copy(
            shard[t], full[t].at[pl.ds(pl.multiple_of(z * per, 16), per)], loc.at[t]
        )
        for t in range(2)
    ]
    for c in own:
        c.start()

    def trade(s, j):
        return pltpu.make_async_remote_copy(
            src_ref=sent.at[s, plane[j][1]],
            dst_ref=cots_ref.at[s, e],
            send_sem=a2a_s.at[s, j],
            recv_sem=a2a_r.at[s, j],
            device_id=plane[j],
            device_id_type=MESH,
        )

    def traded(s, j):
        return pltpu.make_async_remote_copy(
            src_ref=sent.at[s, plane_back[j]],
            dst_ref=cots_ref.at[s, plane_back[j]],
            send_sem=a2a_s.at[s, j],
            recv_sem=a2a_r.at[s, j],
            device_id=plane[j],
            device_id_type=MESH,
        )

    def stay(s):
        return pltpu.make_async_copy(sent.at[s, e], cots_ref.at[s, e], stay_s.at[s])

    blk = min(BLK, length)

    def prepare(s):
        slot = find_slots(buckets_ref[s], experts, cots_ref.shape[2])
        row_ref[s] = slot
        col_ref[s] = jnp.broadcast_to(slot.astype(f32), (8, length)).T[:, :1].astype(jnp.int32)
        place_rows(cot_ref[s], slot, sent.at[s])
        for j in range(experts - 1):
            trade(s, j).start()
        stay(s).start()

    def first_norm(s):
        for a in range(0, length, blk):
            hat, _ = norm_parts(x_ref[s, a : a + blk].astype(f32))
            v = (hat * g_ref[...] + b_ref[...]).astype(bf16)
            for p in range(nz):
                low[p, s * length + a : s * length + a + blk] = v[:, p * per : (p + 1) * per]

    total = seqs * length
    step = min(512, length)

    def product(p, first):
        w = fq_ref[pl.ds(pl.multiple_of(p * per, 16), per)]
        for a in range(0, total, step):
            term = dot(low[p, a : a + step], w)
            if first:
                acc[a : a + step] = term
            else:
                acc[a : a + step] += term

    def arrive(t, p, forward, sem, peer):
        hop(t, p, core, rows_of(full[t], p, core), sem, z_r, peer).wait_recv()
        hop(t, p, core, rows_of(full[t], p, core), core_s, core_r, mate).start()

        @pl.when(forward)
        def _():
            hop(t, p, core, rows_of(full[t], p, core), sem, z_r, peer).start()

    def got(t, p):
        hop(t, p, 1 - core, rows_of(full[t], p, 1 - core), core_s, core_r, mate).wait_recv()

    def arrivals(t, d):
        @pl.when(z - d >= 0)
        def _():
            arrive(t, z - d, z + 1 < nz, up_s, above)

        @pl.when(z + d < nz)
        def _():
            arrive(t, z + d, z > 0, dn_s, below)

    def products(d):
        @pl.when(z - d >= 0)
        def _():
            got(0, z - d)
            product(z - d, False)

        @pl.when(z + d < nz)
        def _():
            got(0, z + d)
            product(z + d, False)

    prepare(0)
    first_norm(0)
    arrivals(0, 1)
    for s in range(1, seqs):
        first_norm(s)
    own[0].wait()
    own[1].wait()
    product(z, True)
    arrivals(0, 2)
    for s in range(1, seqs):
        prepare(s)
    for d in range(1, nz):
        products(d)
        if d + 2 < nz:
            arrivals(0, d + 2)
        if d == 1:
            arrivals(1, 1)

    flights = []
    for n, a in enumerate(range(0, total, step)):
        if n >= 2:
            flights[n - 2].wait()
        stage[n % 2] = acc[a : a + step].astype(bf16)
        flights.append(
            pltpu.make_async_copy(
                stage.at[n % 2],
                qkv_ref.at[a // length, a % length : a % length + step],
                out_s.at[n % 2],
            )
        )
        flights[n].start()
    for d in range(2, nz):
        arrivals(1, d)

    for d in range(1, nz):
        for ok, p in ((z - d >= 0, z - d), (z + d < nz, z + d)):

            @pl.when(ok)
            def _(p=p):
                got(1, p)

    for t in range(2):
        mine = shard[t].at[pl.ds(pl.multiple_of(core * half, 16), half)]

        @pl.when(z + 1 < nz)
        def _(t=t, mine=mine):
            hop(t, z, core, mine, up_s, z_r, above).wait_send()

        @pl.when(z > 0)
        def _(t=t, mine=mine):
            hop(t, z, core, mine, dn_s, z_r, below).wait_send()

        for d in range(1, nz):
            for ok, p, more, sem, peer in (
                (z - d >= 0, z - d, z + 1 < nz, up_s, above),
                (z + d < nz, z + d, z > 0, dn_s, below),
            ):

                @pl.when(ok)
                def _(t=t, p=p):
                    hop(t, p, core, rows_of(full[t], p, core), core_s, core_r, mate).wait_send()

                @pl.when(ok & more)
                def _(t=t, p=p, sem=sem, peer=peer):
                    hop(t, p, core, rows_of(full[t], p, core), sem, z_r, peer).wait_send()

    for c in flights[-2:]:
        c.wait()
    for s in range(seqs):
        stay(s).wait()
        for j in range(experts - 1):
            trade(s, j).wait_send()
            traded(s, j).wait_recv()


def qkv_call(x, gain, bias, wq, wo, buckets, cot, nz, experts, capacity):
    seqs, length, width = x.shape
    triple = wq.shape[1]
    step = min(512, length)
    dma = pltpu.SemaphoreType.DMA
    return pl.pallas_call(
        qkv_body,
        in_specs=[VM] * 7,
        out_specs=[ANY] + [VM] * 4 + [ANY],
        out_shape=[
            sds((seqs, length, triple), bf16),
            sds((width, triple), bf16),
            sds((width, width), bf16),
            sds((seqs, 1, length), jnp.int32),
            sds((seqs, length, 1), jnp.int32),
            sds((seqs, experts, capacity, width), bf16),
        ],
        scratch_shapes=[
            pltpu.VMEM((nz, seqs * length, width // nz), bf16),
            pltpu.VMEM((seqs * length, triple), f32),
            pltpu.VMEM((2, step, triple), bf16),
            pltpu.VMEM((seqs, experts, capacity, width), bf16),
        ]
        + [dma((2, nz))] * 5
        + [dma((2,))]
        + [dma((seqs, experts - 1))] * 2
        + [dma((2,)), dma((seqs,))],
        compiler_params=pltpu.CompilerParams(
            vmem_limit_bytes=60 << 20, collective_id=0, has_side_effects=True
        ),
        cost_estimate=cost(40 << 30, 30 << 20),
    )(x, gain.reshape(1, -1), bias.reshape(1, -1), wq, wo, buckets, cot)


def attn_fwd_body(q_ref, k_ref, v_ref, o_ref, lse_ref, *, blk, hs, scale, depth):
    length = q_ref.shape[1]
    lane = lax.broadcasted_iota(jnp.int32, (1, 2 * hs), 1) // hs
    v_t = v_ref[0].T
    keys = k_ref[0]
    kh = [jnp.where(lane == h, keys, jnp.zeros_like(keys)) for h in range(2)]
    ones = jnp.ones((16, length), bf16)
    vh = [jnp.concatenate([v_t[h * hs : (h + 1) * hs], ones], axis=0) for h in range(2)]
    future = lax.broadcasted_iota(jnp.int32, (blk, blk), 0) > lax.broadcasted_iota(
        jnp.int32, (blk, blk), 1
    )
    tasks = [(i, h) for i in range(length // blk) for h in range(2)]

    def score(task):
        i, h = task
        top = (i + 1) * blk
        q = q_ref[0, i * blk : top, :] * jnp.asarray(scale, bf16)
        s = dot(kh[h][:top], q, NT)
        diag = jnp.where(future, NEG, s[i * blk :])
        s = jnp.concatenate([s[: i * blk], diag], axis=0) if i else diag
        return s, jnp.max(s, axis=0, keepdims=True)

    queue = [score(t) for t in tasks[:depth]]
    done = {}
    for at, task in enumerate(tasks):
        if at + depth < len(tasks):
            queue.append(score(tasks[at + depth]))
        s, largest = queue.pop(0)
        i, h = task
        top = (i + 1) * blk
        o = dot(vh[h][:, :top], jnp.exp(s - largest).astype(bf16))
        total = o[hs : hs + 1]
        done[task] = o[:hs] * (1.0 / total)
        lse_ref[0, 0, h : h + 1, i * blk : top] = largest + jnp.log(total)
        if h == 1:
            both = jnp.concatenate([done[(i, 0)], done[(i, 1)]], axis=0)
            o_ref[0, i * blk : top, :] = both.T.astype(bf16)


def attn_fwd_call(qkv, heads, at, deps=()):
    n, length, triple = 1, *qkv.shape[1:]
    width = triple // 3
    hs = width // heads
    pairs = heads // 2
    blk = min(BLK, length)

    def spec(o, at=0):
        return pl.BlockSpec((1, length, 2 * hs), lambda s, p: (s + at, 0, o * pairs + p))

    return kernel_call(
        functools.partial(attn_fwd_body, blk=blk, hs=hs, scale=hs**-0.5, depth=3),
        args=[qkv, qkv, qkv],
        deps=deps,
        grid=(n, pairs),
        in_specs=[spec(0, at), spec(1, at), spec(2, at)],
        out_specs=[spec(0), pl.BlockSpec((1, 1, 2, length), lambda s, p: (s, p, 0, 0))],
        out_shape=[sds((n, length, width), bf16), sds((n, pairs, 2, length), f32)],
        compiler_params=params(48),
        cost_estimate=cost(13 << 30, n * length * width * 8),
    )


def attn_bwd_body(
    q_ref, k_ref, v_ref, o_ref, do_ref, lse_ref, d_ref, dqa, doa, *, blk, hs, scale, depth
):
    length = q_ref.shape[1]
    n = length // blk
    lanes = lax.broadcasted_iota(jnp.int32, (1, 2 * hs), 1)
    lane = lanes // hs
    spot = lanes % hs
    keys = k_ref[0]
    vals = v_ref[0]
    k_t = (keys * jnp.asarray(scale, bf16)).T
    kh = [jnp.where(lane == h, keys, jnp.zeros_like(keys)) for h in range(2)]
    vh = [
        jnp.where(lane == h, vals, jnp.where(spot < 2, jnp.ones_like(vals), jnp.zeros_like(vals)))
        for h in range(2)
    ]
    future = lax.broadcasted_iota(jnp.int32, (blk, blk), 0) > lax.broadcasted_iota(
        jnp.int32, (blk, blk), 1
    )
    q = q_ref[0] * jnp.asarray(scale, bf16)
    do = do_ref[0]
    prod = do.astype(f32) * o_ref[0].astype(f32)
    for h in range(2):
        inside = lane == h
        inner = -jnp.sum(jnp.where(inside, prod, 0.0), axis=1, keepdims=True)
        high = inner.astype(bf16)
        rest = (inner - high.astype(f32)).astype(bf16)
        doa[h] = jnp.where(
            inside,
            do,
            jnp.where(spot == 0, high, jnp.where(spot == 1, rest, jnp.zeros_like(high))),
        )
    tasks = [(j, h) for j in range(n) for h in range(2)]

    def score(task):
        j, h = task
        a = j * blk
        return (
            dot(kh[h][a : a + blk], q[a:], NT),
            dot(vh[h][a : a + blk], doa[h, a:], NT),
        )

    queue = [score(t) for t in tasks[:depth]]
    kept = None
    for at, task in enumerate(tasks):
        if at + depth < len(tasks):
            queue.append(score(tasks[at + depth]))
        s, dp = queue.pop(0)
        j, h = task
        a = j * blk
        p = jnp.exp(s - lse_ref[0, 0, h : h + 1, a:])
        diag = jnp.where(future, 0.0, p[:, :blk])
        p = jnp.concatenate([diag, p[:, blk:]], axis=1) if j < n - 1 else diag
        ds = (p * dp).astype(bf16)
        dv = dot(p.astype(bf16), do[a:])
        dk = dot(ds, q[a:])
        dq = dot(k_t[h * hs : (h + 1) * hs, a : a + blk], ds)
        if j == 0:
            dqa[h * hs : (h + 1) * hs, :] = dq
        else:
            dqa[h * hs : (h + 1) * hs, a:] += dq
        if h == 0:
            kept = (dk, dv)
        else:
            d_ref[0, 1, a : a + blk, :] = jnp.where(lane == 0, kept[0], dk).astype(bf16)
            d_ref[0, 2, a : a + blk, :] = jnp.where(lane == 0, kept[1], dv).astype(bf16)
            d_ref[0, 0, a : a + blk, :] = dqa[:, a : a + blk].T.astype(bf16)


def attn_bwd_call(qkv, o, do, lse, heads, at, into=None, deps=()):
    seqs, length, triple = qkv.shape
    n = 1
    width = triple // 3
    hs = width // heads
    pairs = heads // 2
    blk = min(BLK, length)

    def spec(o, at=0):
        return pl.BlockSpec((1, length, 2 * hs), lambda s, p: (s + at, 0, o * pairs + p))

    return kernel_call(
        functools.partial(attn_bwd_body, blk=blk, hs=hs, scale=hs**-0.5, depth=2),
        args=[qkv, qkv, qkv, o, do, lse],
        deps=deps,
        grid=(n, pairs),
        in_specs=[spec(0, at), spec(1, at), spec(2, at), spec(0), spec(0)]
        + [pl.BlockSpec((1, 1, 2, length), lambda s, p: (s, p, 0, 0))],
        out_specs=pl.BlockSpec((1, 3, length, 2 * hs), lambda s, p: (at, 0, 0, p)),
        out_shape=sds((seqs, 3, length, width), bf16),
        into=into,
        scratch_shapes=[
            pltpu.VMEM((2 * hs, length), f32),
            pltpu.VMEM((2, length, 2 * hs), bf16),
        ],
        compiler_params=params(48),
        cost_estimate=cost(27 << 30, n * length * width * 16),
    )


def slot_chunk(total):
    return 256 if total % 256 == 0 else total


def place_rows(rows, slot_row, out_ref):
    experts, capacity, _ = out_ref.shape
    base = lax.broadcasted_iota(jnp.int32, (capacity, rows.shape[0]), 0)
    for e in range(experts):
        hot = jnp.where(base + e * capacity == slot_row, 1.0, 0.0).astype(bf16)
        out_ref[e] = dot(hot, rows).astype(bf16)


def take_rows(slots, slot_col):
    total = slots.shape[0]
    at = lax.broadcasted_iota(jnp.int32, (slot_col.shape[0], total), 1)
    return dot(jnp.where(at == slot_col, 1.0, 0.0).astype(bf16), slots)


def out_body(x_ref, mixed_ref, w_ref, g_ref, b_ref, slot_ref, after_ref, sent_ref, toks):
    size = x_ref.shape[1]
    after = x_ref[0].astype(f32) + dot(mixed_ref[0], w_ref[...])
    after_ref[0] = after
    hat, _ = norm_parts(after)
    step = pl.program_id(0)
    toks[pl.ds(pl.multiple_of(step * size, size), size)] = (
        hat * g_ref[...] + b_ref[...]
    ).astype(bf16)

    @pl.when(step == pl.num_programs(0) - 1)
    def _():
        place_rows(toks[...], slot_ref[0], sent_ref)


def out_call(x, mixed, w, gain, bias, slot_row, experts, capacity, at, into=None):
    seqs, length, width = x.shape
    blk = min(BLK, length)

    def keep(*shape):
        return pl.BlockSpec(shape, lambda r: (0,) * len(shape))

    rows = pl.BlockSpec((1, blk, width), lambda r: (at, r, 0))
    return kernel_call(
        out_body,
        args=[x, mixed, w, gain.reshape(1, -1), bias.reshape(1, -1), slot_row],
        into=into,
        grid=(length // blk,),
        in_specs=[
            rows,
            pl.BlockSpec((1, blk, width), lambda r: (0, r, 0)),
            keep(width, width),
            keep(1, width),
            keep(1, width),
            pl.BlockSpec((1, 1, length), lambda r: (at, 0, 0)),
        ],
        out_specs=[rows, keep(experts, capacity, width)],
        out_shape=[sds((seqs, length, width), f32), sds((experts, capacity, width), bf16)],
        scratch_shapes=[pltpu.VMEM((length, width), bf16)],
        compiler_params=params(40),
        cost_estimate=cost(5 << 30, length * width * 12),
    )


def gelu_parts(pre):
    sq = pre * pre
    half = 0.5 + 0.5 * jnp.tanh(pre * (GELU_A + (GELU_A * GELU_B) * sq))
    act = pre * half
    slope = half + (act - act * half) * (2 * GELU_A + (6 * GELU_A * GELU_B) * sq)
    return act, slope


def hidden_rows(rows_ref, cot_ref, w_in, w_down, act_ref, gpre_ref, use=None):
    total = rows_ref.shape[0]
    step = slot_chunk(total)
    starts = list(range(0, total, step))

    def first(a):
        return dot(rows_ref[a : a + step], w_in), dot(cot_ref[a : a + step], w_down, NT)

    ahead = first(starts[0])
    for at, a in enumerate(starts):
        pre, gact = ahead
        if at + 1 < len(starts):
            ahead = first(starts[at + 1])
        act, slope = gelu_parts(pre)
        act_low = act.astype(bf16)
        gpre_low = (gact * slope).astype(bf16)
        act_ref[0, a : a + step] = act_low
        gpre_ref[0, a : a + step] = gpre_low
        if use is not None:
            use(a, a + step, act_low, gpre_low)


def join_cols(refs):
    return jnp.concatenate([r[...] for r in refs], axis=1)


def join_rows(refs):
    return jnp.concatenate([r[...] for r in refs], axis=0)


def expert_a_body(*refs, nz):
    rows_ref, cot_ref = refs[:2]
    w_in = join_cols(refs[2 : 2 + nz])
    w_down = join_rows(refs[2 + nz : 2 + 2 * nz])
    act_ref, gpre_ref = refs[2 + 2 * nz :]
    hidden_rows(rows_ref, cot_ref.at[0], w_in, w_down, act_ref, gpre_ref)


def weight_specs(width, hidden, nz, first=0):
    per = hidden // (nz * FFT)
    ins = [
        pl.BlockSpec((width, FFT), lambda c, z=z: (0, z * per + c + first)) for z in range(nz)
    ]
    downs = [
        pl.BlockSpec((FFT, width), lambda c, z=z: (z * per + c + first, 0)) for z in range(nz)
    ]
    return ins + downs


def expert_a_call(rows, cot, w_in, w_down, nz, deps=()):
    total, width = rows.shape
    hidden = w_in.shape[1]
    chunks = hidden // (nz * FFT)
    tile = nz * FFT
    keep = pl.BlockSpec((total, width), lambda c: (0, 0))
    cots = pl.BlockSpec((1, total, width), lambda c: (0, 0, 0))
    mid = pl.BlockSpec((1, total, tile), lambda c: (c, 0, 0))
    return kernel_call(
        functools.partial(expert_a_body, nz=nz),
        args=[rows, cot, *([w_in] * nz), *([w_down] * nz)],
        deps=deps,
        grid=(chunks,),
        in_specs=[keep, cots] + weight_specs(width, hidden, nz),
        out_specs=[mid, mid],
        out_shape=[sds((chunks, total, tile), bf16)] * 2,
        compiler_params=params(60),
        cost_estimate=cost(20 << 30, 30 << 20),
    )


def expert_b_body(*refs, nz):
    rows_a, cot_a, act_a, gpre_a, rows_b, cot_b = refs[:6]
    w_in = join_cols(refs[6 : 6 + nz])
    w_down = join_rows(refs[6 + nz : 6 + 2 * nz])
    act_b, gpre_b, gdown_ref, gin_ref = refs[6 + 2 * nz :]
    cot_a, cot_b = cot_a.at[0], cot_b.at[0]
    hidden_rows(rows_b, cot_b, w_in, w_down, act_b, gpre_b)
    for z in range(nz):
        cols = slice(z * FFT, (z + 1) * FFT)
        gdown = dot(act_a[0, :, cols], cot_a[...], TN) + dot(act_b[0, :, cols], cot_b[...], TN)
        gdown_ref[z, 0] = gdown.astype(bf16)
        gin = dot(rows_a[...], gpre_a[0, :, cols], TN) + dot(rows_b[...], gpre_b[0, :, cols], TN)
        gin_ref[z, 0] = gin.astype(bf16)


def expert_b_call(rows_a, act_a, gpre_a, rows_b, cots, w_in, w_down, nz, first, count, deps=()):
    total, width = rows_a.shape
    hidden = w_in.shape[1]
    tile = nz * FFT
    keep = pl.BlockSpec((total, width), lambda c: (0, 0))
    mid = pl.BlockSpec((1, total, tile), lambda c: (c + first, 0, 0))

    def cot(s):
        return pl.BlockSpec((1, total, width), lambda c: (s, 0, 0))

    mid_out = pl.BlockSpec((1, total, tile), lambda c: (c, 0, 0))
    return kernel_call(
        functools.partial(expert_b_body, nz=nz),
        args=[rows_a, cots, act_a, gpre_a, rows_b, cots, *([w_in] * nz), *([w_down] * nz)],
        deps=deps,
        grid=(count,),
        in_specs=[keep, cot(0), mid, mid, keep, cot(1)] + weight_specs(width, hidden, nz, first),
        out_specs=[
            mid_out,
            mid_out,
            pl.BlockSpec((nz, 1, FFT, width), lambda c: (0, c, 0, 0)),
            pl.BlockSpec((nz, 1, width, FFT), lambda c: (0, c, 0, 0)),
        ],
        out_shape=[
            sds((count, total, tile), bf16),
            sds((count, total, tile), bf16),
            sds((nz, count, FFT, width), bf16),
            sds((nz, count, width, FFT), bf16),
        ],
        compiler_params=params(60),
        cost_estimate=cost(20 * count << 30, 30 << 20),
    )


def expert_c_body(*refs, nz, counts, dims):
    parts = len(counts)
    mids = refs[:parts]
    w_refs = refs[parts : parts + nz]
    out_ref, acc = refs[parts + nz :]
    w = join_cols(w_refs) if dims is NT else join_rows(w_refs)
    c = pl.program_id(0)
    total = acc.shape[0]
    step = slot_chunk(total)
    lo = 0
    for m, k in zip(mids, counts):

        @pl.when((c >= lo) & (c < lo + k))
        def _(m=m, lo=lo):
            for a in range(0, total, step):
                term = dot(m[0, a : a + step], w, dims)
                if lo == 0:
                    acc[a : a + step] = jnp.where(c == 0, term, acc[a : a + step] + term)
                else:
                    acc[a : a + step] += term

        lo += k

    @pl.when(c == pl.num_programs(0) - 1)
    def _():
        out_ref[...] = acc[...].astype(bf16)


def expert_c_call(mids, w, nz, dims, deps=()):
    total, tile = mids[0].shape[1:]
    hidden = tile * sum(m.shape[0] for m in mids)
    width = w.shape[0] if dims is NT else w.shape[1]
    chunks = hidden // tile
    specs = weight_specs(width, hidden, nz)
    specs = specs[:nz] if dims is NT else specs[nz:]
    counts = [m.shape[0] for m in mids]
    blocks = []
    for n, k in enumerate(counts):
        lo = sum(counts[:n])
        blocks.append(
            pl.BlockSpec(
                (1, total, tile), lambda c, lo=lo, k=k: (jnp.clip(c - lo, 0, k - 1), 0, 0)
            )
        )
    return kernel_call(
        functools.partial(expert_c_body, nz=nz, counts=counts, dims=dims),
        args=[*mids, *([w] * nz)],
        deps=deps,
        grid=(chunks,),
        in_specs=blocks + specs,
        out_specs=pl.BlockSpec((total, width), lambda c: (0, 0)),
        out_shape=sds((total, width), bf16),
        scratch_shapes=[pltpu.VMEM((total, width), f32)],
        compiler_params=params(60),
        cost_estimate=cost(10 << 30, 14 << 20),
    )


def norm_two_body(
    back_ref, slot_ref, after_ref, cot_ref, mixed_ref, w_ref, g_ref, ga_ref, gmix_ref, gw_ref, sums_ref, low
):
    size = after_ref.shape[1]
    part = size // 2
    starts = [0, part]
    back = back_ref[...]
    gts = [take_rows(back, slot_ref[0, a : a + part]) for a in starts]
    gain_sum = 0.0
    bias_sum = 0.0
    for a, gt in zip(starts, gts):
        rows = slice(a, a + part)
        hat, r = norm_parts(after_ref[0, rows])
        gain_sum = gain_sum + jnp.sum(gt * hat, axis=0, keepdims=True)
        bias_sum = bias_sum + jnp.sum(gt, axis=0, keepdims=True)
        s = gt * g_ref[...]
        ga = cot_ref[0, rows].astype(f32) + r * (
            s
            - jnp.mean(s, axis=-1, keepdims=True)
            - hat * jnp.mean(s * hat, axis=-1, keepdims=True)
        )
        ga_ref[0, rows] = ga
        low[rows] = ga.astype(bf16)
        gmix_ref[0, rows] = dot(low[rows], w_ref[...], NT).astype(bf16)
    gw = dot(mixed_ref[0], low[...], TN)

    @pl.when(pl.program_id(0) == 0)
    def _():
        gw_ref[...] = gw
        sums_ref[0:1] = gain_sum
        sums_ref[1:2] = bias_sum

    @pl.when(pl.program_id(0) > 0)
    def _():
        gw_ref[...] += gw
        sums_ref[0:1] += gain_sum
        sums_ref[1:2] += bias_sum


def norm_two_call(back, slot_col, after, cot, mixed, w, gain, at, into=None, deps=()):
    seqs, length, width = after.shape
    total = back.shape[0]
    blk = min(2 * BLK, length)

    def keep(*shape):
        return pl.BlockSpec(shape, lambda r: (0,) * len(shape))

    rows = pl.BlockSpec((1, blk, width), lambda r: (at, r, 0))
    single = pl.BlockSpec((1, blk, width), lambda r: (0, r, 0))
    return kernel_call(
        norm_two_body,
        args=[back, slot_col, after, cot, mixed, w, gain.reshape(1, -1)],
        deps=deps,
        into=into,
        grid=(length // blk,),
        in_specs=[
            keep(total, width),
            pl.BlockSpec((1, blk, 1), lambda r: (at, r, 0)),
            rows,
            rows,
            single,
            keep(width, width),
            keep(1, width),
        ],
        out_specs=[rows, single, keep(width, width), keep(2, width)],
        out_shape=[
            sds((seqs, length, width), f32),
            sds((1, length, width), bf16),
            sds((width, width), f32),
            sds((2, width), f32),
        ],
        scratch_shapes=[pltpu.VMEM((blk, width), bf16)],
        compiler_params=params(56),
        cost_estimate=cost(9 << 30, length * width * 20),
    )


GROUPS = 4


def last_body(*refs, seqs, per_seq, plan):
    (dw_ref, d_ref, xw_ref, x_ref, w_ref, g_ref, b_ref, ga_ref) = refs[:8]
    gwos = refs[8 : 8 + seqs]
    sums_ref, after_ref = refs[8 + seqs : 10 + seqs]
    backs = refs[10 + seqs : 10 + 2 * seqs]
    slot_ref = refs[10 + 2 * seqs]
    gx_ref, res_ref, gq_ref, go_ref, tot_ref = refs[11 + 2 * seqs : 16 + 2 * seqs]
    acc, low, pay, r1, r2, s2, r3, fin, w0, v1, w1, v2, w2, v3 = refs[16 + 2 * seqs : 30 + 2 * seqs]
    send_s, recv_s, vs_s, vr_s = refs[30 + 2 * seqs :]
    nz = lax.axis_size("dp")
    experts = lax.axis_size("expert")
    z = lax.axis_index("dp")
    e = lax.axis_index("expert")
    chips = experts // 2
    core = e % 2
    chip = e // 2
    mate = (z, chip * 2 + 1 - core)
    others = [(z, lax.rem(chip + j, chips) * 2 + core) for j in range(1, chips)]
    layers = [(lax.rem(z + j, nz), e) for j in range(1, nz)]
    peers = [mate] + others + layers
    width = x_ref.shape[2]
    step = pl.program_id(0)
    last = pl.num_programs(0) - 1
    s1 = r1

    def copy(src, dst, at, peer, sems=None):
        a, b = sems or (send_s, recv_s)
        return pltpu.make_async_remote_copy(
            src_ref=src,
            dst_ref=dst,
            send_sem=a.at[at],
            recv_sem=b.at[at],
            device_id=peer,
            device_id_type=MESH,
        )

    def stage(n, t):
        if n == 1:
            return [copy(pay.at[t, 1 - core], r1.at[t], (t, 0), mate)]
        if n == 2:
            return [
                copy(
                    s1.at[t, lax.rem(chip + j, chips)], r2.at[t, j - 1], (t, j), others[j - 1]
                )
                for j in range(1, chips)
            ]
        if n == 3:
            return [
                copy(
                    s2.at[t, lax.rem(z + j, nz)], r3.at[t, j - 1], (t, chips + j), layers[j - 1]
                )
                for j in range(1, nz)
            ]
        if n == 4:
            here = fin.at[t, core, chip]
            return [
                copy(here, here, (t, chips + nz + j), others[j - 1]) for j in range(1, chips)
            ]
        side = fin.at[t, core]
        return [copy(side, side, (t, 2 * chips + nz), mate)]

    def vector(n):
        sems = (vs_s, vr_s)
        if n == 1:
            return [copy(w0, v1, 0, mate, sems)]
        if n == 2:
            return [copy(w1, v2.at[j - 1], j, others[j - 1], sems) for j in range(1, chips)]
        return [copy(w2, v3.at[j - 1], chips + j, layers[j - 1], sems) for j in range(1, nz)]

    def start(n, t):
        for c in vector(n) if t is None else stage(n, t):
            c.start()

    def finish(n, t):
        for c in vector(n) if t is None else stage(n, t):
            c.wait()
        if t is None:
            if n == 1:
                w1[...] = w0[...] + v1[...]
            elif n == 2:
                line = w1[...]
                for j in range(1, chips):
                    line = line + v2[j - 1]
                w2[...] = line
            else:
                line = w2[...]
                for j in range(1, nz):
                    line = line + v3[j - 1]
                tot_ref[...] = line
            if n < 3:
                start(n + 1, None)
            return
        if n == 1:
            for k in range(chips):
                s1[t, k] = (pay[t, core, k].astype(f32) + r1[t, k].astype(f32)).astype(bf16)
        elif n == 2:
            part = s1[t, chip].astype(f32)
            for j in range(1, chips):
                part = part + r2[t, j - 1].astype(f32)
            s2[t] = part.astype(bf16)
        elif n == 3:
            part = s2[t, z].astype(f32)
            for j in range(1, nz):
                part = part + r3[t, j - 1].astype(f32)
            fin[t, core, chip] = part.astype(bf16)
        elif n == 5:
            piece = fin.shape[3]
            for c in range(2):
                for k in range(chips):
                    at = (c * chips + k) * piece
                    value = fin[t, c, k].astype(f32)
                    if t < 3:
                        gq_ref[at : at + piece, t * width : (t + 1) * width] = value
                    else:
                        go_ref[at : at + piece, :] = value
        if n < 5:
            start(n + 1, t)

    def pack(value, t):
        per = value.shape[0] // nz
        piece = pay.shape[4]
        for zz in range(nz):
            for c in range(2):
                for k in range(chips):
                    at = zz * per + (c * chips + k) * piece
                    pay[t, c, k, zz] = value[at : at + piece].astype(bf16)
        start(1, t)

    @pl.when(step == 0)
    def _():
        pl.semaphore_wait(greet(peers), len(peers))
        gwo = gwos[0][...]
        for s in range(1, seqs):
            gwo = gwo + gwos[s][...]
        pack(gwo, 3)

    for n in range(3 * seqs):
        t, s = n // seqs, n % seqs

        @pl.when(step == n)
        def _(t=t, s=s):
            if t == 0:
                hat, _ = norm_parts(xw_ref[0].astype(f32))
                low[s] = (hat * g_ref[...] + b_ref[...]).astype(bf16)
            term = dot(low[s], dw_ref[0, 0], TN)
            if s == 0:
                acc[...] = term
            elif s < seqs - 1:
                acc[...] += term
            else:
                pack(acc[...] + term, t)

    base = 3 * seqs

    @pl.when(step == base)
    def _():
        w0[0:2] = jnp.zeros((2, width), f32)
        w0[2:8] = sums_ref[2:8]

    @pl.when((step >= base) & (step < base + seqs * per_seq))
    def _():
        hat, r = norm_parts(x_ref[0].astype(f32))
        gn = 0.0
        for t in range(3):
            gn = gn + dot(d_ref[0, t], w_ref[:, t * width : (t + 1) * width], NT)
        w0[0:1] += jnp.sum(gn * hat, axis=0, keepdims=True)
        w0[1:2] += jnp.sum(gn, axis=0, keepdims=True)
        g = gn * g_ref[...]
        gx_ref[0] = ga_ref[0] + r * (
            g
            - jnp.mean(g, axis=-1, keepdims=True)
            - hat * jnp.mean(g * hat, axis=-1, keepdims=True)
        )

    base = base + seqs * per_seq

    @pl.when(step == base - 1)
    def _():
        start(1, None)

    for s in range(seqs):

        @pl.when((step >= base + s * per_seq) & (step < base + (s + 1) * per_seq))
        def _(s=s):
            res_ref[0] = after_ref[0] + take_rows(backs[s][...], slot_ref[0])

    for when, events in plan:

        @pl.when(step == when)
        def _(events=events):
            for n, t in events:
                finish(n, t)


def last_plan(seqs, per_seq):
    dw = 3 * seqs
    end = dw + 2 * seqs * per_seq - 1
    mid = dw + seqs * per_seq
    first = [
        (2, [(1, 3)]),
        (4, [(1, 0)]),
        (dw, [(1, 1)]),
        (dw + 1, [(2, 3)]),
        (dw + 2, [(1, 2)]),
        (dw + 3, [(3, 3)]),
        (dw + 5, [(2, 0)]),
        (dw + 6, [(4, 3)]),
        (dw + 7, [(3, 0)]),
        (mid, [(5, 3)]),
        (mid + 1, [(2, 1), (1, None)]),
        (mid + 2, [(4, 0)]),
        (mid + 3, [(3, 1), (2, None)]),
        (mid + 4, [(5, 0)]),
        (mid + 5, [(3, None)]),
        (mid + 6, [(4, 1)]),
        (end, [(2, 2), (5, 1), (3, 2), (4, 2), (5, 2)]),
    ]
    return [(min(a, end), b) for a, b in first]


def last_call(d, x, w, gain, bias, ga, gwos, sums, after, backs, slot_col, experts, nz, deps=()):
    seqs, length, width = x.shape
    blk = min(BLK, length)
    per_seq = length // blk
    total = backs[0].shape[0]
    dw = 3 * seqs
    mid = dw + seqs * per_seq
    chips = experts // 2
    piece = width // nz // experts
    per = width // nz
    dma = pltpu.SemaphoreType.DMA
    once = pl.Buffered(1)

    def keep(*shape):
        return pl.BlockSpec(shape, lambda r: (0,) * len(shape), pipeline_mode=once)

    def at(first, r):
        n = jnp.clip(r - first, 0, seqs * per_seq - 1)
        return n // per_seq, n % per_seq

    def dw_at(r):
        n = jnp.minimum(r, dw - 1)
        return n % seqs, n // seqs, 0, 0

    def rows(first):
        return pl.BlockSpec((1, blk, width), lambda r: (*at(first, r), 0))

    def d_at(r):
        s, b = at(dw, r)
        return s, 0, b, 0

    steps = mid + seqs * per_seq
    in_specs = [
        pl.BlockSpec((1, 1, length, width), dw_at),
        pl.BlockSpec((1, 3, blk, width), d_at),
        pl.BlockSpec((1, length, width), lambda r: (jnp.minimum(r, seqs - 1), 0, 0)),
        rows(dw),
        keep(width, 3 * width),
        keep(1, width),
        keep(1, width),
        rows(dw),
    ]
    in_specs += [keep(width, width)] * seqs + [keep(8, width), rows(mid)]
    in_specs += [keep(total, width)] * seqs
    in_specs += [pl.BlockSpec((1, blk, 1), lambda r: (*at(mid, r), 0))]
    return pl.pallas_call(
        functools.partial(last_body, seqs=seqs, per_seq=per_seq, plan=last_plan(seqs, per_seq)),
        grid=(steps,),
        in_specs=in_specs,
        out_specs=[rows(dw), rows(mid), keep(per, 3 * width), keep(per, width), keep(8, width)],
        out_shape=[
            sds((seqs, length, width), f32),
            sds((seqs, length, width), f32),
            sds((per, 3 * width), f32),
            sds((per, width), f32),
            sds((8, width), f32),
        ],
        scratch_shapes=[
            pltpu.VMEM((width, width), f32),
            pltpu.VMEM((seqs, length, width), bf16),
            pltpu.VMEM((GROUPS, 2, chips, nz, piece, width), bf16),
            pltpu.VMEM((GROUPS, chips, nz, piece, width), bf16),
            pltpu.VMEM((GROUPS, chips - 1, nz, piece, width), bf16),
            pltpu.VMEM((GROUPS, nz, piece, width), bf16),
            pltpu.VMEM((GROUPS, nz - 1, piece, width), bf16),
            pltpu.VMEM((GROUPS, 2, chips, piece, width), bf16),
            pltpu.VMEM((8, width), f32),
            pltpu.VMEM((8, width), f32),
            pltpu.VMEM((8, width), f32),
            pltpu.VMEM((chips - 1, 8, width), f32),
            pltpu.VMEM((8, width), f32),
            pltpu.VMEM((nz - 1, 8, width), f32),
        ]
        + [dma((GROUPS, 2 * chips + nz + 1))] * 2
        + [dma((chips + nz,))] * 2,
        compiler_params=pltpu.CompilerParams(
            vmem_limit_bytes=62 << 20, collective_id=1, has_side_effects=True
        ),
        cost_estimate=cost(50 << 30, 150 << 20),
    )(
        d,
        d,
        x,
        x,
        w,
        gain.reshape(1, -1),
        bias.reshape(1, -1),
        ga,
        *gwos,
        sums,
        after,
        *backs,
        slot_col,
    )


def exchange(parts):
    got = lax.all_to_all(parts, "expert", split_axis=0, concat_axis=0, tiled=True)
    return got.reshape(-1, parts.shape[-1])


def on_device(
    tokens_in,
    buckets,
    ln1_gain,
    ln1_bias,
    w_qkv,
    w_out,
    ln2_gain,
    ln2_bias,
    w_in,
    w_down,
    cotangent,
):
    experts = lax.axis_size("expert")
    nz = lax.axis_size("dp")
    seqs, length, width = tokens_in.shape
    capacity = 5 * length // (4 * experts)
    total = experts * capacity
    w_in_local = w_in[0]
    w_down_local = w_down[0]
    hidden = w_in_local.shape[1]
    chunks = hidden // (nz * FFT)

    qkv, full_qkv, full_out, slot_row, slot_col, cots = qkv_call(
        tokens_in,
        ln1_gain,
        ln1_bias,
        w_qkv,
        w_out,
        buckets.reshape(seqs, 1, length),
        cotangent,
        nz,
        experts,
        capacity,
    )
    cots = cots.reshape(seqs, total, width)
    saved = []
    rows = []
    last = ()
    after = None
    for s in range(seqs):
        mixed, lse = attn_fwd_call(qkv, HEADS, s, deps=last)
        after, sent = out_call(
            tokens_in,
            mixed,
            full_out,
            ln2_gain,
            ln2_bias,
            slot_row,
            experts,
            capacity,
            s,
            into={0: after} if s else None,
        )
        last = (sent,)
        rows.append(exchange(sent))
        saved.append((mixed, lse))

    act_a, gpre_a = expert_a_call(rows[0], cots, w_in_local, w_down_local, nz, deps=last)
    last = (gpre_a,)
    acts, gpres, gdowns, gins = [], [], [], []
    for first, many in ((0, 1), (1, chunks - 1)):
        act_b, gpre_b, gdown, gin = expert_b_call(
            rows[0],
            act_a,
            gpre_a,
            rows[1],
            cots,
            w_in_local,
            w_down_local,
            nz,
            first,
            many,
            deps=last,
        )
        last = (act_b,)
        acts.append(act_b)
        gpres.append(gpre_b)
        gdowns.append(lax.psum_scatter(gdown, "dp", scatter_dimension=0, tiled=True))
        gins.append(lax.psum_scatter(gin, "dp", scatter_dimension=0, tiled=True))

    def tokens_of(mids, w, dims, last):
        made = expert_c_call(mids, w, nz, dims, deps=last)
        return exchange(made.reshape(experts, capacity, width)), (made,)

    gtok_a, last = tokens_of([gpre_a], w_in_local, NT, last)
    gtok_b, last = tokens_of(gpres, w_in_local, NT, last)
    out_a, last = tokens_of([act_a], w_down_local, NN, last)
    gtoks = [gtok_a, gtok_b]

    d = ga = None
    gwos = []
    sums_two = 0.0
    for s in range(seqs):
        mixed, lse = saved[s]
        ga, gmix, gwo, sums = norm_two_call(
            gtoks[s],
            slot_col,
            after,
            cotangent,
            mixed,
            full_out,
            ln2_gain,
            s,
            into={0: ga} if s else None,
            deps=last,
        )
        sums_two = sums_two + sums
        gwos.append(gwo)
        d = attn_bwd_call(qkv, mixed, gmix, lse, HEADS, s, into={0: d} if s else None)
        if s == 0:
            out_b, last = tokens_of(acts, w_down_local, NN, (gmix,))
    outs = [out_a, out_b]
    sums = jnp.concatenate([sums_two] * 4, axis=0)
    gxs, results, gq, go, sums = last_call(
        d,
        tokens_in,
        full_qkv,
        ln1_gain,
        ln1_bias,
        ga,
        gwos,
        sums,
        after,
        outs,
        slot_col,
        experts,
        nz,
    )
    mine = lax.dynamic_slice_in_dim(
        sums, lax.axis_index("dp") * (width // nz), width // nz, axis=1
    )
    gdown = jnp.concatenate([g[0] for g in gdowns], axis=0).reshape(1, hidden // nz, width)
    gin = jnp.concatenate([g[0, i] for g in gins for i in range(g.shape[1])], axis=1)[None]
    return (
        results,
        gxs,
        mine[0],
        mine[1],
        gq,
        go,
        mine[2],
        mine[3],
        gin.astype(f32),
        gdown.astype(f32),
    )


def solution(mesh):
    placed = (
        P(("dp", "expert"), None, None),
        P(("dp", "expert"), None),
        P(),
        P(),
        P("dp", None),
        P("dp", None),
        P(),
        P(),
        P("expert", None, None),
        P("expert", None, None),
        P(("dp", "expert"), None, None),
    )
    return jax.shard_map(
        on_device,
        mesh=mesh,
        in_specs=placed,
        out_specs=(
            P(("dp", "expert"), None, None),
            P(("dp", "expert"), None, None),
            P("dp"),
            P("dp"),
            P("dp", None),
            P("dp", None),
            P("dp"),
            P("dp"),
            P("expert", None, "dp"),
            P("expert", "dp", None),
        ),
        check_vma=False,
    )
```

time: 562 us -> 459 us (0.82)
  blocking collectives: 57.2 us -> 0 us
  Pallas kernels: 387 us -> 363 us
  local copies, waits for them, and re-layouts: 36.8 us -> 28.1 us
  waiting for transfers between devices: 19 us -> 13.1 us
    all_to_all x2 -> x0, blocking collectives: 57.2 us -> none  [exchange(): lax.all_to_all(parts, 'expert', split_axis=0, concat_axis=0, tiled=True)]
    pallas_call x21 -> x17, Pallas kernels: 387 us -> 363 us  [the longest x15 232 us: kernel_call(): pl.pallas_call(wrapped, in_specs=list(in_specs) + [ANY] * extra, input_ou...]
    squeeze x5 -> x0, local copies, waits for them, and re-layouts: 6.48 us -> none  [the longest x1 3.38 us: on_device(): tokens_in[s]]
    all_to_all x6, waiting for transfers between devices: 18.2 us -> 11.9 us  [exchange(): lax.all_to_all(parts, 'expert', split_axis=0, concat_axis=0, tiled=True)]
    unnamed x98 -> x46, local copies, waits for them, and re-layouts: 25.7 us -> 20.2 us
  transfers between devices with their start and end apart: 10 -> 10, of which waited for: 2 -> 5; matrix products, arithmetic and copies ran while one was open for 3% -> 2% of each run, Pallas kernels for 53% -> 59%
where the time goes in v3:
time: 459 us; the launch traced here: 451 us
  Pallas kernels  363 us (79%)
  local copies, waits for them, and re-layouts  28.1 us (6%)
  starting transfers between devices  25.8 us (6%)
  between operations  14.3 us (3%)
  waiting for transfers between devices  13.1 us (3%)
  other arithmetic  6.96 us (2%)
    pallas_call x15, Pallas kernels, kernel_call(): pl.pallas_call(wrapped, in_specs=list(in_specs) + [ANY] * extra, input_ou...  232 us
    pallas_call x1, Pallas kernels, last_call(): pl.pallas_call(functools.partial(last_body, seqs=seqs, per_seq=per_seq, p...  72.6 us
    pallas_call x1, Pallas kernels, qkv_call(): pl.pallas_call(qkv_body, in_specs=[VM] * 7, out_specs=[ANY] + [VM] * 4 +...  58.7 us
    all_to_all x6, starting transfers between devices, exchange(): lax.all_to_all(parts, 'expert', split_axis=0, concat_axis=0, tiled=True)  25.7 us
    unnamed x46, local copies, waits for them, and re-layouts  20.2 us
    all_to_all x6, waiting for transfers between devices, exchange(): lax.all_to_all(parts, 'expert', split_axis=0, concat_axis=0, tiled=True)  11.9 us
  transfers between devices with their start and end apart: 10, of which 5 were waited for; matrix products, arithmetic and copies ran while one was open for 2% of the time, Pallas kernels for 59%

profile of v3, /device:TPU:0, one launch (start us, length us, event | category | flops | bytes accessed | tf_op | source)
XLA Modules:
  0.0 451.1 jit_solution(11665582511053260896)
XLA Ops:
  12.4 58.7 %shard_map.186 = (bf16[2,1024,2304]{2,1,0:T(8,128)(2,1)}, bf16[768,2304]{1,0:T(8,128)(2,1)}, bf16[768,768]{1,0:T(8,128)(2,1)}, s32[2,1,1024]{2,1,0:T(1,128)}, s3...) custom-call(bf16[2,1024,768]{2,1,0:T(8,128)(2,1)} %refs_3_.5, f32[1,768]{1,0:T(1,128)} %reshape.135.g_ref.refs_5_, ...), custom_call_target="tpu_custom_call" | custom-call | flops 42949672960 | bytes 31457280 | tf_op jit(solution)/shard_map/pallas_call | solution.py:352
  71.2 12.1 %shard_map.187 = (bf16[1,1024,768]{2,1,0:T(8,128)(2,1)S(1)}, f32[1,6,2,1024]{3,2,1,0:T(2,128)S(1)}) custom-call(bf16[2,1024,2304]{2,1,0:T(8,128)(2,1)} %get-tuple-element.47.refs_0_.refs_1_.refs_2_, bf16[2,1024,2304]{2,1,0:T(8,128)(2,1)} %get-tuple-element.47.refs_0_.refs_1_.refs_2_, bf16[2,1024,2304]{2,1,0:T(8,128)(2,1)} %get-tuple-element.47.refs_0_.refs_1_.refs_2_), custom_call_target="tpu_custom_call" | custom-call | flops 13958643712 | bytes 6291456 | tf_op jit(solution)/shard_map/pallas_call | solution.py:52
  83.3 6.4 %shard_map.188 = (f32[2,1024,768]{2,1,0:T(8,128)S(1)}, bf16[8,160,768]{2,1,0:T(8,128)(2,1)}) custom-call(bf16[2,1024,768]{2,1,0:T(8,128)(2,1)S(1)} %copy-done.1, bf16[1,1024,768]{2,1,0:T(8,128)(2,1)S(1)} %get-tuple-element.48.refs_1_.refs_4_.refs_3_, bf16[768,768]{1,0:T(8,128)(2,1)S(1)} %copy-done.7, f32[1,768]{1,0:T(1,128)S(1)} %reshape.138.refs_3_.refs_6_, ...), custom_call_target="tpu_custom_call" | custom-call | flops 5368709120 | bytes 9437184 | tf_op jit(solution)/shard_map/pallas_call | solution.py:52
  92.4 4.7 %all-to-all-start = ((bf16[8,160,768]{2,1,0:T(8,128)(2,1)}), bf16[8,160,768]{2,1,0:T(8,128)(2,1)}, u32[]{:S(2)}, u32[]{:S(2)}) async-start(bf16[8,160,768]{2,1,0:T(8,128)(2,1)} %get-tuple-element.51.refs_3_), calls=%async_computation | async-start | bytes 3932160 | tf_op jit(solution)/shard_map/all_to_all | solution.py:1186
  97.2 12.1 %shard_map.189 = (bf16[1,1024,768]{2,1,0:T(8,128)(2,1)S(1)}, f32[1,6,2,1024]{3,2,1,0:T(2,128)S(1)}) custom-call(bf16[2,1024,2304]{2,1,0:T(8,128)(2,1)} %get-tuple-element.47.refs_0_.refs_1_.refs_2_, bf16[2,1024,2304]{2,1,0:T(8,128)(2,1)} %get-tuple-element.47.refs_0_.refs_1_.refs_2_, bf16[2,1024,2304]{2,1,0:T(8,128)(2,1)} %get-tuple-element.47.refs_0_.refs_1_.refs_2_, ...), custom_call_target="tpu_custom_call" | custom-call | flops 13958643712 | bytes 6291456 | tf_op jit(solution)/shard_map/pallas_call | solution.py:52
  110.6 6.3 %shard_map.190 = (f32[2,1024,768]{2,1,0:T(8,128)S(1)}, bf16[8,160,768]{2,1,0:T(8,128)(2,1)}) custom-call(bf16[2,1024,768]{2,1,0:T(8,128)(2,1)S(1)} %copy-done.1, bf16[1,1024,768]{2,1,0:T(8,128)(2,1)S(1)} %get-tuple-element.52.refs_1_.refs_4_.refs_3_, bf16[768,768]{1,0:T(8,128)(2,1)S(1)} %copy-done.8, ...), custom_call_target="tpu_custom_call", output_to_operand_aliasing={{0}: (6, {})} | custom-call | flops 5368709120 | bytes 9437184 | tf_op jit(solution)/shard_map/pallas_call | solution.py:52
  122.6 3.6 all-to-all-start.1
  126.3 19.8 %shard_map.191 = (bf16[3,1280,1024]{2,1,0:T(8,128)(2,1)}, bf16[3,1280,1024]{2,1,0:T(8,128)(2,1)}) custom-call(bf16[1280,768]{1,0:T(8,128)(2,1)} %bitcast.refs_0_, bf16[2,1280,768]{2,1,0:T(8,128)(2,1)} %bitcast.84, bf16[768,3072]{1,0:T(8,128)(2,1)} %bitcast.44, bf16[768,3072]{1,0:T(8,128)(2,1)} %bitcast.45, bf16[768,3072]{1,0:T(8,128)(2,1)} %bitcast.46, ...), custom_call_target="tpu_custom_call" | custom-call | flops 21474836480 | bytes 31457280 | tf_op jit(solution)/shard_map/pallas_call | solution.py:52
  146.1 5.3 %all-to-all-done.1 = bf16[8,160,768]{2,1,0:T(8,128)(2,1)S(1)} async-done(((bf16[8,160,768]{2,1,0:T(8,128)(2,1)}), bf16[8,160,768]{2,1,0:T(8,128)(2,1)S(1)}, u32[]{:S(2)}, u32[]{:S(2)}) %all-to-all-start.1) | async-done | bytes 1966112 | tf_op jit(solution)/shard_map/all_to_all | solution.py:1186
  152.7 20.3 %shard_map.192 = (bf16[1,1280,1024]{2,1,0:T(8,128)(2,1)}, bf16[1,1280,1024]{2,1,0:T(8,128)(2,1)}, bf16[4,1,256,768]{3,2,1,0:T(8,128)(2,1)}, bf16[4,1,768,256]{3,2,1,0:T(8,128)(2,1)}) custom-call(bf16[1280,768]{1,0:T(8,128)(2,1)} %bitcast.refs_0_, bf16[2,1280,768]{2,1,0:T(8,128)(2,1)} %bitcast.85, bf16[3,1280,1024]{2,1,0:T(8,128)(2,1)} %get-tuple-element.56.refs_2_.refs_0_, ...), custom_call_target="tpu_custom_call" | custom-call | flops 21474836480 | bytes 31457280 | tf_op jit(solution)/shard_map/pallas_call | solution.py:52
  173.1 36.8 %shard_map.193 = (bf16[2,1280,1024]{2,1,0:T(8,128)(2,1)}, bf16[2,1280,1024]{2,1,0:T(8,128)(2,1)}, bf16[4,2,256,768]{3,2,1,0:T(8,128)(2,1)}, bf16[4,2,768,256]{3,2,1,0:T(8,128)(2,1)}) custom-call(bf16[1280,768]{1,0:T(8,128)(2,1)} %bitcast.refs_0_, bf16[2,1280,768]{2,1,0:T(8,128)(2,1)} %bitcast.87, bf16[3,1280,1024]{2,1,0:T(8,128)(2,1)} %get-tuple-element.56.refs_2_.refs_0_, ...), custom_call_target="tpu_custom_call" | custom-call | flops 42949672960 | bytes 31457280 | tf_op jit(solution)/shard_map/pallas_call | solution.py:52
  210.7 10.8 %shard_map.194.refs_6_ = bf16[1280,768]{1,0:T(8,128)(2,1)} custom-call(bf16[3,1280,1024]{2,1,0:T(8,128)(2,1)} %get-tuple-element.57.refs_3_.refs_14_.refs_0_, bf16[768,3072]{1,0:T(8,128)(2,1)} %bitcast.56, bf16[768,3072]{1,0:T(8,128)(2,1)} %bitcast.57, bf16[768,3072]{1,0:T(8,128)(2,1)} %bitcast.58, bf16[768,3072]{1,0:T(8,128)(2,1)} %bitcast.59, ...), custom_call_target="tpu_custom_call" | custom-call | flops 10737418240 | bytes 14680064 | tf_op jit(solution)/shard_map/pallas_call | solution.py:52
  225.7 11.6 %shard_map.195.refs_5_ = bf16[1280,768]{1,0:T(8,128)(2,1)} custom-call(bf16[1,1280,1024]{2,1,0:T(8,128)(2,1)} %get-tuple-element.58.refs_0_, bf16[2,1280,1024]{2,1,0:T(8,128)(2,1)} %get-tuple-element.60.refs_1_, bf16[768,3072]{1,0:T(8,128)(2,1)} %bitcast.60, bf16[768,3072]{1,0:T(8,128)(2,1)} %bitcast.61, bf16[768,3072]{1,0:T(8,128)(2,1)} %bitcast.62, ...), custom_call_target="tpu_custom_call" | custom-call | flops 10737418240 | bytes 14680064 | tf_op jit(solution)/shard_map/pallas_call | solution.py:52
  237.3 10.7 %shard_map.196.refs_7_ = bf16[1280,768]{1,0:T(8,128)(2,1)} custom-call(bf16[3,1280,1024]{2,1,0:T(8,128)(2,1)} %get-tuple-element.56.refs_2_.refs_0_, bf16[3072,768]{1,0:T(8,128)(2,1)} %bitcast.76, bf16[3072,768]{1,0:T(8,128)(2,1)} %bitcast.77, bf16[3072,768]{1,0:T(8,128)(2,1)} %bitcast.78, bf16[3072,768]{1,0:T(8,128)(2,1)} %bitcast.79, ...), custom_call_target="tpu_custom_call" | custom-call | flops 10737418240 | bytes 14680064 | tf_op jit(solution)/shard_map/pallas_call | solution.py:52
  250.2 4.3 all-to-all-start.2
  254.6 12.0 %shard_map.197 = (f32[2,1024,768]{2,1,0:T(8,128)}, bf16[1,1024,768]{2,1,0:T(8,128)(2,1)}, f32[768,768]{1,0:T(8,128)}, f32[2,768]{1,0:T(2,128)}) custom-call(bf16[1280,768]{1,0:T(8,128)(2,1)} %bitcast.34, s32[2,1024,1]{2,1,0:T(8,128)} %get-tuple-element.62.refs_1_.refs_14_, f32[2,1024,768]{2,1,0:T(8,128)} %copy-done.4, bf16[2,1024,768]{2,1,0:T(8,128)(2,1)} %refs_3_.4, ...), custom_call_target="tpu_custom_call" | custom-call | flops 9663676416 | bytes 15728640 | tf_op jit(solution)/shard_map/pallas_call | solution.py:52
  266.6 11.5 %shard_map.198.refs_8_ = bf16[1280,768]{1,0:T(8,128)(2,1)} custom-call(bf16[1,1280,1024]{2,1,0:T(8,128)(2,1)} %get-tuple-element.59.refs_14_.refs_0_, bf16[2,1280,1024]{2,1,0:T(8,128)(2,1)} %get-tuple-element.61.refs_5_.refs_1_, bf16[3072,768]{1,0:T(8,128)(2,1)} %bitcast.80, bf16[3072,768]{1,0:T(8,128)(2,1)} %bitcast.81, bf16[3072,768]{1,0:T(8,128)(2,1)} %bitcast.82, ...), custom_call_target="tpu_custom_call" | custom-call | flops 10737418240 | bytes 14680064 | tf_op jit(solution)/shard_map/pallas_call | solution.py:52
  279.9 4.8 %all-to-all-start.4 = ((bf16[8,160,768]{2,1,0:T(8,128)(2,1)}), bf16[8,160,768]{2,1,0:T(8,128)(2,1)}, u32[]{:S(2)}, u32[]{:S(2)}) async-start(bf16[8,160,768]{2,1,0:T(8,128)(2,1)} %bitcast.9), calls=%async_computation.4 | async-start | bytes 3932160 | tf_op jit(solution)/shard_map/all_to_all | solution.py:1186
  284.7 12.0 %shard_map.199 = (f32[2,1024,768]{2,1,0:T(8,128)}, bf16[1,1024,768]{2,1,0:T(8,128)(2,1)}, f32[768,768]{1,0:T(8,128)}, f32[2,768]{1,0:T(2,128)}) custom-call(bf16[1280,768]{1,0:T(8,128)(2,1)} %bitcast.6.refs_0_, s32[2,1024,1]{2,1,0:T(8,128)} %get-tuple-element.62.refs_1_.refs_14_, f32[2,1024,768]{2,1,0:T(8,128)} %copy-done.4, ...), custom_call_target="tpu_custom_call", output_to_operand_aliasing={{0}: (7, {})} | custom-call | flops 9663676416 | bytes 15728640 | tf_op jit(solution)/shard_map/pallas_call | solution.py:52
  298.0 24.4 %shard_map.200.refs_6_ = bf16[2,3,1024,768]{3,2,1,0:T(8,128)(2,1)} custom-call(bf16[2,1024,2304]{2,1,0:T(8,128)(2,1)} %get-tuple-element.47.refs_0_.refs_1_.refs_2_, bf16[2,1024,2304]{2,1,0:T(8,128)(2,1)} %get-tuple-element.47.refs_0_.refs_1_.refs_2_, bf16[2,1024,2304]{2,1,0:T(8,128)(2,1)} %get-tuple-element.47.refs_0_.refs_1_.refs_2_, ...), custom_call_target="tpu_custom_call" | custom-call | flops 28991029248 | bytes 12582912 | tf_op jit(solution)/shard_map/pallas_call | solution.py:52
  322.5 4.6 %all-to-all-start.5 = ((bf16[8,160,768]{2,1,0:T(8,128)(2,1)}), bf16[8,160,768]{2,1,0:T(8,128)(2,1)}, u32[]{:S(2)}, u32[]{:S(2)}) async-start(bf16[8,160,768]{2,1,0:T(8,128)(2,1)} %bitcast.31), calls=%async_computation.5 | async-start | bytes 3932160 | tf_op jit(solution)/shard_map/all_to_all | solution.py:1186
  327.1 24.5 %shard_map.201.refs_0_.refs_1_ = bf16[2,3,1024,768]{3,2,1,0:T(8,128)(2,1)} custom-call(bf16[2,1024,2304]{2,1,0:T(8,128)(2,1)} %get-tuple-element.47.refs_0_.refs_1_.refs_2_, bf16[2,1024,2304]{2,1,0:T(8,128)(2,1)} %get-tuple-element.47.refs_0_.refs_1_.refs_2_, ...), custom_call_target="tpu_custom_call", output_to_operand_aliasing={{}: (6, {})} | custom-call | flops 28991029248 | bytes 12582912 | tf_op jit(solution)/shard_map/pallas_call | solution.py:52
  352.4 72.6 %shard_map.202 = (f32[2,1024,768]{2,1,0:T(8,128)}, f32[2,1024,768]{2,1,0:T(8,128)}, f32[192,2304]{1,0:T(8,128)}, f32[192,768]{1,0:T(8,128)}, f32[8,768]{1,0:T(8,128)}) custom-call(bf16[2,3,1024,768]{3,2,1,0:T(8,128)(2,1)} %shard_map.201.refs_0_.refs_1_, bf16[2,3,1024,768]{3,2,1,0:T(8,128)(2,1)} %shard_map.201.refs_0_.refs_1_, bf16[2,1024,768]{2,1,0:T(8,128)(2,1)} %refs_3_.5, ...), custom_call_target="tpu_custom_call" | custom-call | flops 53687091200 | bytes 157286400 | tf_op jit(solution)/shard_map/pallas_call | solution.py:1134
  433.3 6.0 %copy.31 = f32[2,1024,768]{2,1,0:T(8,128)} copy(f32[2,1024,768]{2,1,0:T(8,128)} %get-tuple-element.100) | data formatting | bytes 12582912
  (76 shorter events, 40.7 us)
Async XLA Ops:
  7.9 101.4 %copy-start = (f32[1,768]{1,0:T(1,128)}, f32[1,768]{1,0:T(1,128)S(1)}, u32[]{:S(2)}) copy-start(f32[1,768]{1,0:T(1,128)S(1)} %reshape.138.refs_3_.refs_6_) | copy-start | bytes 9220
  71.1 12.2 %copy-start.1 = (bf16[2,1024,768]{2,1,0:T(8,128)(2,1)S(1)}, bf16[2,1024,768]{2,1,0:T(8,128)(2,1)}, u32[]{:S(2)}) copy-start(bf16[2,1024,768]{2,1,0:T(8,128)(2,1)} %refs_3_.5) | copy-start | bytes 9437188
  71.1 12.2 %copy-start.7 = (bf16[768,768]{1,0:T(8,128)(2,1)S(1)}, bf16[768,768]{1,0:T(8,128)(2,1)}, u32[]{:S(2)}) copy-start(bf16[768,768]{1,0:T(8,128)(2,1)} %get-tuple-element.49.refs_2_.refs_5_) | copy-start | bytes 3538948
  71.1 12.2 %copy-start.13 = (s32[2,1,1024]{2,1,0:T(1,128)S(1)}, s32[2,1,1024]{2,1,0:T(1,128)}, u32[]{:S(2)}) copy-start(s32[2,1,1024]{2,1,0:T(1,128)} %get-tuple-element.50.refs_5_) | copy-start | bytes 24580
  83.3 6.4 %copy-start.11 = (bf16[1,1024,768]{2,1,0:T(8,128)(2,1)}, bf16[1,1024,768]{2,1,0:T(8,128)(2,1)S(1)}, u32[]{:S(2)}) copy-start(bf16[1,1024,768]{2,1,0:T(8,128)(2,1)S(1)} %get-tuple-element.48.refs_1_.refs_4_.refs_3_) | copy-start | bytes 4718596
  92.4 30.2 %all-to-all-start = ((bf16[8,160,768]{2,1,0:T(8,128)(2,1)}), bf16[8,160,768]{2,1,0:T(8,128)(2,1)}, u32[]{:S(2)}, u32[]{:S(2)}) async-start(bf16[8,160,768]{2,1,0:T(8,128)(2,1)} %get-tuple-element.51.refs_3_), calls=%async_computation | async-start | bytes 3932160 | tf_op jit(solution)/shard_map/all_to_all | solution.py:1186
  97.2 12.2 %copy-start.3 = (f32[2,1024,768]{2,1,0:T(8,128)S(1)}, f32[2,1024,768]{2,1,0:T(8,128)}, u32[]{:S(2)}) copy-start(f32[2,1024,768]{2,1,0:T(8,128)} %copy-done.2) | copy-start | bytes 18874372
  122.6 28.8 %all-to-all-start.1 = ((bf16[8,160,768]{2,1,0:T(8,128)(2,1)}), bf16[8,160,768]{2,1,0:T(8,128)(2,1)S(1)}, u32[]{:S(2)}, u32[]{:S(2)}) async-start(bf16[8,160,768]{2,1,0:T(8,128)(2,1)} %get-tuple-element.55.refs_10_), calls=%async_computation.1 | async-start | bytes 3932160 | tf_op jit(solution)/shard_map/all_to_all | solution.py:1186
  126.2 300.2 %reduce-scatter.9.cloned.1.call-start = ((), (), s32[]{:S(2)}) async-start(), calls=%async_computation.12 | async-start | bytes 1966080 | tf_op jit(solution)/shard_map/reduce_scatter | solution.py:1268
  173.0 253.4 %reduce-scatter.11.cloned.1.call-start = ((), (), s32[]{:S(2)}) async-start(), calls=%async_computation.13 | async-start | bytes 3932160 | tf_op jit(solution)/shard_map/reduce_scatter | solution.py:1268
  209.9 217.9 %reduce-scatter.7.cloned.1.call-start = ((), (), s32[]{:S(2)}) async-start(), calls=%async_computation.11 | async-start | bytes 3932160 | tf_op jit(solution)/shard_map/reduce_scatter | solution.py:1269
  221.5 28.8 %all-to-all-start.3 = ((bf16[8,160,768]{2,1,0:T(8,128)(2,1)}), bf16[8,160,768]{2,1,0:T(8,128)(2,1)S(1)}, u32[]{:S(2)}, u32[]{:S(2)}) async-start(bf16[8,160,768]{2,1,0:T(8,128)(2,1)} %bitcast.36), calls=%async_computation.3 | async-start | bytes 3932160 | tf_op jit(solution)/shard_map/all_to_all | solution.py:1186
  225.1 205.5 %reduce-scatter.5.cloned.1.call-start = ((), (), s32[]{:S(2)}) async-start(), calls=%async_computation.10 | async-start | bytes 1966080 | tf_op jit(solution)/shard_map/reduce_scatter | solution.py:1269
  250.2 4.4 copy-start.15
  250.2 29.6 %all-to-all-start.2 = ((bf16[8,160,768]{2,1,0:T(8,128)(2,1)}), bf16[8,160,768]{2,1,0:T(8,128)(2,1)}, u32[]{:S(2)}, u32[]{:S(2)}) async-start(bf16[8,160,768]{2,1,0:T(8,128)(2,1)} %bitcast.35), calls=%async_computation.2 | async-start | bytes 3932160 | tf_op jit(solution)/shard_map/all_to_all | solution.py:1186
  279.9 42.6 %all-to-all-start.4 = ((bf16[8,160,768]{2,1,0:T(8,128)(2,1)}), bf16[8,160,768]{2,1,0:T(8,128)(2,1)}, u32[]{:S(2)}, u32[]{:S(2)}) async-start(bf16[8,160,768]{2,1,0:T(8,128)(2,1)} %bitcast.9), calls=%async_computation.4 | async-start | bytes 3932160 | tf_op jit(solution)/shard_map/all_to_all | solution.py:1186
  284.6 12.1 %copy-start.18 = (f32[2,768]{1,0:T(2,128)S(1)}, f32[2,768]{1,0:T(2,128)}, u32[]{:S(2)}) copy-start(f32[2,768]{1,0:T(2,128)} %get-tuple-element.73) | copy-start | bytes 18436
  284.6 13.4 %copy-start.9 = (bf16[1,1024,768]{2,1,0:T(8,128)(2,1)S(1)}, bf16[1,1024,768]{2,1,0:T(8,128)(2,1)}, u32[]{:S(2)}) copy-start(bf16[1,1024,768]{2,1,0:T(8,128)(2,1)} %get-tuple-element.65.refs_6_.refs_4_) | copy-start | bytes 4718596
  284.6 13.4 %copy-start.12 = (bf16[1,1024,768]{2,1,0:T(8,128)(2,1)S(1)}, bf16[1,1024,768]{2,1,0:T(8,128)(2,1)}, u32[]{:S(2)}) copy-start(bf16[1,1024,768]{2,1,0:T(8,128)(2,1)} %copy-done.11) | copy-start | bytes 4718596
  322.5 4.6 %copy-start.6 = (bf16[1,1024,768]{2,1,0:T(8,128)(2,1)S(1)}, bf16[1,1024,768]{2,1,0:T(8,128)(2,1)}, u32[]{:S(2)}) copy-start(bf16[1,1024,768]{2,1,0:T(8,128)(2,1)} %copy-done.5) | copy-start | bytes 4718596
  322.5 4.6 %copy-start.10 = (bf16[1,1024,768]{2,1,0:T(8,128)(2,1)S(1)}, bf16[1,1024,768]{2,1,0:T(8,128)(2,1)}, u32[]{:S(2)}) copy-start(bf16[1,1024,768]{2,1,0:T(8,128)(2,1)} %get-tuple-element.66.refs_4_) | copy-start | bytes 4718596
  322.5 29.9 %all-to-all-start.5 = ((bf16[8,160,768]{2,1,0:T(8,128)(2,1)}), bf16[8,160,768]{2,1,0:T(8,128)(2,1)}, u32[]{:S(2)}, u32[]{:S(2)}) async-start(bf16[8,160,768]{2,1,0:T(8,128)(2,1)} %bitcast.31), calls=%async_computation.5 | async-start | bytes 3932160 | tf_op jit(solution)/shard_map/all_to_all | solution.py:1186
  430.6 8.8 %slice-start = ((s8[6291456]{0:T(1024)(128)(4,1)}), s8[4194304]{0:T(1024)(128)(4,1)S(1)}, s32[]{:S(2)}) async-start(s8[6291456]{0:T(1024)(128)(4,1)} %bitcast.28), calls=%async_computation.14 | async-start | bytes 8388608
  433.3 6.0 %slice-start.1 = ((s8[6291456]{0:T(1024)(128)(4,1)}), s8[2097152]{0:T(1024)(128)(4,1)S(1)}, s32[]{:S(2)}) async-start(s8[6291456]{0:T(1024)(128)(4,1)} %bitcast.28), calls=%async_computation.15 | async-start | bytes 4194304
  (7 other events, 13.3 us)
Sparse Core Ops, SparseCore 0:
  173.1 33.5 reduce-scatter.8
  210.0 58.5 reduce-scatter.10
  270.9 60.2 reduce-scatter.6
  333.4 35.2 reduce-scatter.4
